TPU v7x, 1024 devices: a whole 8x8x8 slice. The times are simulated.
1024 devices in a mesh: dp: 64 (over x_lo, y, core), fsdp: 16 (over x_hi, z).
Axes of the slice: x: 8 (x_hi: 2, x_lo: 4; x = x_hi * 4 + x_lo), y: 8, z: 8, core: 2. Of those that a mesh axis runs over, the one named last changes fastest.
Arguments:
- shots_in: bfloat16 [8192, 32768], P(('dp', 'fsdp')), may hold values from -24 to 24
- cotangent: bfloat16 [8192, 32768], P(('dp', 'fsdp')), may hold values from -6 to 6
- blocks: bfloat16 [256, 256, 256], P('fsdp'), may hold values from -0.25 to 0.25
- block_rows: int32 [256], replicated, may hold values from 0 to 127, as said below
- block_cols: int32 [256], replicated, may hold values from 0 to 127, as said below
Outputs:
- shots_out: bfloat16 [8192, 32768], P(('dp', 'fsdp'))
- input_grad: bfloat16 [8192, 32768], P(('dp', 'fsdp'))
- weight_grad: float32 [256, 256, 256], P('fsdp', 'dp')
Inputs may be any that keep to these rules, and one draw needn't show every extreme that they name: Blocks are stored in runs of 2: blocks 2 * j to 2 * j + 1 share one block row; every block row holds exactly 2 blocks with different block columns; every block column holds at least one block; block_rows and block_cols list the same blocks in the same order. `block_cols`: see block_rows.
All inputs are finite; a program needn't handle non-finite values.
Results may differ from a plain program's by a relative error of at most 0.001.
Values may be sent and summed in bfloat16 or wider, within the bound.
No kernel may reach another device: no remote copies, remote signals or barrier semaphores. Data moves between devices by JAX's collectives and lax.ppermute only.
A program may use at most 32 MiB of HBM per device.

v0:
```python
import jax
import jax.numpy as jnp
from jax import lax
from jax.sharding import PartitionSpec as P

PER_ROW = 2


def shards(shots_in, cotangent, blocks, block_rows, block_cols):
    shot_count = shots_in.shape[0]
    block_width = blocks.shape[1]
    owned_count = blocks.shape[0]
    row_count = owned_count // PER_ROW
    group_size = lax.axis_size("fsdp")
    inputs = shots_in.reshape(shot_count, -1, block_width)
    cotangent_view = cotangent.reshape(shot_count, -1, block_width)
    column_total = inputs.shape[1]
    row_total = cotangent_view.shape[1]
    pair_rows = block_rows.reshape(row_total, PER_ROW)[:, 0]
    send_columns = jnp.take(inputs, block_cols, axis=1).reshape(
        shot_count, group_size, owned_count, block_width
    )
    send_rows = jnp.take(cotangent_view, pair_rows, axis=1).reshape(
        shot_count, group_size, row_count, block_width
    )
    columns_here = lax.all_to_all(send_columns, "fsdp", split_axis=1, concat_axis=0, tiled=True)
    rows_here = lax.all_to_all(send_rows, "fsdp", split_axis=1, concat_axis=0, tiled=True)
    columns_here = columns_here[:, 0]
    rows_repeated = jnp.repeat(rows_here[:, 0], PER_ROW, axis=1)
    factor = float(shot_count * lax.axis_size("dp") * group_size) ** (-0.5)
    products = jnp.einsum("gkb,kbc->gkc", columns_here, blocks, preferred_element_type=jnp.float32)
    row_values = (
        products.reshape(products.shape[0], row_count, PER_ROW, block_width)
        .sum(axis=2)
        .astype(jnp.bfloat16)
    )
    rows_back = lax.all_to_all(row_values, "fsdp", split_axis=0, concat_axis=1, tiled=True)
    row_ids = jnp.arange(row_total, dtype=jnp.int32)
    matches = (pair_rows[None, :] == row_ids[:, None]).astype(jnp.int32)
    inverse = jnp.sum(matches * row_ids[None, :], axis=1)
    shots_out = jnp.take(rows_back, inverse, axis=1).reshape(shot_count, -1)
    partial_terms = jnp.einsum(
        "gkc,kbc->gkb", rows_repeated, blocks, preferred_element_type=jnp.float32
    )
    terms_back = lax.all_to_all(partial_terms, "fsdp", split_axis=0, concat_axis=1, tiled=True)
    column_ids = jnp.arange(column_total, dtype=jnp.int32)
    selector = (block_cols[:, None] == column_ids[None, :]).astype(jnp.float32)
    summed_columns = jnp.einsum(
        "skb,kc->scb",
        terms_back,
        selector,
        precision=lax.Precision.HIGHEST,
        preferred_element_type=jnp.float32,
    )
    input_grad = summed_columns.reshape(shot_count, -1).astype(jnp.bfloat16)
    term = jnp.einsum(
        "gkb,gkc->kbc", columns_here, rows_repeated, preferred_element_type=jnp.float32
    )
    weight_grad = lax.psum_scatter(term, "dp", scatter_dimension=1, tiled=True) * factor
    return (shots_out, input_grad, weight_grad)


def solution(mesh):
    return jax.shard_map(
        shards,
        mesh=mesh,
        in_specs=(
            P(("dp", "fsdp"), None),
            P(("dp", "fsdp"), None),
            P("fsdp", None, None),
            P(),
            P(),
        ),
        out_specs=(P(("dp", "fsdp"), None), P(("dp", "fsdp"), None), P("fsdp", "dp", None)),
        check_vma=False,
    )
```

profile of v0, /device:TPU:383, one launch (start us, length us, event | category | flops | bytes accessed | tf_op | source)
XLA Modules:
  0.0 426.9 jit_solution(14926732585059872950)
XLA Ops:
  7.2 1.0 reshape.49
  8.3 1.7 gather_fusion.2
  11.1 17.9 %all-to-all-start.2 = ((bf16[8,16,8,256]{3,2,0,1:T(8,128)(2,1)}), bf16[8,16,8,256]{3,2,0,1:T(8,128)(2,1)}, u32[]{:S(2)}, u32[]{:S(2)}) async-start(bf16[8,16,8,256]{3,2,0,1:T(8,128)(2,1)} %copy.67), calls=%async_computation.2 | async-start | bytes 1048576 | tf_op jit(solution)/shard_map/all_to_all | solution.py:27
  29.1 1.8 gather_fusion
  31.3 1.1 copy.61
  32.4 11.1 %all-to-all-done.2 = bf16[8,16,8,256]{3,2,0,1:T(8,128)(2,1)} async-done(((bf16[8,16,8,256]{3,2,0,1:T(8,128)(2,1)}), bf16[8,16,8,256]{3,2,0,1:T(8,128)(2,1)}, u32[]{:S(2)}, u32[]{:S(2)}) %all-to-all-start.2) | async-done | bytes 524320 | tf_op jit(solution)/shard_map/all_to_all | solution.py:27
  43.5 10.0 %all-to-all-start = ((bf16[8,16,16,256]{3,2,0,1:T(8,128)(2,1)}), bf16[8,16,16,256]{3,2,0,1:T(8,128)(2,1)}, u32[]{:S(2)}, u32[]{:S(2)}) async-start(bf16[8,16,16,256]{3,2,0,1:T(8,128)(2,1)} %copy.61), calls=%async_computation | async-start | bytes 2097152 | tf_op jit(solution)/shard_map/all_to_all | solution.py:26
  53.6 1.9 copy.68
  55.5 22.4 %all-to-all-done = bf16[8,16,16,256]{3,2,0,1:T(8,128)(2,1)} async-done(((bf16[8,16,16,256]{3,2,0,1:T(8,128)(2,1)}), bf16[8,16,16,256]{3,2,0,1:T(8,128)(2,1)}, u32[]{:S(2)}, u32[]{:S(2)}) %all-to-all-start) | async-done | bytes 1048608 | tf_op jit(solution)/shard_map/all_to_all | solution.py:26
  77.9 1.1 broadcast_in_dim.34
  79.1 2.0 fusion.1
  81.1 4.4 %copy.72 = f32[16,256,256]{2,0,1:T(8,128)} copy(f32[16,256,256]{2,1,0:T(8,128)S(1)} %fusion.1) | data formatting | bytes 8388608 | tf_op jit(solution)/shard_map/gkb,gkc->kbc/dot_general | solution.py:56
  85.5 2.1 bitcast_reduce_fusion
  87.6 1.1 copy.63
  88.6 12.1 %all-to-all-start.1 = ((bf16[128,8,256]{2,1,0:T(8,128)(2,1)}), bf16[128,8,256]{2,1,0:T(8,128)(2,1)}, u32[]{:S(2)}, u32[]{:S(2)}) async-start(bf16[128,8,256]{2,1,0:T(8,128)(2,1)} %copy.63), calls=%async_computation.1 | async-start | bytes 1048576 | tf_op jit(solution)/shard_map/all_to_all | solution.py:37
  101.6 2.6 copy.69
  104.1 11.1 %all-to-all-done.1 = bf16[128,8,256]{2,1,0:T(8,128)(2,1)} async-done(((bf16[128,8,256]{2,1,0:T(8,128)(2,1)}), bf16[128,8,256]{2,1,0:T(8,128)(2,1)}, u32[]{:S(2)}, u32[]{:S(2)}) %all-to-all-start.1) | async-done | bytes 524320 | tf_op jit(solution)/shard_map/all_to_all | solution.py:37
  115.2 10.3 %all-to-all-start.3 = ((f32[128,16,256]{2,1,0:T(8,128)}), f32[128,16,256]{2,1,0:T(8,128)}, u32[]{:S(2)}, u32[]{:S(2)}) async-start(f32[128,16,256]{2,1,0:T(8,128)} %copy.69), calls=%async_computation.3 | async-start | bytes 4194304 | tf_op jit(solution)/shard_map/all_to_all | solution.py:45
  125.6 1.1 copy.89
  127.7 1.0 broadcast_select_fusion.2
  128.7 52.1 %all-to-all-done.3 = f32[128,16,256]{2,1,0:T(8,128)} async-done(((f32[128,16,256]{2,1,0:T(8,128)}), f32[128,16,256]{2,1,0:T(8,128)}, u32[]{:S(2)}, u32[]{:S(2)}) %all-to-all-start.3) | async-done | bytes 2097184 | tf_op jit(solution)/shard_map/all_to_all | solution.py:45
  180.8 1.8 copy.70
  183.5 1.1 copy.79
  184.6 233.9 %reduce-scatter.2.cloned.1.call-done = f32[16,4,256]{2,0,1:T(8,128)} async-done(((f32[16,256,256]{2,0,1:T(8,128)}), f32[16,4,256]{2,0,1:T(8,128)}) %reduce-scatter.2.cloned.1.call-update) | async-done | bytes 65552 | tf_op jit(solution)/shard_map/reduce_scatter | solution.py:59
  (28 shorter events, 6.0 us)
Async XLA Ops:
  7.2 78.3 %copy-start = (bf16[16,256,256]{2,1,0:T(8,128)(2,1)S(1)}, bf16[16,256,256]{2,1,0:T(8,128)(2,1)}, u32[]{:S(2)}) copy-start(bf16[16,256,256]{2,1,0:T(8,128)(2,1)} %param.9) | copy-start | bytes 6291460
  8.3 20.7 %copy-start.1 = (s32[256]{0:T(256)S(1)}, s32[256]{0:T(256)}, u32[]{:S(2)}) copy-start(s32[256]{0:T(256)} %param.11) | copy-start | bytes 3076
  11.1 32.4 %all-to-all-start.2 = ((bf16[8,16,8,256]{3,2,0,1:T(8,128)(2,1)}), bf16[8,16,8,256]{3,2,0,1:T(8,128)(2,1)}, u32[]{:S(2)}, u32[]{:S(2)}) async-start(bf16[8,16,8,256]{3,2,0,1:T(8,128)(2,1)} %copy.67), calls=%async_computation.2 | async-start | bytes 1048576 | tf_op jit(solution)/shard_map/all_to_all | solution.py:27
  43.5 34.5 %all-to-all-start = ((bf16[8,16,16,256]{3,2,0,1:T(8,128)(2,1)}), bf16[8,16,16,256]{3,2,0,1:T(8,128)(2,1)}, u32[]{:S(2)}, u32[]{:S(2)}) async-start(bf16[8,16,16,256]{3,2,0,1:T(8,128)(2,1)} %copy.61), calls=%async_computation | async-start | bytes 2097152 | tf_op jit(solution)/shard_map/all_to_all | solution.py:26
  53.5 365.0 %reduce-scatter.2.cloned.1.call-start = ((), (), s32[]{:S(2)}) async-start(), calls=%async_computation.5 | async-start | bytes 4259840 | tf_op jit(solution)/shard_map/reduce_scatter | solution.py:59
  88.6 26.6 %all-to-all-start.1 = ((bf16[128,8,256]{2,1,0:T(8,128)(2,1)}), bf16[128,8,256]{2,1,0:T(8,128)(2,1)}, u32[]{:S(2)}, u32[]{:S(2)}) async-start(bf16[128,8,256]{2,1,0:T(8,128)(2,1)} %copy.63), calls=%async_computation.1 | async-start | bytes 1048576 | tf_op jit(solution)/shard_map/all_to_all | solution.py:37
  115.2 65.6 %all-to-all-start.3 = ((f32[128,16,256]{2,1,0:T(8,128)}), f32[128,16,256]{2,1,0:T(8,128)}, u32[]{:S(2)}, u32[]{:S(2)}) async-start(f32[128,16,256]{2,1,0:T(8,128)} %copy.69), calls=%async_computation.3 | async-start | bytes 4194304 | tf_op jit(solution)/shard_map/all_to_all | solution.py:45
Sparse Core Ops, SparseCore 0:
  85.6 332.8 reduce-scatter.1
where the time goes:
time: 428 us; the launch traced here: 427 us
  waiting for transfers between devices  331 us (77%)
  starting transfers between devices  50.4 us (12%)
  local copies, waits for them, and re-layouts  23.5 us (5%)
  between operations  14.2 us (3%)
  matrix products  5.73 us (1%)
    reduce_scatter x1, waiting for transfers between devices, shards(): lax.psum_scatter(term, 'dp', scatter_dimension=1, tiled=True) * factor  234 us
    all_to_all x1, waiting for transfers between devices, shards(): lax.all_to_all(partial_terms, 'fsdp', split_axis=0, concat_axis=1, tiled=...  52.1 us
    all_to_all x1, waiting for transfers between devices, shards(): lax.all_to_all(send_columns, 'fsdp', split_axis=1, concat_axis=0, tiled=T...  22.4 us
    all_to_all x1, starting transfers between devices, shards(): lax.all_to_all(send_rows, 'fsdp', split_axis=1, concat_axis=0, tiled=True)  17.9 us
    all_to_all x1, starting transfers between devices, shards(): lax.all_to_all(row_values, 'fsdp', split_axis=0, concat_axis=1, tiled=True)  12.1 us
    all_to_all x1, waiting for transfers between devices, shards(): lax.all_to_all(send_rows, 'fsdp', split_axis=1, concat_axis=0, tiled=True)  11.1 us
    all_to_all x1, waiting for transfers between devices, shards(): lax.all_to_all(row_values, 'fsdp', split_axis=0, concat_axis=1, tiled=True)  11.1 us
    all_to_all x1, starting transfers between devices, shards(): lax.all_to_all(partial_terms, 'fsdp', split_axis=0, concat_axis=1, tiled=...  10.3 us
  transfers between devices with their start and end apart: 5, of which 5 were waited for; matrix products, arithmetic and copies ran while one was open for 4% of the time, Pallas kernels for 0%

commit v1 on v0

v1 whole, which is shorter than its diff:
```python
import functools

import jax
import jax.numpy as jnp
from jax import lax
from jax.experimental import pallas as pl
from jax.experimental.pallas import tpu as pltpu
from jax.sharding import PartitionSpec as P

AXES = ("dp", "fsdp")
XL, Y, CORES, XH, Z = 4, 8, 2, 2, 8
OWNERS = XH * Z
S = 8
B = 256
HALF = 12 * B
MESSAGE = 2 * HALF
SCALES = 128
STEPS = 16.0


def device(xl, y, core, xh, z):
    return (((xl * Y + y) * CORES + core) * XH + xh) * Z + z


def groups():
    return [
        [device((xl + 2 * xh) % XL, y, core, xh, z) for xh in range(XH) for z in range(Z)]
        for xl in range(XL)
        for y in range(Y)
        for core in range(CORES)
    ]


def moves(target):
    return [
        (device(xl, y, core, xh, z), device(*target(xl, y, core), xh, z))
        for xl in range(XL)
        for y in range(Y)
        for core in range(CORES)
        for xh in range(XH)
        for z in range(Z)
    ]


def gather_kernel(cols, rows, x_ref, g_ref, out_ref):
    base = pl.program_id(0) * 4

    @pl.loop(0, 4)
    def _(p):
        for half in range(2):
            for j in range(8):
                col = pl.multiple_of(cols[(base + p) * 16 + half * 8 + j] * B, B)
                at = half * HALF + j * B
                out_ref[p, :, at : at + B] = x_ref[:, pl.ds(col, B)]
            for j in range(4):
                row = pl.multiple_of(rows[(base + p) * 16 + half * 8 + 2 * j] * B, B)
                at = half * HALF + (8 + j) * B
                out_ref[p, :, at : at + B] = g_ref[:, pl.ds(row, B)]


def gather(block_cols, block_rows, shots_in, cotangent):
    return pl.pallas_call(
        gather_kernel,
        out_shape=jax.ShapeDtypeStruct((OWNERS, S, MESSAGE), jnp.bfloat16),
        grid_spec=pltpu.PrefetchScalarGridSpec(
            num_scalar_prefetch=2,
            grid=(4,),
            in_specs=[
                pl.BlockSpec((S, 128 * B), lambda i, c, r: (0, 0)),
                pl.BlockSpec((S, 128 * B), lambda i, c, r: (0, 0)),
            ],
            out_specs=pl.BlockSpec((4, S, MESSAGE), lambda i, c, r: (i, 0, 0)),
        ),
        name="gather",
    )(block_cols, block_rows, shots_in, cotangent)


def fixed(v):
    top = jnp.max(jnp.abs(v), axis=1, keepdims=True)
    e = jnp.ceil(jnp.log2(jnp.maximum(top, 2.0**-120)) * STEPS + 0.01)
    q = v * jnp.exp2(e * (-1.0 / STEPS)) * 32760.0
    return jnp.clip(jnp.round(q), -32767.0, 32767.0), e


def decoded(e):
    return jnp.exp2(e.astype(jnp.int32).astype(jnp.float32) * (1.0 / STEPS)) * (1.0 / 32760.0)


def apply_kernel(x_ref, g_ref, w_ref, out_ref, scale_ref):
    s = pl.program_id(0)
    lanes = lax.broadcasted_iota(jnp.int32, (OWNERS * S, SCALES), 1)
    x = x_ref[...]
    g = g_ref[...]

    def put(slot, v):
        q, e = fixed(v)
        at = pl.multiple_of(s * (3 * B), B) + slot * B
        out_ref[:, pl.ds(at, B)] = q.astype(jnp.int32).astype(jnp.int16)
        scale_ref[...] = jnp.where(lanes == s * 3 + slot, e, scale_ref[...])

    @pl.when(s == 0)
    def _():
        scale_ref[...] = jnp.zeros_like(scale_ref)

    dot = functools.partial(lax.dot_general, preferred_element_type=jnp.float32)
    put(0, dot(x[:, :B], w_ref[0], (((1,), (0,)), ((), ()))) + dot(x[:, B:], w_ref[1], (((1,), (0,)), ((), ()))))
    put(1, dot(g, w_ref[0], (((1,), (1,)), ((), ()))))
    put(2, dot(g, w_ref[1], (((1,), (1,)), ((), ()))))

    @pl.when(s == 7)
    def _():
        out_ref[:, MESSAGE:] = scale_ref[...].astype(jnp.int32).astype(jnp.int16)


def apply(received, blocks):
    shots = OWNERS * S
    return pl.pallas_call(
        apply_kernel,
        out_shape=jax.ShapeDtypeStruct((shots, MESSAGE + SCALES), jnp.int16),
        grid=(8,),
        in_specs=[
            pl.BlockSpec((shots, 2 * B), lambda s: (0, s // 4 * 6 + s % 4)),
            pl.BlockSpec((shots, B), lambda s: (0, s // 4 * 12 + 8 + s % 4)),
            pl.BlockSpec((2, B, B), lambda s: (s, 0, 0)),
        ],
        out_specs=pl.BlockSpec((shots, MESSAGE + SCALES), lambda s: (0, 0)),
        scratch_shapes=[pltpu.VMEM((shots, SCALES), jnp.float32)],
        name="apply",
    )(received, received, blocks)


def grad_kernel(ids, own_ref, other_ref, *refs):
    outs, wg_ref, scale_ref = refs[:Y], refs[Y], refs[Y + 1]
    y = ids[1]
    dot = functools.partial(lax.dot_general, dimension_numbers=(((0,), (0,)), ((), ())), preferred_element_type=jnp.float32)
    lanes = lax.broadcasted_iota(jnp.int32, (B, SCALES), 1)
    scales = jnp.zeros((B, SCALES), jnp.float32)
    for j in range(8):
        a = slice(j * B, (j + 1) * B)
        b = slice((8 + j // 2) * B, (9 + j // 2) * B)
        wg = dot(own_ref[:, a], own_ref[:, b]) + dot(other_ref[:, a], other_ref[:, b])
        q, e = fixed(wg)
        scales = jnp.where(lanes == j, e, scales)
        wg_ref[...] = q.reshape(XL, Y, S, B)
        for d in range(Y):
            part = wg_ref[:, pl.ds(lax.rem(y + d, Y), 1)].reshape(XL * S, B)
            outs[d][:, a] = part.astype(jnp.int32).astype(jnp.int16)
    scale_ref[...] = scales.reshape(XL, Y, S, SCALES)
    for d in range(Y):
        part = scale_ref[:, pl.ds(lax.rem(y + d, Y), 1)].reshape(XL * S, SCALES)
        outs[d][:, 8 * B :] = part.astype(jnp.int32).astype(jnp.int16)


def grad(ids, received, other):
    shots = OWNERS * S
    part = (XL * S, 8 * B + SCALES)
    return pl.pallas_call(
        grad_kernel,
        out_shape=[jax.ShapeDtypeStruct(part, jnp.int16)] * Y,
        grid_spec=pltpu.PrefetchScalarGridSpec(
            num_scalar_prefetch=1,
            grid=(1,),
            in_specs=[
                pl.BlockSpec((shots, HALF), lambda i, ids: (0, ids[0])),
                pl.BlockSpec((shots, HALF), lambda i, ids: (0, 0)),
            ],
            out_specs=[pl.BlockSpec(part, lambda i, ids: (0, 0))] * Y,
            scratch_shapes=[
                pltpu.VMEM((XL, Y, S, B), jnp.float32),
                pltpu.VMEM((XL, Y, S, SCALES), jnp.float32),
            ],
        ),
        name="grad",
    )(ids, received, other)


def sum_kernel(ids, *refs):
    ins, outs, total_ref = refs[:Y], refs[Y : Y + XL], refs[Y + XL]
    xl = ids[2]
    scales = [decoded(ref[:, 8 * B :]) for ref in ins]
    for j in range(8):
        total = jnp.zeros((XL * S, B), jnp.float32)
        for ref, scale in zip(ins, scales):
            q = ref[:, j * B : (j + 1) * B].astype(jnp.int32).astype(jnp.float32)
            total = total + q * scale[:, j : j + 1]
        total_ref[...] = total.reshape(XL, S, B)
        for d in range(XL):
            outs[d][j] = total_ref[lax.rem(xl + d, XL)]


def sum_groups(ids, parts):
    part = (XL * S, 8 * B + SCALES)
    return pl.pallas_call(
        sum_kernel,
        out_shape=[jax.ShapeDtypeStruct((8, S, B), jnp.float32)] * XL,
        grid_spec=pltpu.PrefetchScalarGridSpec(
            num_scalar_prefetch=1,
            grid=(1,),
            in_specs=[pl.BlockSpec(part, lambda i, ids: (0, 0))] * Y,
            out_specs=[pl.BlockSpec((8, S, B), lambda i, ids: (0, 0, 0))] * XL,
            scratch_shapes=[pltpu.VMEM((XL, S, B), jnp.float32)],
        ),
        name="sum_groups",
    )(ids, *parts)


def place_kernel(cols, rows, in_ref, out_ref, grad_ref, total_ref):
    step = pl.program_id(0)

    @pl.when(step == 0)
    def _():
        total_ref[...] = jnp.zeros_like(total_ref)

    @pl.loop(0, 4)
    def _(i):
        p = step * 4 + i
        scale = decoded(in_ref[i, :, MESSAGE:])
        for s in range(8):
            def value(slot):
                at = s * 3 * B + slot * B
                q = in_ref[i, :, at : at + B].astype(jnp.int32).astype(jnp.float32)
                return q * scale[:, s * 3 + slot : s * 3 + slot + 1]

            row = pl.multiple_of(rows[p * 16 + 2 * s] * B, B)
            out_ref[:, pl.ds(row, B)] = value(0).astype(jnp.bfloat16)
            for member in range(2):
                col = pl.multiple_of(cols[p * 16 + 2 * s + member] * B, B)
                total_ref[:, pl.ds(col, B)] += value(1 + member)

    @pl.when(step == 3)
    def _():
        grad_ref[...] = total_ref[...].astype(jnp.bfloat16)


def place(block_cols, block_rows, back):
    return pl.pallas_call(
        place_kernel,
        out_shape=[jax.ShapeDtypeStruct((S, 128 * B), jnp.bfloat16)] * 2,
        grid_spec=pltpu.PrefetchScalarGridSpec(
            num_scalar_prefetch=2,
            grid=(4,),
            in_specs=[pl.BlockSpec((4, S, MESSAGE + SCALES), lambda i, c, r: (i, 0, 0))],
            out_specs=[pl.BlockSpec((S, 128 * B), lambda i, c, r: (0, 0))] * 2,
            scratch_shapes=[pltpu.VMEM((S, 128 * B), jnp.float32)],
        ),
        name="place",
    )(block_cols, block_rows, back)


def shards(shots_in, cotangent, blocks, block_rows, block_cols):
    dp = lax.axis_index("dp")
    core, y, xl = dp % CORES, dp // CORES % Y, dp // (CORES * Y)
    ids = jnp.stack([core, y, xl]).astype(jnp.int32)
    permute = functools.partial(lax.ppermute, axis_name=AXES)
    exchange = functools.partial(
        lax.all_to_all, axis_name=AXES, split_axis=0, concat_axis=0, axis_index_groups=groups(), tiled=True
    )

    received = exchange(gather(block_cols, block_rows, shots_in, cotangent)).reshape(OWNERS * S, MESSAGE)
    theirs = lax.dynamic_slice_in_dim(received, (1 - core) * HALF, HALF, axis=1)
    other = permute(theirs, perm=moves(lambda a, b, c: (a, b, 1 - c)))
    result = apply(received, blocks)
    back = exchange(result.reshape(OWNERS, S, MESSAGE + SCALES))
    parts = grad(ids, received, other)
    parts = [parts[0]] + [
        permute(parts[d], perm=moves(lambda a, b, c, d=d: (a, (b + d) % Y, c))) for d in range(1, Y)
    ]
    sums = sum_groups(ids, parts)
    total = sums[0]
    for d in range(1, XL):
        total = total + permute(sums[d], perm=moves(lambda a, b, c, d=d: ((a + d) % XL, b, c)))
    total = (total * (8192.0**-0.5)).reshape(8, 2, 4, B)
    mine = lax.dynamic_index_in_dim(total, core, 1, keepdims=False)
    swapped = permute(
        lax.dynamic_index_in_dim(total, 1 - core, 1, keepdims=False), perm=moves(lambda a, b, c: (a, b, 1 - c))
    )
    weight_grad = jnp.where(
        core == 0, jnp.concatenate([mine, swapped]), jnp.concatenate([swapped, mine])
    )
    shots_out, input_grad = place(block_cols, block_rows, back)
    return shots_out, input_grad, weight_grad


def solution(mesh):
    return jax.shard_map(
        shards,
        mesh=mesh,
        in_specs=(P(AXES, None), P(AXES, None), P("fsdp", None, None), P(), P()),
        out_specs=(P(AXES, None), P(AXES, None), P("fsdp", "dp", None)),
        check_vma=False,
    )
```

time: 428 us -> 167 us (0.39)
  the two profiles are of different devices: /device:TPU:383 before, /device:TPU:1 now
where the time goes in v1:
time: 167 us; the launch traced here: 165 us
  starting transfers between devices  59.3 us (36%)
  blocking collectives  56 us (34%)
  Pallas kernels  24.5 us (15%)
  waiting for transfers between devices  18.1 us (11%)
  local copies, waits for them, and re-layouts  3.72 us (2%)
  other arithmetic  2.1 us (1%)
    all_to_all x1, blocking collectives, shards(): exchange(gather(block_cols, block_rows, shots_in, cotangent))  56 us
    ppermute x7, starting transfers between devices, shards(): permute(parts[d], perm=moves(lambda a, b, c, d=d: (a, (b + d) % Y, c)))  28.9 us
    all_to_all x1, starting transfers between devices, shards(): back = exchange(result.reshape(OWNERS, S, MESSAGE + SCALES))  13.4 us
    ppermute x7, waiting for transfers between devices, shards(): permute(parts[d], perm=moves(lambda a, b, c, d=d: (a, (b + d) % Y, c)))  12.8 us
    ppermute x3, starting transfers between devices, shards(): permute(sums[d], perm=moves(lambda a, b, c, d=d: ((a + d) % XL, b, c)))  9.13 us
    pallas_call x1, Pallas kernels, apply(): pl.pallas_call(apply_kernel, out_shape=jax.ShapeDtypeStruct((shots, MESSA...  7.71 us
    pallas_call x1, Pallas kernels, place(): pl.pallas_call(place_kernel, out_shape=[jax.ShapeDtypeStruct((S, 128 * B)...  5.53 us
    ppermute x1, starting transfers between devices, shards(): permute(lax.dynamic_index_in_dim(total, 1 - core, 1, keepdims=False), per...  4.93 us
  transfers between devices with their start and end apart: 13, of which 8 were waited for; matrix products, arithmetic and copies ran while one was open for 2% of the time, Pallas kernels for 4%

profile of v1, /device:TPU:1, one launch (start us, length us, event | category | flops | bytes accessed | tf_op | source)
XLA Modules:
  0.0 164.6 jit_solution(11823229028021347461)
XLA Ops:
  0.6 3.9 %gather.1 = bf16[16,8,6144]{2,1,0:T(8,128)(2,1)} custom-call(s32[256]{0:T(256)} %cols.3, s32[256]{0:T(256)} %rows.3, bf16[8,32768]{1,0:T(8,128)(2,1)} %x_ref.1, bf16[8,32768]{1,0:T(8,128)(2,1)} %g_ref.1), custom_call_target="tpu_custom_call" | custom-call | tf_op jit(solution)/shard_map/gather/pallas_call | solution.py:62
  4.6 56.0 %all_to_all.10 = bf16[16,8,6144]{2,1,0:T(8,128)(2,1)} all-to-all(bf16[16,8,6144]{2,1,0:T(8,128)(2,1)} %gather.1), channel_id=1, replica_groups={{0,1,2,3,4,5,6,7,520,521,522,523,524,525,526,527},{16,17,18,19,20,21,22..., dimensions={0} | all-to-all | bytes 3145728 | tf_op jit(solution)/shard_map/all_to_all | solution.py:259
  60.5 7.7 %apply.1 = s16[128,6272]{1,0:T(8,128)(2,1)} custom-call(bf16[128,6144]{1,0:T(8,128)(2,1)} %bitcast.9, bf16[128,6144]{1,0:T(8,128)(2,1)} %bitcast.10, bf16[16,256,256]{2,1,0:T(8,128)(2,1)} %w_ref.1), custom_call_target="tpu_custom_call" | custom-call | tf_op jit(solution)/shard_map/apply/pallas_call | solution.py:117
  68.3 13.4 %all-to-all-start.1 = ((s16[16,8,6272]{2,1,0:T(8,128)(2,1)}), s16[16,8,6272]{2,1,0:T(8,128)(2,1)S(1)}, u32[]{:S(2)}, u32[]{:S(2)}) async-start(s16[16,8,6272]{2,1,0:T(8,128)(2,1)} %bitcast.13), calls=%async_computation.1 | async-start | bytes 3211264 | tf_op jit(solution)/shard_map/all_to_all | solution.py:263
  82.6 3.0 %collective-permute-start = (bf16[128,3072]{1,0:T(8,128)(2,1)}, bf16[128,3072]{1,0:T(8,128)(2,1)S(1)}, u32[]{:S(2)}, u32[]{:S(2)}) collective-permute-start(bf16[128,3072]{1,0:T(8,128)(2,1)} %constant_dynamic-slice_fusion), channel_id=1, source_target_pairs={{0,16},{1,17},{2,18},{3,19},{4,20},{5,21},{6,22},{7,23},{8,24},{9,... | collective-permute-start | bytes 2359304 | tf_op jit(solution)/shard_map/ppermute | solution.py:261
  86.3 1.5 collective-permute-done.other_ref
  88.6 4.3 %grad.1 = (s16[32,2176]{1,0:T(8,128)(2,1)}, s16[32,2176]{1,0:T(8,128)(2,1)}, s16[32,2176]{1,0:T(8,128)(2,1)}, s16[32,2176]{1,0:T(8,128)(2,1)}, s16[32,2176]{1,0:...) custom-call(s32[3]{0:T(128)} %pad_add_fusion.ids, ...), custom_call_target="tpu_custom_call" | custom-call | tf_op jit(solution)/shard_map/grad/pallas_call | solution.py:157
  92.9 3.3 %collective-permute-start.1 = (s16[32,2176]{1,0:T(8,128)(2,1)}, s16[32,2176]{1,0:T(8,128)(2,1)S(1)}, u32[]{:S(2)}, u32[]{:S(2)}) collective-permute-start(s16[32,2176]{1,0:T(8,128)(2,1)} %get-tuple-element.20), channel_id=1, source_target_pairs={{0,32},{1,33},{2,34},{3,35},{4,36},{5,37},{6,38},{7,39},{8,40},{9,... | collective-permute-start | bytes 417800 | tf_op jit(solution)/shard_map/ppermute | solution.py:266
  96.3 4.4 %collective-permute-start.2 = (s16[32,2176]{1,0:T(8,128)(2,1)}, s16[32,2176]{1,0:T(8,128)(2,1)S(1)}, u32[]{:S(2)}, u32[]{:S(2)}) collective-permute-start(s16[32,2176]{1,0:T(8,128)(2,1)} %get-tuple-element.21), channel_id=1, source_target_pairs={{0,64},{1,65},{2,66},{3,67},{4,68},{5,69},{6,70},{7,71},{8,72},{9,... | collective-permute-start | bytes 417800 | tf_op jit(solution)/shard_map/ppermute | solution.py:266
  100.7 5.0 %collective-permute-start.3 = (s16[32,2176]{1,0:T(8,128)(2,1)}, s16[32,2176]{1,0:T(8,128)(2,1)S(1)}, u32[]{:S(2)}, u32[]{:S(2)}) collective-permute-start(s16[32,2176]{1,0:T(8,128)(2,1)} %get-tuple-element.22), channel_id=1, source_target_pairs={{0,96},{1,97},{2,98},{3,99},{4,100},{5,101},{6,102},{7,103},{8,104... | collective-permute-start | bytes 417800 | tf_op jit(solution)/shard_map/ppermute | solution.py:266
  105.7 3.1 %collective-permute-start.4 = (s16[32,2176]{1,0:T(8,128)(2,1)}, s16[32,2176]{1,0:T(8,128)(2,1)S(1)}, u32[]{:S(2)}, u32[]{:S(2)}) collective-permute-start(s16[32,2176]{1,0:T(8,128)(2,1)} %get-tuple-element.23), channel_id=1, source_target_pairs={{0,128},{1,129},{2,130},{3,131},{4,132},{5,133},{6,134},{7,135},{8... | collective-permute-start | bytes 417800 | tf_op jit(solution)/shard_map/ppermute | solution.py:266
  108.8 5.4 %collective-permute-start.5 = (s16[32,2176]{1,0:T(8,128)(2,1)}, s16[32,2176]{1,0:T(8,128)(2,1)S(1)}, u32[]{:S(2)}, u32[]{:S(2)}) collective-permute-start(s16[32,2176]{1,0:T(8,128)(2,1)} %get-tuple-element.24), channel_id=1, source_target_pairs={{0,160},{1,161},{2,162},{3,163},{4,164},{5,165},{6,166},{7,167},{8... | collective-permute-start | bytes 417800 | tf_op jit(solution)/shard_map/ppermute | solution.py:266
  114.3 4.7 %collective-permute-start.6 = (s16[32,2176]{1,0:T(8,128)(2,1)}, s16[32,2176]{1,0:T(8,128)(2,1)S(1)}, u32[]{:S(2)}, u32[]{:S(2)}) collective-permute-start(s16[32,2176]{1,0:T(8,128)(2,1)} %get-tuple-element.25), channel_id=1, source_target_pairs={{0,192},{1,193},{2,194},{3,195},{4,196},{5,197},{6,198},{7,199},{8... | collective-permute-start | bytes 417800 | tf_op jit(solution)/shard_map/ppermute | solution.py:266
  119.0 2.9 %collective-permute-start.7 = (s16[32,2176]{1,0:T(8,128)(2,1)}, s16[32,2176]{1,0:T(8,128)(2,1)S(1)}, u32[]{:S(2)}, u32[]{:S(2)}) collective-permute-start(s16[32,2176]{1,0:T(8,128)(2,1)} %get-tuple-element.26), channel_id=1, source_target_pairs={{0,224},{1,225},{2,226},{3,227},{4,228},{5,229},{6,230},{7,231},{8... | collective-permute-start | bytes 417800 | tf_op jit(solution)/shard_map/ppermute | solution.py:266
  122.5 2.8 %collective-permute-done.5.refs_5_ = s16[32,2176]{1,0:T(8,128)(2,1)S(1)} collective-permute-done((s16[32,2176]{1,0:T(8,128)(2,1)}, s16[32,2176]{1,0:T(8,128)(2,1)S(1)}, u32[]{:S(2)}, u32[]{:S(2)}) %collective-permute-start.5) | collective-permute-done | bytes 139296 | tf_op jit(solution)/shard_map/ppermute | solution.py:266
  125.3 9.1 %collective-permute-done.6.refs_6_ = s16[32,2176]{1,0:T(8,128)(2,1)S(1)} collective-permute-done((s16[32,2176]{1,0:T(8,128)(2,1)}, s16[32,2176]{1,0:T(8,128)(2,1)S(1)}, u32[]{:S(2)}, u32[]{:S(2)}) %collective-permute-start.6) | collective-permute-done | bytes 139296 | tf_op jit(solution)/shard_map/ppermute | solution.py:266
  135.3 3.0 %sum_groups.1 = (f32[8,8,256]{2,1,0:T(8,128)}, f32[8,8,256]{2,1,0:T(8,128)}, f32[8,8,256]{2,1,0:T(8,128)}, f32[8,8,256]{2,1,0:T(8,128)}) custom-call(s32[3]{0:T(128)} %pad_add_fusion.ids, s16[32,2176]{1,0:T(8,128)(2,1)} %get-tuple-element.19.refs_0_, s16[32,2176]{1,0:T(8,128)(2,1)} %copy-done.3, s16[32,2176]{1,0:T(8,128)(2,1)} %copy-done.4, ...), custom_call_target="tpu_custom_call" | custom-call | tf_op jit(solution)/shard_map/sum_groups/pallas_call | solution.py:193
  138.4 1.9 %collective-permute-start.10 = (f32[8,8,256]{2,1,0:T(8,128)}, f32[8,8,256]{2,1,0:T(8,128)S(1)}, u32[]{:S(2)}, u32[]{:S(2)}) collective-permute-start(f32[8,8,256]{2,1,0:T(8,128)} %get-tuple-element.30), channel_id=1, source_target_pairs={{0,768},{1,769},{2,770},{3,771},{4,772},{5,773},{6,774},{7,775},{8... | collective-permute-start | bytes 196616 | tf_op jit(solution)/shard_map/ppermute | solution.py:271
  140.3 3.4 %collective-permute-start.8 = (f32[8,8,256]{2,1,0:T(8,128)}, f32[8,8,256]{2,1,0:T(8,128)S(1)}, u32[]{:S(2)}, u32[]{:S(2)}) collective-permute-start(f32[8,8,256]{2,1,0:T(8,128)} %get-tuple-element.28), channel_id=1, source_target_pairs={{0,256},{1,257},{2,258},{3,259},{4,260},{5,261},{6,262},{7,263},{8... | collective-permute-start | bytes 196616 | tf_op jit(solution)/shard_map/ppermute | solution.py:271
  143.7 3.9 %collective-permute-start.9 = (f32[8,8,256]{2,1,0:T(8,128)}, f32[8,8,256]{2,1,0:T(8,128)S(1)}, u32[]{:S(2)}, u32[]{:S(2)}) collective-permute-start(f32[8,8,256]{2,1,0:T(8,128)} %get-tuple-element.29), channel_id=1, source_target_pairs={{0,512},{1,513},{2,514},{3,515},{4,516},{5,517},{6,518},{7,519},{8... | collective-permute-start | bytes 196616 | tf_op jit(solution)/shard_map/ppermute | solution.py:271
  147.8 2.7 %collective-permute-done.9 = f32[8,8,256]{2,1,0:T(8,128)S(1)} collective-permute-done((f32[8,8,256]{2,1,0:T(8,128)}, f32[8,8,256]{2,1,0:T(8,128)S(1)}, u32[]{:S(2)}, u32[]{:S(2)}) %collective-permute-start.9) | collective-permute-done | bytes 65568 | tf_op jit(solution)/shard_map/ppermute | solution.py:271
  151.5 4.9 %collective-permute-start.11 = (f32[8,4,256]{2,1,0:T(4,128)S(1)}, f32[8,4,256]{2,1,0:T(4,128)S(1)}, u32[]{:S(2)}, u32[]{:S(2)}) collective-permute-start(f32[8,4,256]{2,1,0:T(4,128)S(1)} %get-tuple-element.32), channel_id=1, source_target_pairs={{0,16},{1,17},{2,18},{3,19},{4,20},{5,21},{6,22},{7,23},{8,24},{9,... | collective-permute-start | bytes 98312 | tf_op jit(solution)/shard_map/ppermute | solution.py:274
  157.9 1.2 copy-done.1
  159.1 5.5 %place.1 = (bf16[8,32768]{1,0:T(8,128)(2,1)}, bf16[8,32768]{1,0:T(8,128)(2,1)}) custom-call(s32[256]{0:T(256)} %cols.3, s32[256]{0:T(256)} %rows.3, s16[16,8,6272]{2,1,0:T(8,128)(2,1)} %copy-done.1), custom_call_target="tpu_custom_call" | custom-call | tf_op jit(solution)/shard_map/place/pallas_call | solution.py:236
  (34 shorter events, 6.6 us)
Async XLA Ops:
  68.2 13.4 %copy-start = (bf16[16,8,6144]{2,1,0:T(8,128)(2,1)S(1)}, bf16[16,8,6144]{2,1,0:T(8,128)(2,1)}, u32[]{:S(2)}) copy-start(bf16[16,8,6144]{2,1,0:T(8,128)(2,1)} %all_to_all.10) | copy-start | bytes 4718596
  68.3 89.6 %all-to-all-start.1 = ((s16[16,8,6272]{2,1,0:T(8,128)(2,1)}), s16[16,8,6272]{2,1,0:T(8,128)(2,1)S(1)}, u32[]{:S(2)}, u32[]{:S(2)}) async-start(s16[16,8,6272]{2,1,0:T(8,128)(2,1)} %bitcast.13), calls=%async_computation.1 | async-start | bytes 3211264 | tf_op jit(solution)/shard_map/all_to_all | solution.py:263
  82.6 5.1 %collective-permute-start = (bf16[128,3072]{1,0:T(8,128)(2,1)}, bf16[128,3072]{1,0:T(8,128)(2,1)S(1)}, u32[]{:S(2)}, u32[]{:S(2)}) collective-permute-start(bf16[128,3072]{1,0:T(8,128)(2,1)} %constant_dynamic-slice_fusion), channel_id=1, source_target_pairs={{0,16},{1,17},{2,18},{3,19},{4,20},{5,21},{6,22},{7,23},{8,24},{9,... | collective-permute-start | bytes 2359304 | tf_op jit(solution)/shard_map/ppermute | solution.py:261
  87.8 0.9 copy-start.2
  92.9 21.3 %collective-permute-start.1 = (s16[32,2176]{1,0:T(8,128)(2,1)}, s16[32,2176]{1,0:T(8,128)(2,1)S(1)}, u32[]{:S(2)}, u32[]{:S(2)}) collective-permute-start(s16[32,2176]{1,0:T(8,128)(2,1)} %get-tuple-element.20), channel_id=1, source_target_pairs={{0,32},{1,33},{2,34},{3,35},{4,36},{5,37},{6,38},{7,39},{8,40},{9,... | collective-permute-start | bytes 417800 | tf_op jit(solution)/shard_map/ppermute | solution.py:266
  96.3 22.8 %collective-permute-start.2 = (s16[32,2176]{1,0:T(8,128)(2,1)}, s16[32,2176]{1,0:T(8,128)(2,1)S(1)}, u32[]{:S(2)}, u32[]{:S(2)}) collective-permute-start(s16[32,2176]{1,0:T(8,128)(2,1)} %get-tuple-element.21), channel_id=1, source_target_pairs={{0,64},{1,65},{2,66},{3,67},{4,68},{5,69},{6,70},{7,71},{8,72},{9,... | collective-permute-start | bytes 417800 | tf_op jit(solution)/shard_map/ppermute | solution.py:266
  100.7 21.2 %collective-permute-start.3 = (s16[32,2176]{1,0:T(8,128)(2,1)}, s16[32,2176]{1,0:T(8,128)(2,1)S(1)}, u32[]{:S(2)}, u32[]{:S(2)}) collective-permute-start(s16[32,2176]{1,0:T(8,128)(2,1)} %get-tuple-element.22), channel_id=1, source_target_pairs={{0,96},{1,97},{2,98},{3,99},{4,100},{5,101},{6,102},{7,103},{8,104... | collective-permute-start | bytes 417800 | tf_op jit(solution)/shard_map/ppermute | solution.py:266
  105.7 16.8 %collective-permute-start.4 = (s16[32,2176]{1,0:T(8,128)(2,1)}, s16[32,2176]{1,0:T(8,128)(2,1)S(1)}, u32[]{:S(2)}, u32[]{:S(2)}) collective-permute-start(s16[32,2176]{1,0:T(8,128)(2,1)} %get-tuple-element.23), channel_id=1, source_target_pairs={{0,128},{1,129},{2,130},{3,131},{4,132},{5,133},{6,134},{7,135},{8... | collective-permute-start | bytes 417800 | tf_op jit(solution)/shard_map/ppermute | solution.py:266
  108.8 16.6 %collective-permute-start.5 = (s16[32,2176]{1,0:T(8,128)(2,1)}, s16[32,2176]{1,0:T(8,128)(2,1)S(1)}, u32[]{:S(2)}, u32[]{:S(2)}) collective-permute-start(s16[32,2176]{1,0:T(8,128)(2,1)} %get-tuple-element.24), channel_id=1, source_target_pairs={{0,160},{1,161},{2,162},{3,163},{4,164},{5,165},{6,166},{7,167},{8... | collective-permute-start | bytes 417800 | tf_op jit(solution)/shard_map/ppermute | solution.py:266
  114.2 20.4 %copy-start.3 = (s16[32,2176]{1,0:T(8,128)(2,1)}, s16[32,2176]{1,0:T(8,128)(2,1)S(1)}, u32[]{:S(2)}) copy-start(s16[32,2176]{1,0:T(8,128)(2,1)S(1)} %collective-permute-done.1.refs_1_) | copy-start | bytes 417796
  114.3 20.2 %collective-permute-start.6 = (s16[32,2176]{1,0:T(8,128)(2,1)}, s16[32,2176]{1,0:T(8,128)(2,1)S(1)}, u32[]{:S(2)}, u32[]{:S(2)}) collective-permute-start(s16[32,2176]{1,0:T(8,128)(2,1)} %get-tuple-element.25), channel_id=1, source_target_pairs={{0,192},{1,193},{2,194},{3,195},{4,196},{5,197},{6,198},{7,199},{8... | collective-permute-start | bytes 417800 | tf_op jit(solution)/shard_map/ppermute | solution.py:266
  119.0 15.7 %copy-start.4 = (s16[32,2176]{1,0:T(8,128)(2,1)}, s16[32,2176]{1,0:T(8,128)(2,1)S(1)}, u32[]{:S(2)}) copy-start(s16[32,2176]{1,0:T(8,128)(2,1)S(1)} %collective-permute-done.2.refs_2_) | copy-start | bytes 417796
  119.0 15.7 %collective-permute-start.7 = (s16[32,2176]{1,0:T(8,128)(2,1)}, s16[32,2176]{1,0:T(8,128)(2,1)S(1)}, u32[]{:S(2)}, u32[]{:S(2)}) collective-permute-start(s16[32,2176]{1,0:T(8,128)(2,1)} %get-tuple-element.26), channel_id=1, source_target_pairs={{0,224},{1,225},{2,226},{3,227},{4,228},{5,229},{6,230},{7,231},{8... | collective-permute-start | bytes 417800 | tf_op jit(solution)/shard_map/ppermute | solution.py:266
  121.9 12.8 %copy-start.5 = (s16[32,2176]{1,0:T(8,128)(2,1)}, s16[32,2176]{1,0:T(8,128)(2,1)S(1)}, u32[]{:S(2)}) copy-start(s16[32,2176]{1,0:T(8,128)(2,1)S(1)} %collective-permute-done.3.refs_3_) | copy-start | bytes 417796
  122.5 12.2 %copy-start.6 = (s16[32,2176]{1,0:T(8,128)(2,1)}, s16[32,2176]{1,0:T(8,128)(2,1)S(1)}, u32[]{:S(2)}) copy-start(s16[32,2176]{1,0:T(8,128)(2,1)S(1)} %collective-permute-done.4.refs_4_) | copy-start | bytes 417796
  125.3 9.4 %copy-start.7 = (s16[32,2176]{1,0:T(8,128)(2,1)}, s16[32,2176]{1,0:T(8,128)(2,1)S(1)}, u32[]{:S(2)}) copy-start(s16[32,2176]{1,0:T(8,128)(2,1)S(1)} %collective-permute-done.5.refs_5_) | copy-start | bytes 417796
  134.4 0.6 copy-start.8
  134.7 0.7 copy-start.9
  138.4 9.2 %collective-permute-start.10 = (f32[8,8,256]{2,1,0:T(8,128)}, f32[8,8,256]{2,1,0:T(8,128)S(1)}, u32[]{:S(2)}, u32[]{:S(2)}) collective-permute-start(f32[8,8,256]{2,1,0:T(8,128)} %get-tuple-element.30), channel_id=1, source_target_pairs={{0,768},{1,769},{2,770},{3,771},{4,772},{5,773},{6,774},{7,775},{8... | collective-permute-start | bytes 196616 | tf_op jit(solution)/shard_map/ppermute | solution.py:271
  140.3 7.5 %collective-permute-start.8 = (f32[8,8,256]{2,1,0:T(8,128)}, f32[8,8,256]{2,1,0:T(8,128)S(1)}, u32[]{:S(2)}, u32[]{:S(2)}) collective-permute-start(f32[8,8,256]{2,1,0:T(8,128)} %get-tuple-element.28), channel_id=1, source_target_pairs={{0,256},{1,257},{2,258},{3,259},{4,260},{5,261},{6,262},{7,263},{8... | collective-permute-start | bytes 196616 | tf_op jit(solution)/shard_map/ppermute | solution.py:271
  143.7 6.9 %collective-permute-start.9 = (f32[8,8,256]{2,1,0:T(8,128)}, f32[8,8,256]{2,1,0:T(8,128)S(1)}, u32[]{:S(2)}, u32[]{:S(2)}) collective-permute-start(f32[8,8,256]{2,1,0:T(8,128)} %get-tuple-element.29), channel_id=1, source_target_pairs={{0,512},{1,513},{2,514},{3,515},{4,516},{5,517},{6,518},{7,519},{8... | collective-permute-start | bytes 196616 | tf_op jit(solution)/shard_map/ppermute | solution.py:271
  151.5 5.8 %collective-permute-start.11 = (f32[8,4,256]{2,1,0:T(4,128)S(1)}, f32[8,4,256]{2,1,0:T(4,128)S(1)}, u32[]{:S(2)}, u32[]{:S(2)}) collective-permute-start(f32[8,4,256]{2,1,0:T(4,128)S(1)} %get-tuple-element.32), channel_id=1, source_target_pairs={{0,16},{1,17},{2,18},{3,19},{4,20},{5,21},{6,22},{7,23},{8,24},{9,... | collective-permute-start | bytes 98312 | tf_op jit(solution)/shard_map/ppermute | solution.py:274
  157.9 1.2 copy-start.1

commit v2 on v1

v2 whole, which is shorter than its diff:
```python
import functools

import jax
import jax.numpy as jnp
from jax import lax
from jax.experimental import pallas as pl
from jax.experimental.pallas import tpu as pltpu
from jax.sharding import PartitionSpec as P

AXES = ("dp", "fsdp")
XL, Y, CORES, XH, Z = 4, 8, 2, 2, 8
OWNERS = XH * Z
S = 8
B = 256
HALF = 12 * B
MESSAGE = 2 * HALF
SCALES = 128
STEPS = 16.0
ROOM = pltpu.CompilerParams(vmem_limit_bytes=24 * 2**20)


def device(xl, y, core, xh, z):
    return (((xl * Y + y) * CORES + core) * XH + xh) * Z + z


def groups():
    return [
        [device((xl + 2 * xh) % XL, y, core, xh, z) for xh in range(XH) for z in range(Z)]
        for xl in range(XL)
        for y in range(Y)
        for core in range(CORES)
    ]


def moves(target):
    return [
        (device(xl, y, core, xh, z), device(*target(xl, y, core), xh, z))
        for xl in range(XL)
        for y in range(Y)
        for core in range(CORES)
        for xh in range(XH)
        for z in range(Z)
    ]


LONG = pl.CostEstimate(flops=20_000_000_000, bytes_accessed=1_000_000, transcendentals=0)


def gather_kernel(cols, rows, x_ref, g_ref, out_ref):
    base = pl.program_id(0) * 4
    for p in range(4):
        for half in range(2):
            first = (base + p) * 16 + half * 8
            for j in range(8):
                col = pl.multiple_of(cols[first + j] * B, B)
                at = half * HALF + j * B
                out_ref[p, :, at : at + B] = x_ref[:, pl.ds(col, B)]
            for j in range(4):
                row = pl.multiple_of(rows[first + 2 * j] * B, B)
                at = half * HALF + (8 + j) * B
                out_ref[p, :, at : at + B] = g_ref[:, pl.ds(row, B)]


def gather(block_cols, block_rows, shots_in, cotangent):
    return pl.pallas_call(
        gather_kernel,
        out_shape=jax.ShapeDtypeStruct((OWNERS, S, MESSAGE), jnp.bfloat16),
        grid_spec=pltpu.PrefetchScalarGridSpec(
            num_scalar_prefetch=2,
            grid=(4,),
            in_specs=[
                pl.BlockSpec((S, 128 * B), lambda i, c, r: (0, 0)),
                pl.BlockSpec((S, 128 * B), lambda i, c, r: (0, 0)),
            ],
            out_specs=pl.BlockSpec((4, S, MESSAGE), lambda i, c, r: (i, 0, 0)),
        ),
        name="gather",
    )(block_cols, block_rows, shots_in, cotangent)


def fixed(v):
    top = jnp.max(jnp.abs(v), axis=1, keepdims=True)
    e = jnp.ceil(jnp.log2(jnp.maximum(top, 2.0**-120)) * STEPS + 0.01)
    return jnp.round(v * (jnp.exp2(e * (-1.0 / STEPS)) * 32760.0)).astype(jnp.int32).astype(jnp.int16), e


def decoded(e):
    return jnp.exp2(e.astype(jnp.int32).astype(jnp.float32) * (1.0 / STEPS)) * (1.0 / 32760.0)


def widened(q):
    return q.astype(jnp.int32).astype(jnp.float32)


def at(j, width=B):
    return slice(j * B, j * B + width)


def dot(u, v, over):
    return lax.dot_general(u, v, (over, ((), ())), preferred_element_type=jnp.float32)


def put_scales(ref, scales):
    lanes = lax.broadcasted_iota(jnp.int32, (scales[0].shape[0], SCALES), 1)
    out = jnp.zeros(lanes.shape, jnp.float32)
    for j, e in enumerate(scales):
        out = jnp.where(lanes == j, e, out)
    ref[:, ref.shape[1] - SCALES :] = out.astype(jnp.int32).astype(jnp.int16)


def grad_kernel(ids, in_ref, other_ref, send_ref, keep_ref, wg_ref):
    core, parity = ids[0], lax.rem(ids[1], 2)
    scales = []
    for j in range(8):
        own = lambda slot: in_ref[:, pl.ds(pl.multiple_of(core * HALF + slot * B, B), B)]
        x0, g0 = own(j), own(8 + j // 2)
        x1, g1 = other_ref[:, at(j)], other_ref[:, at(8 + j // 2)]
        wg = dot(x0, g0, ((0,), (0,))) + dot(x1, g1, ((0,), (0,)))
        wg_ref[...] = wg.reshape(16, 2, S, B)
        keep_ref[:, at(j)] = wg_ref[:, pl.ds(parity, 1)].reshape(128, B)
        q, e = fixed(wg_ref[:, pl.ds(1 - parity, 1)].reshape(128, B))
        send_ref[:, at(j)] = q
        scales.append(e)
    put_scales(send_ref, scales)


def apply_kernel(in_ref, w_ref, after_ref, out_ref):
    scales = []
    for s in range(8):
        first = s // 4 * 12 + s % 4 * 2
        x0, x1, g = in_ref[:, at(first)], in_ref[:, at(first + 1)], in_ref[:, at(s // 4 * 12 + 8 + s % 4)]
        w0, w1 = w_ref[2 * s], w_ref[2 * s + 1]
        values = (
            dot(x0, w0, ((1,), (0,))) + dot(x1, w1, ((1,), (0,))),
            dot(g, w0, ((1,), (1,))),
            dot(g, w1, ((1,), (1,))),
        )
        for slot, value in enumerate(values):
            q, e = fixed(value)
            out_ref[:, at(3 * s + slot)] = q
            scales.append(e)
    put_scales(out_ref, scales)


def here(*arrays):
    return [pltpu.with_memory_space_constraint(a, pltpu.VMEM) for a in arrays]


def vmem(n):
    return [pl.BlockSpec(memory_space=pltpu.VMEM)] * n


SMEM = pl.BlockSpec(memory_space=pltpu.SMEM)
PART = 8 * B + SCALES


def grad(ids, received, other):
    return pl.pallas_call(
        grad_kernel,
        out_shape=[pltpu.VMEM((128, PART), jnp.int16), pltpu.VMEM((128, 8 * B), jnp.float32)],
        in_specs=[SMEM] + vmem(2),
        out_specs=vmem(2),
        scratch_shapes=[pltpu.VMEM((16, 2, S, B), jnp.float32)],
        compiler_params=ROOM,
        name="grad",
    )(ids, *here(received, other))


def apply(received, blocks, after):
    return pl.pallas_call(
        apply_kernel,
        out_shape=jax.ShapeDtypeStruct((OWNERS * S, MESSAGE + SCALES), jnp.int16),
        in_specs=vmem(3),
        compiler_params=ROOM,
        cost_estimate=pl.CostEstimate(flops=5_000_000_000, bytes_accessed=20_000_000, transcendentals=0),
        name="apply",
    )(*here(received, blocks, after))


def pairs_kernel(ids, keep_ref, got_ref, *refs):
    outs, own_ref, total_ref = refs[:3], refs[3], refs[4]
    pair = ids[1] // 2
    scale = decoded(got_ref[:, 8 * B :])
    scales = [[] for _ in range(3)]
    for j in range(8):
        total = keep_ref[:, at(j)] + widened(got_ref[:, at(j)]) * scale[:, j : j + 1]
        total_ref[...] = total.reshape(XL, 4, S, B)
        own_ref[:, at(j)] = total_ref[:, pl.ds(pair, 1)].reshape(32, B)
        for d in range(3):
            q, e = fixed(total_ref[:, pl.ds(lax.rem(pair + d + 1, 4), 1)].reshape(32, B))
            outs[d][:, at(j)] = q
            scales[d].append(e)
    for d in range(3):
        put_scales(outs[d], scales[d])


def pairs(ids, keep, got):
    return pl.pallas_call(
        pairs_kernel,
        out_shape=[pltpu.VMEM((32, PART), jnp.int16)] * 3
        + [pltpu.VMEM((32, 8 * B), jnp.float32)],
        in_specs=[SMEM] + vmem(2),
        out_specs=vmem(4),
        scratch_shapes=[pltpu.VMEM((XL, 4, S, B), jnp.float32)],
        compiler_params=ROOM,
        cost_estimate=LONG,
        name="pairs",
    )(ids, *here(keep, got))


def halves_kernel(ids, own_ref, a_ref, b_ref, c_ref, keep_ref, send_ref, total_ref):
    parity = lax.rem(ids[2], 2)
    ins = (a_ref, b_ref, c_ref)
    scales = [decoded(ref[:, 8 * B :]) for ref in ins]
    for j in range(8):
        total = own_ref[:, at(j)]
        for ref, scale in zip(ins, scales):
            total = total + widened(ref[:, at(j)]) * scale[:, j : j + 1]
        total_ref[...] = total.reshape(2, 2, S, B)
        keep_ref[:, at(j)] = total_ref[:, pl.ds(parity, 1)].reshape(16, B)
        send_ref[:, at(j)] = total_ref[:, pl.ds(1 - parity, 1)].reshape(16, B)


def halves(ids, own, parts):
    return pl.pallas_call(
        halves_kernel,
        out_shape=[pltpu.VMEM((16, 8 * B), jnp.float32)] * 2,
        in_specs=[SMEM] + vmem(4),
        out_specs=vmem(2),
        scratch_shapes=[pltpu.VMEM((2, 2, S, B), jnp.float32)],
        compiler_params=ROOM,
        name="halves",
    )(ids, *here(own, *parts))


def place_kernel(cols, rows, in_ref, out_ref, grad_ref, first_ref, second_ref):
    totals = (first_ref, second_ref)
    for ref in totals:
        ref[...] = jnp.zeros_like(ref)

    @pl.loop(0, OWNERS)
    def _(p):
        scale = decoded(in_ref[p, :, MESSAGE:])
        values = [widened(in_ref[p, :, at(j)]) * scale[:, j : j + 1] for j in range(24)]
        for s in range(8):
            row = pl.multiple_of(rows[p * 16 + 2 * s] * B, B)
            out_ref[:, pl.ds(row, B)] = values[3 * s].astype(jnp.bfloat16)
            for member, ref in enumerate(totals):
                col = pl.multiple_of(cols[p * 16 + 2 * s + member] * B, B)
                ref[:, pl.ds(col, B)] += values[3 * s + 1 + member]

    grad_ref[...] = (first_ref[...] + second_ref[...]).astype(jnp.bfloat16)


def place(block_cols, block_rows, back):
    return pl.pallas_call(
        place_kernel,
        out_shape=[jax.ShapeDtypeStruct((S, 128 * B), jnp.bfloat16)] * 2,
        in_specs=[SMEM, SMEM] + vmem(1),
        scratch_shapes=[pltpu.VMEM((S, 128 * B), jnp.float32)] * 2,
        compiler_params=ROOM,
        name="place",
    )(block_cols, block_rows, *here(back))


def shards(shots_in, cotangent, blocks, block_rows, block_cols):
    dp = lax.axis_index("dp")
    core, y, xl = dp % CORES, dp // CORES % Y, dp // (CORES * Y)
    ids = jnp.stack([core, y, xl]).astype(jnp.int32)
    permute = functools.partial(lax.ppermute, axis_name=AXES)
    exchange = functools.partial(
        lax.all_to_all, axis_name=AXES, split_axis=0, concat_axis=0, axis_index_groups=groups(), tiled=True
    )

    received = exchange(gather(block_cols, block_rows, shots_in, cotangent)).reshape(OWNERS * S, MESSAGE)
    theirs = lax.dynamic_slice_in_dim(received, (1 - core) * HALF, HALF, axis=1)
    other = permute(theirs, perm=moves(lambda a, b, c: (a, b, 1 - c)))
    send, keep = grad(ids, received, other)
    result = apply(received, blocks, keep)
    got = permute(send, perm=moves(lambda a, b, c: (a, b ^ 1, c)))
    back = exchange(result.reshape(OWNERS, S, MESSAGE + SCALES))
    *parts, own = pairs(ids, keep, got)
    parts = [
        permute(part, perm=moves(lambda a, b, c, d=d: (a, (b + 2 * d + 2) % Y, c))) for d, part in enumerate(parts)
    ]
    keep, send = halves(ids, own, parts)
    total = keep + permute(send, perm=moves(lambda a, b, c: (a ^ 1, b, c)))
    total = total.reshape(2, S, 8 * B)
    send = lax.dynamic_index_in_dim(total, 1 - xl // 2, 0, keepdims=False)
    total = lax.dynamic_index_in_dim(total, xl // 2, 0, keepdims=False)
    total = total + permute(send, perm=moves(lambda a, b, c: (a ^ 2, b, c)))
    total = (total * (8192.0**-0.5)).reshape(2, 4, 8, B)
    mine = lax.dynamic_index_in_dim(total, core, 0, keepdims=False)
    swapped = permute(
        lax.dynamic_index_in_dim(total, 1 - core, 0, keepdims=False), perm=moves(lambda a, b, c: (a, b, 1 - c))
    )
    weight_grad = jnp.where(
        core == 0, jnp.concatenate([mine, swapped], axis=1), jnp.concatenate([swapped, mine], axis=1)
    ).transpose(1, 0, 2)
    shots_out, input_grad = place(block_cols, block_rows, back)
    return shots_out, input_grad, weight_grad


def solution(mesh):
    return jax.shard_map(
        shards,
        mesh=mesh,
        in_specs=(P(AXES, None), P(AXES, None), P("fsdp", None, None), P(), P()),
        out_specs=(P(AXES, None), P(AXES, None), P("fsdp", "dp", None)),
        check_vma=False,
    )
```

time: 167 us -> 145 us (0.87)
  blocking collectives: 56 us -> 0 us
  waiting for transfers between devices: 18.1 us -> 63.8 us
  Pallas kernels: 24.5 us -> 15.1 us
  starting transfers between devices: 59.3 us -> 63.1 us
  local copies, waits for them, and re-layouts: 3.72 us -> 0.8 us
  other arithmetic: 2.1 us -> 0.11 us
    all_to_all x1 -> x0, blocking collectives: 56 us -> none  [shards(): exchange(gather(block_cols, block_rows, shots_in, cotangent))]
    all_to_all x0 -> x1, waiting for transfers between devices: none -> 40.2 us  [shards(): exchange(gather(block_cols, block_rows, shots_in, cotangent))]
    all_to_all x0 -> x1, starting transfers between devices: none -> 20.5 us  [shards(): exchange(gather(block_cols, block_rows, shots_in, cotangent))]
    ppermute x11 -> x7, starting transfers between devices: 42.9 us -> 26.1 us  [the longest x3 14.4 us: shards(): permute(part, perm=moves(lambda a, b, c, d=d: (a, (b + 2 * d + 2) % Y, c)))]
    pallas_call x3 -> x4, Pallas kernels: 15 us -> 7.66 us  [the longest x1 2.95 us: grad(): pl.pallas_call(grad_kernel, out_shape=[pltpu.VMEM((128, PART), jnp.int16)...]
    ppermute x11 -> x7, waiting for transfers between devices: 16.6 us -> 21.9 us  [the longest x3 8.92 us: shards(): permute(part, perm=moves(lambda a, b, c, d=d: (a, (b + 2 * d + 2) % Y, c)))]
    unnamed x20 -> x8, local copies, waits for them, and re-layouts: 2.73 us -> 0.72 us
    pallas_call x1, Pallas kernels: 5.53 us -> 3.6 us  [place(): pl.pallas_call(place_kernel, out_shape=[jax.ShapeDtypeStruct((S, 128 * B)...]
  transfers between devices with their start and end apart: 13 -> 10, of which waited for: 8 -> 7; matrix products, arithmetic and copies ran while one was open for 2% -> 1% of each run, Pallas kernels for 4% -> 3%
where the time goes in v2:
time: 145 us; the launch traced here: 144 us
  waiting for transfers between devices  63.8 us (44%)
  starting transfers between devices  63.1 us (44%)
  Pallas kernels  15.1 us (10%)
    all_to_all x1, waiting for transfers between devices, shards(): exchange(gather(block_cols, block_rows, shots_in, cotangent))  40.2 us
    all_to_all x1, starting transfers between devices, shards(): exchange(gather(block_cols, block_rows, shots_in, cotangent))  20.5 us
    ppermute x3, starting transfers between devices, shards(): permute(part, perm=moves(lambda a, b, c, d=d: (a, (b + 2 * d + 2) % Y, c)))  14.4 us
    all_to_all x1, starting transfers between devices, shards(): back = exchange(result.reshape(OWNERS, S, MESSAGE + SCALES))  12.9 us
    ppermute x3, waiting for transfers between devices, shards(): permute(part, perm=moves(lambda a, b, c, d=d: (a, (b + 2 * d + 2) % Y, c)))  8.92 us
    ppermute x1, waiting for transfers between devices, shards(): total = keep + permute(send, perm=moves(lambda a, b, c: (a ^ 1, b, c)))  8.37 us
    pallas_call x1, Pallas kernels, gather(): pl.pallas_call(gather_kernel, out_shape=jax.ShapeDtypeStruct((OWNERS, S,...  3.87 us
    ppermute x1, waiting for transfers between devices, shards(): total = total + permute(send, perm=moves(lambda a, b, c: (a ^ 2, b, c)))  3.74 us
  transfers between devices with their start and end apart: 10, of which 7 were waited for; matrix products, arithmetic and copies ran while one was open for 1% of the time, Pallas kernels for 3%

profile of v2, /device:TPU:1, one launch (start us, length us, event | category | flops | bytes accessed | tf_op | source)
XLA Modules:
  0.0 143.9 jit_solution(6679154769881844350)
XLA Ops:
  0.6 3.9 %gather.1 = bf16[16,8,6144]{2,1,0:T(8,128)(2,1)} custom-call(s32[256]{0:T(256)} %cols.3, s32[256]{0:T(256)} %rows.3, bf16[8,32768]{1,0:T(8,128)(2,1)} %x_ref.1, bf16[8,32768]{1,0:T(8,128)(2,1)} %g_ref.1), custom_call_target="tpu_custom_call" | custom-call | tf_op jit(solution)/shard_map/gather/pallas_call | solution.py:65
  4.5 20.5 %all-to-all-start = ((bf16[16,8,6144]{2,1,0:T(8,128)(2,1)}), bf16[16,8,6144]{2,1,0:T(8,128)(2,1)S(1)}, u32[]{:S(2)}, u32[]{:S(2)}) async-start(bf16[16,8,6144]{2,1,0:T(8,128)(2,1)} %gather.1), calls=%async_computation | async-start | bytes 3145728 | tf_op jit(solution)/shard_map/all_to_all | solution.py:275
  25.0 40.2 %all-to-all-done = bf16[16,8,6144]{2,1,0:T(8,128)(2,1)S(1)} async-done(((bf16[16,8,6144]{2,1,0:T(8,128)(2,1)}), bf16[16,8,6144]{2,1,0:T(8,128)(2,1)S(1)}, u32[]{:S(2)}, u32[]{:S(2)}) %all-to-all-start) | async-done | bytes 1572896 | tf_op jit(solution)/shard_map/all_to_all | solution.py:275
  65.3 3.7 %collective-permute-start = (bf16[128,3072]{1,0:T(8,128)(2,1)S(1)}, bf16[128,3072]{1,0:T(8,128)(2,1)S(1)}, u32[]{:S(2)}, u32[]{:S(2)}) collective-permute-start(bf16[128,3072]{1,0:T(8,128)(2,1)S(1)} %constant_dynamic-slice_fusion), channel_id=1, source_target_pairs={{0,16},{1,17},{2,18},{3,19},{4,20},{5,21},{6,22},{7,23},{8,24},{9,... | collective-permute-start | bytes 2359304 | tf_op jit(solution)/shard_map/ppermute | solution.py:277
  69.1 1.8 %collective-permute-done.other_ref = bf16[128,3072]{1,0:T(8,128)(2,1)S(1)} collective-permute-done((bf16[128,3072]{1,0:T(8,128)(2,1)S(1)}, bf16[128,3072]{1,0:T(8,128)(2,1)S(1)}, u32[]{:S(2)}, u32[]{:S(2)}) %collective-permute-start) | collective-permute-done | bytes 786464 | tf_op jit(solution)/shard_map/ppermute | solution.py:277
  70.8 3.0 %grad.1 = (s16[128,2176]{1,0:T(8,128)(2,1)}, f32[128,2048]{1,0:T(8,128)S(1)}) custom-call(s32[3]{0:T(128)S(1)} %pad_add_fusion.ids, bf16[128,6144]{1,0:T(8,128)(2,1)S(1)} %bitcast.23, bf16[128,3072]{1,0:T(8,128)(2,1)S(1)} %collective-permute-done.other_ref), custom_call_target="tpu_custom_call" | custom-call | tf_op jit(solution)/shard_map/grad/pallas_call | solution.py:158
  73.8 3.3 %collective-permute-start.1 = (s16[128,2176]{1,0:T(8,128)(2,1)}, s16[128,2176]{1,0:T(8,128)(2,1)S(1)}, u32[]{:S(2)}, u32[]{:S(2)}) collective-permute-start(s16[128,2176]{1,0:T(8,128)(2,1)} %get-tuple-element.16), channel_id=1, source_target_pairs={{0,32},{1,33},{2,34},{3,35},{4,36},{5,37},{6,38},{7,39},{8,40},{9,... | collective-permute-start | bytes 1671176 | tf_op jit(solution)/shard_map/ppermute | solution.py:280
  77.1 2.5 %apply.1 = s16[128,6272]{1,0:T(8,128)(2,1)} custom-call(bf16[128,6144]{1,0:T(8,128)(2,1)S(1)} %bitcast.24, bf16[16,256,256]{2,1,0:T(8,128)(2,1)S(1)} %copy-done.2, f32[128,2048]{1,0:T(8,128)S(1)} %get-tuple-element.13.after_ref.keep_ref), custom_call_target="tpu_custom_call" | custom-call | flops 5000000000 | bytes 20000000 | tf_op jit(solution)/shard_map/apply/pallas_call | solution.py:170
  79.6 12.9 %all-to-all-start.1 = ((s16[16,8,6272]{2,1,0:T(8,128)(2,1)}), s16[16,8,6272]{2,1,0:T(8,128)(2,1)S(1)}, u32[]{:S(2)}, u32[]{:S(2)}) async-start(s16[16,8,6272]{2,1,0:T(8,128)(2,1)} %bitcast.4), calls=%async_computation.1 | async-start | bytes 3211264 | tf_op jit(solution)/shard_map/all_to_all | solution.py:281
  92.4 1.5 %pairs.1 = (s16[32,2176]{1,0:T(8,128)(2,1)S(1)}, s16[32,2176]{1,0:T(8,128)(2,1)S(1)}, s16[32,2176]{1,0:T(8,128)(2,1)S(1)}, f32[32,2048]{1,0:T(8,128)S(1)}) custom-call(s32[3]{0:T(128)S(1)} %pad_add_fusion.ids, f32[128,2048]{1,0:T(8,128)S(1)} %get-tuple-element.13.after_ref.keep_ref, s16[128,2176]{1,0:T(8,128)(2,1)S(1)} %collective-permute-done.1.got_ref), custom_call_target="tpu_custom_call" | custom-call | flops 20000000000 | bytes 1000000 | tf_op jit(solution)/shard_map/pairs/pallas_call | solution.py:198
  94.0 4.4 %collective-permute-start.2 = (s16[32,2176]{1,0:T(8,128)(2,1)S(1)}, s16[32,2176]{1,0:T(8,128)(2,1)S(1)}, u32[]{:S(2)}, u32[]{:S(2)}) collective-permute-start(s16[32,2176]{1,0:T(8,128)(2,1)S(1)} %get-tuple-element.18), channel_id=1, source_target_pairs={{0,64},{1,65},{2,66},{3,67},{4,68},{5,69},{6,70},{7,71},{8,72},{9,... | collective-permute-start | bytes 417800 | tf_op jit(solution)/shard_map/ppermute | solution.py:284
  98.4 5.2 %collective-permute-start.3 = (s16[32,2176]{1,0:T(8,128)(2,1)S(1)}, s16[32,2176]{1,0:T(8,128)(2,1)S(1)}, u32[]{:S(2)}, u32[]{:S(2)}) collective-permute-start(s16[32,2176]{1,0:T(8,128)(2,1)S(1)} %get-tuple-element.19), channel_id=1, source_target_pairs={{0,128},{1,129},{2,130},{3,131},{4,132},{5,133},{6,134},{7,135},{8... | collective-permute-start | bytes 417800 | tf_op jit(solution)/shard_map/ppermute | solution.py:284
  103.7 4.7 %collective-permute-start.4 = (s16[32,2176]{1,0:T(8,128)(2,1)S(1)}, s16[32,2176]{1,0:T(8,128)(2,1)S(1)}, u32[]{:S(2)}, u32[]{:S(2)}) collective-permute-start(s16[32,2176]{1,0:T(8,128)(2,1)S(1)} %get-tuple-element.20), channel_id=1, source_target_pairs={{0,192},{1,193},{2,194},{3,195},{4,196},{5,197},{6,198},{7,199},{8... | collective-permute-start | bytes 417800 | tf_op jit(solution)/shard_map/ppermute | solution.py:284
  108.4 3.3 %collective-permute-done.3.b_ref = s16[32,2176]{1,0:T(8,128)(2,1)S(1)} collective-permute-done((s16[32,2176]{1,0:T(8,128)(2,1)S(1)}, s16[32,2176]{1,0:T(8,128)(2,1)S(1)}, u32[]{:S(2)}, u32[]{:S(2)}) %collective-permute-start.3) | collective-permute-done | bytes 139296 | tf_op jit(solution)/shard_map/ppermute | solution.py:284
  111.7 5.6 %collective-permute-done.4.c_ref = s16[32,2176]{1,0:T(8,128)(2,1)S(1)} collective-permute-done((s16[32,2176]{1,0:T(8,128)(2,1)S(1)}, s16[32,2176]{1,0:T(8,128)(2,1)S(1)}, u32[]{:S(2)}, u32[]{:S(2)}) %collective-permute-start.4) | collective-permute-done | bytes 139296 | tf_op jit(solution)/shard_map/ppermute | solution.py:284
  117.3 0.7 halves.1
  118.1 2.7 %collective-permute-start.5 = (f32[16,2048]{1,0:T(8,128)S(1)}, f32[16,2048]{1,0:T(8,128)S(1)}, u32[]{:S(2)}, u32[]{:S(2)}) collective-permute-start(f32[16,2048]{1,0:T(8,128)S(1)} %get-tuple-element.22), channel_id=1, source_target_pairs={{0,256},{1,257},{2,258},{3,259},{4,260},{5,261},{6,262},{7,263},{8... | collective-permute-start | bytes 393224 | tf_op jit(solution)/shard_map/ppermute | solution.py:287
  120.8 8.4 %collective-permute-done.5 = f32[16,2048]{1,0:T(8,128)S(1)} collective-permute-done((f32[16,2048]{1,0:T(8,128)S(1)}, f32[16,2048]{1,0:T(8,128)S(1)}, u32[]{:S(2)}, u32[]{:S(2)}) %collective-permute-start.5) | collective-permute-done | bytes 131104 | tf_op jit(solution)/shard_map/ppermute | solution.py:287
  129.2 2.1 %collective-permute-start.6 = (f32[8,2048]{1,0:T(8,128)S(1)}, f32[8,2048]{1,0:T(8,128)S(1)}, u32[]{:S(2)}, u32[]{:S(2)}) collective-permute-start(f32[8,2048]{1,0:T(8,128)S(1)} %dynamic-slice_bitcast_fusion), channel_id=1, source_target_pairs={{0,512},{1,513},{2,514},{3,515},{4,516},{5,517},{6,518},{7,519},{8... | collective-permute-start | bytes 196616 | tf_op jit(solution)/shard_map/ppermute | solution.py:291
  131.4 3.7 %collective-permute-done.6 = f32[8,2048]{1,0:T(8,128)S(1)} collective-permute-done((f32[8,2048]{1,0:T(8,128)S(1)}, f32[8,2048]{1,0:T(8,128)S(1)}, u32[]{:S(2)}, u32[]{:S(2)}) %collective-permute-start.6) | collective-permute-done | bytes 65568 | tf_op jit(solution)/shard_map/ppermute | solution.py:291
  135.2 3.5 %collective-permute-start.7 = (f32[4,8,256]{2,1,0:T(8,128)S(1)}, f32[4,8,256]{2,1,0:T(8,128)S(1)}, u32[]{:S(2)}, u32[]{:S(2)}) collective-permute-start(f32[4,8,256]{2,1,0:T(8,128)S(1)} %get-tuple-element.27), channel_id=1, source_target_pairs={{0,16},{1,17},{2,18},{3,19},{4,20},{5,21},{6,22},{7,23},{8,24},{9,... | collective-permute-start | bytes 98312 | tf_op jit(solution)/shard_map/ppermute | solution.py:294
  138.7 0.8 collective-permute-done.7
  139.6 0.7 copy.8
  140.3 3.6 %place.1 = (bf16[8,32768]{1,0:T(8,128)(2,1)}, bf16[8,32768]{1,0:T(8,128)(2,1)}) custom-call(s32[256]{0:T(256)S(1)} %copy-done, s32[256]{0:T(256)S(1)} %copy-done.1, s16[16,8,6272]{2,1,0:T(8,128)(2,1)S(1)} %all-to-all-done.1.in_ref), custom_call_target="tpu_custom_call" | custom-call | tf_op jit(solution)/shard_map/place/pallas_call | solution.py:256
  (17 shorter events, 0.3 us)
Async XLA Ops:
  4.5 60.7 %all-to-all-start = ((bf16[16,8,6144]{2,1,0:T(8,128)(2,1)}), bf16[16,8,6144]{2,1,0:T(8,128)(2,1)S(1)}, u32[]{:S(2)}, u32[]{:S(2)}) async-start(bf16[16,8,6144]{2,1,0:T(8,128)(2,1)} %gather.1), calls=%async_computation | async-start | bytes 3145728 | tf_op jit(solution)/shard_map/all_to_all | solution.py:275
  65.3 5.6 %collective-permute-start = (bf16[128,3072]{1,0:T(8,128)(2,1)S(1)}, bf16[128,3072]{1,0:T(8,128)(2,1)S(1)}, u32[]{:S(2)}, u32[]{:S(2)}) collective-permute-start(bf16[128,3072]{1,0:T(8,128)(2,1)S(1)} %constant_dynamic-slice_fusion), channel_id=1, source_target_pairs={{0,16},{1,17},{2,18},{3,19},{4,20},{5,21},{6,22},{7,23},{8,24},{9,... | collective-permute-start | bytes 2359304 | tf_op jit(solution)/shard_map/ppermute | solution.py:277
  69.0 8.1 %copy-start.2 = (bf16[16,256,256]{2,1,0:T(8,128)(2,1)S(1)}, bf16[16,256,256]{2,1,0:T(8,128)(2,1)}, u32[]{:S(2)}) copy-start(bf16[16,256,256]{2,1,0:T(8,128)(2,1)} %w_ref.1) | copy-start | bytes 6291460
  73.8 18.6 %collective-permute-start.1 = (s16[128,2176]{1,0:T(8,128)(2,1)}, s16[128,2176]{1,0:T(8,128)(2,1)S(1)}, u32[]{:S(2)}, u32[]{:S(2)}) collective-permute-start(s16[128,2176]{1,0:T(8,128)(2,1)} %get-tuple-element.16), channel_id=1, source_target_pairs={{0,32},{1,33},{2,34},{3,35},{4,36},{5,37},{6,38},{7,39},{8,40},{9,... | collective-permute-start | bytes 1671176 | tf_op jit(solution)/shard_map/ppermute | solution.py:280
  79.6 60.7 %all-to-all-start.1 = ((s16[16,8,6272]{2,1,0:T(8,128)(2,1)}), s16[16,8,6272]{2,1,0:T(8,128)(2,1)S(1)}, u32[]{:S(2)}, u32[]{:S(2)}) async-start(s16[16,8,6272]{2,1,0:T(8,128)(2,1)} %bitcast.4), calls=%async_computation.1 | async-start | bytes 3211264 | tf_op jit(solution)/shard_map/all_to_all | solution.py:281
  94.0 46.3 %copy-start = (s32[256]{0:T(256)S(1)}, s32[256]{0:T(256)}, u32[]{:S(2)}) copy-start(s32[256]{0:T(256)} %cols.3) | copy-start | bytes 3076
  94.0 46.3 %copy-start.1 = (s32[256]{0:T(256)S(1)}, s32[256]{0:T(256)}, u32[]{:S(2)}) copy-start(s32[256]{0:T(256)} %rows.3) | copy-start | bytes 3076
  94.0 14.4 %collective-permute-start.2 = (s16[32,2176]{1,0:T(8,128)(2,1)S(1)}, s16[32,2176]{1,0:T(8,128)(2,1)S(1)}, u32[]{:S(2)}, u32[]{:S(2)}) collective-permute-start(s16[32,2176]{1,0:T(8,128)(2,1)S(1)} %get-tuple-element.18), channel_id=1, source_target_pairs={{0,64},{1,65},{2,66},{3,67},{4,68},{5,69},{6,70},{7,71},{8,72},{9,... | collective-permute-start | bytes 417800 | tf_op jit(solution)/shard_map/ppermute | solution.py:284
  98.4 13.3 %collective-permute-start.3 = (s16[32,2176]{1,0:T(8,128)(2,1)S(1)}, s16[32,2176]{1,0:T(8,128)(2,1)S(1)}, u32[]{:S(2)}, u32[]{:S(2)}) collective-permute-start(s16[32,2176]{1,0:T(8,128)(2,1)S(1)} %get-tuple-element.19), channel_id=1, source_target_pairs={{0,128},{1,129},{2,130},{3,131},{4,132},{5,133},{6,134},{7,135},{8... | collective-permute-start | bytes 417800 | tf_op jit(solution)/shard_map/ppermute | solution.py:284
  103.7 13.7 %collective-permute-start.4 = (s16[32,2176]{1,0:T(8,128)(2,1)S(1)}, s16[32,2176]{1,0:T(8,128)(2,1)S(1)}, u32[]{:S(2)}, u32[]{:S(2)}) collective-permute-start(s16[32,2176]{1,0:T(8,128)(2,1)S(1)} %get-tuple-element.20), channel_id=1, source_target_pairs={{0,192},{1,193},{2,194},{3,195},{4,196},{5,197},{6,198},{7,199},{8... | collective-permute-start | bytes 417800 | tf_op jit(solution)/shard_map/ppermute | solution.py:284
  118.1 11.1 %collective-permute-start.5 = (f32[16,2048]{1,0:T(8,128)S(1)}, f32[16,2048]{1,0:T(8,128)S(1)}, u32[]{:S(2)}, u32[]{:S(2)}) collective-permute-start(f32[16,2048]{1,0:T(8,128)S(1)} %get-tuple-element.22), channel_id=1, source_target_pairs={{0,256},{1,257},{2,258},{3,259},{4,260},{5,261},{6,262},{7,263},{8... | collective-permute-start | bytes 393224 | tf_op jit(solution)/shard_map/ppermute | solution.py:287
  129.2 5.9 %collective-permute-start.6 = (f32[8,2048]{1,0:T(8,128)S(1)}, f32[8,2048]{1,0:T(8,128)S(1)}, u32[]{:S(2)}, u32[]{:S(2)}) collective-permute-start(f32[8,2048]{1,0:T(8,128)S(1)} %dynamic-slice_bitcast_fusion), channel_id=1, source_target_pairs={{0,512},{1,513},{2,514},{3,515},{4,516},{5,517},{6,518},{7,519},{8... | collective-permute-start | bytes 196616 | tf_op jit(solution)/shard_map/ppermute | solution.py:291
  135.2 4.4 %collective-permute-start.7 = (f32[4,8,256]{2,1,0:T(8,128)S(1)}, f32[4,8,256]{2,1,0:T(8,128)S(1)}, u32[]{:S(2)}, u32[]{:S(2)}) collective-permute-start(f32[4,8,256]{2,1,0:T(8,128)S(1)} %get-tuple-element.27), channel_id=1, source_target_pairs={{0,16},{1,17},{2,18},{3,19},{4,20},{5,21},{6,22},{7,23},{8,24},{9,... | collective-permute-start | bytes 98312 | tf_op jit(solution)/shard_map/ppermute | solution.py:294

commit v3 on v2

--- a/solution.py
+++ b/solution.py
@@ -16,6 +16,7 @@
 MESSAGE = 2 * HALF
 SCALES = 128
 STEPS = 16.0
+PAIR_STEPS = (1, 3, 2)
 ROOM = pltpu.CompilerParams(vmem_limit_bytes=24 * 2**20)
 
 
@@ -43,7 +44,7 @@
     ]
 
 
-LONG = pl.CostEstimate(flops=20_000_000_000, bytes_accessed=1_000_000, transcendentals=0)
+LONG = pl.CostEstimate(flops=80_000_000_000, bytes_accessed=1_000_000, transcendentals=0)
 
 
 def gather_kernel(cols, rows, x_ref, g_ref, out_ref):
@@ -187,7 +188,7 @@
         total_ref[...] = total.reshape(XL, 4, S, B)
         own_ref[:, at(j)] = total_ref[:, pl.ds(pair, 1)].reshape(32, B)
         for d in range(3):
-            q, e = fixed(total_ref[:, pl.ds(lax.rem(pair + d + 1, 4), 1)].reshape(32, B))
+            q, e = fixed(total_ref[:, pl.ds(lax.rem(pair + PAIR_STEPS[d], 4), 1)].reshape(32, B))
             outs[d][:, at(j)] = q
             scales[d].append(e)
     for d in range(3):
@@ -208,28 +209,60 @@
     )(ids, *here(keep, got))
 
 
-def halves_kernel(ids, own_ref, a_ref, b_ref, c_ref, keep_ref, send_ref, total_ref):
-    parity = lax.rem(ids[2], 2)
+def cut_kernel(ids, own_ref, a_ref, b_ref, c_ref, *refs):
+    outs, keep_ref, total_ref = refs[:3], refs[3], refs[4]
+    xl = ids[2]
+    ins = (a_ref, b_ref, c_ref)
+    before = [decoded(ref[:, 8 * B :]) for ref in ins]
+    scales = [[] for _ in range(3)]
+    for j in range(8):
+        total = own_ref[:, at(j)]
+        for ref, scale in zip(ins, before):
+            total = total + widened(ref[:, at(j)]) * scale[:, j : j + 1]
+        total_ref[...] = total.reshape(XL, S, B)
+        keep_ref[:, at(j)] = total_ref[xl]
+        for d in range(3):
+            q, e = fixed(total_ref[xl ^ (d + 1)])
+            outs[d][:, at(j)] = q
+            scales[d].append(e)
+    for d in range(3):
+        put_scales(outs[d], scales[d])
+
+
+def cut(ids, own, parts):
+    return pl.pallas_call(
+        cut_kernel,
+        out_shape=[pltpu.VMEM((S, PART), jnp.int16)] * 3 + [pltpu.VMEM((S, 8 * B), jnp.float32)],
+        in_specs=[SMEM] + vmem(4),
+        out_specs=vmem(4),
+        scratch_shapes=[pltpu.VMEM((XL, S, B), jnp.float32)],
+        compiler_params=ROOM,
+        name="cut",
+    )(ids, *here(own, *parts))
+
+
+def last_kernel(ids, own_ref, a_ref, b_ref, c_ref, mine_ref, send_ref):
     ins = (a_ref, b_ref, c_ref)
     scales = [decoded(ref[:, 8 * B :]) for ref in ins]
+    first = ids[0] == 0
     for j in range(8):
         total = own_ref[:, at(j)]
         for ref, scale in zip(ins, scales):
             total = total + widened(ref[:, at(j)]) * scale[:, j : j + 1]
-        total_ref[...] = total.reshape(2, 2, S, B)
-        keep_ref[:, at(j)] = total_ref[:, pl.ds(parity, 1)].reshape(16, B)
-        send_ref[:, at(j)] = total_ref[:, pl.ds(1 - parity, 1)].reshape(16, B)
-
-
-def halves(ids, own, parts):
-    return pl.pallas_call(
-        halves_kernel,
-        out_shape=[pltpu.VMEM((16, 8 * B), jnp.float32)] * 2,
+        total = total * 8192.0**-0.5
+        top, bottom = total[:4], total[4:]
+        mine_ref[j] = jnp.where(first, top, bottom)
+        send_ref[j] = jnp.where(first, bottom, top)
+
+
+def last(ids, own, parts):
+    return pl.pallas_call(
+        last_kernel,
+        out_shape=[pltpu.VMEM((8, 4, B), jnp.float32)] * 2,
         in_specs=[SMEM] + vmem(4),
         out_specs=vmem(2),
-        scratch_shapes=[pltpu.VMEM((2, 2, S, B), jnp.float32)],
-        compiler_params=ROOM,
-        name="halves",
+        compiler_params=ROOM,
+        name="last",
     )(ids, *here(own, *parts))
 
 
@@ -281,22 +314,15 @@
     back = exchange(result.reshape(OWNERS, S, MESSAGE + SCALES))
     *parts, own = pairs(ids, keep, got)
     parts = [
-        permute(part, perm=moves(lambda a, b, c, d=d: (a, (b + 2 * d + 2) % Y, c))) for d, part in enumerate(parts)
+        permute(part, perm=moves(lambda a, b, c, d=d: (a, (b + 2 * d) % Y, c))) for d, part in zip(PAIR_STEPS, parts)
     ]
-    keep, send = halves(ids, own, parts)
-    total = keep + permute(send, perm=moves(lambda a, b, c: (a ^ 1, b, c)))
-    total = total.reshape(2, S, 8 * B)
-    send = lax.dynamic_index_in_dim(total, 1 - xl // 2, 0, keepdims=False)
-    total = lax.dynamic_index_in_dim(total, xl // 2, 0, keepdims=False)
-    total = total + permute(send, perm=moves(lambda a, b, c: (a ^ 2, b, c)))
-    total = (total * (8192.0**-0.5)).reshape(2, 4, 8, B)
-    mine = lax.dynamic_index_in_dim(total, core, 0, keepdims=False)
-    swapped = permute(
-        lax.dynamic_index_in_dim(total, 1 - core, 0, keepdims=False), perm=moves(lambda a, b, c: (a, b, 1 - c))
-    )
-    weight_grad = jnp.where(
-        core == 0, jnp.concatenate([mine, swapped], axis=1), jnp.concatenate([swapped, mine], axis=1)
-    ).transpose(1, 0, 2)
+    *parts, own = cut(ids, own, parts)
+    parts = [
+        permute(part, perm=moves(lambda a, b, c, d=d: (a ^ (d + 1), b, c))) for d, part in enumerate(parts)
+    ]
+    mine, send = last(ids, own, parts)
+    swapped = permute(send, perm=moves(lambda a, b, c: (a, b, 1 - c)))
+    weight_grad = jnp.where(core == 0, jnp.concatenate([mine, swapped]), jnp.concatenate([swapped, mine]))
     shots_out, input_grad = place(block_cols, block_rows, back)
     return shots_out, input_grad, weight_grad
 

time: 145 us -> 145 us (level)
  waiting for transfers between devices: 63.8 us -> 52.5 us
  starting transfers between devices: 63.1 us -> 73.8 us
    ppermute x6 -> x7, waiting for transfers between devices: 21.9 us -> 10.6 us  [the longest x3 7.64 us: shards(): permute(part, perm=moves(lambda a, b, c, d=d: (a, (b + 2 * d) % Y, c)))]
    ppermute x6 -> x7, starting transfers between devices: 22.8 us -> 33.5 us  [the longest x3 14.4 us: shards(): permute(part, perm=moves(lambda a, b, c, d=d: (a, (b + 2 * d) % Y, c)))]
  transfers between devices with their start and end apart: 10 -> 11, of which waited for: 7 -> 7; matrix products, arithmetic and copies ran while one was open for 1% -> 1% of each run, Pallas kernels for 3% -> 4%
where the time goes in v3:
time: 145 us; the launch traced here: 144 us
  starting transfers between devices  73.8 us (51%)
  waiting for transfers between devices  52.5 us (36%)
  Pallas kernels  16.2 us (11%)
    all_to_all x1, waiting for transfers between devices, shards(): exchange(gather(block_cols, block_rows, shots_in, cotangent))  40.2 us
    all_to_all x1, starting transfers between devices, shards(): exchange(gather(block_cols, block_rows, shots_in, cotangent))  20.5 us
    ppermute x3, starting transfers between devices, shards(): permute(part, perm=moves(lambda a, b, c, d=d: (a, (b + 2 * d) % Y, c)))  14.4 us
    all_to_all x1, starting transfers between devices, shards(): back = exchange(result.reshape(OWNERS, S, MESSAGE + SCALES))  12.9 us
    ppermute x1, starting transfers between devices, shards(): swapped = permute(send, perm=moves(lambda a, b, c: (a, b, 1 - c)))  9.85 us
    ppermute x3, starting transfers between devices, shards(): permute(part, perm=moves(lambda a, b, c, d=d: (a ^ d + 1, b, c)))  9.27 us
    ppermute x3, waiting for transfers between devices, shards(): permute(part, perm=moves(lambda a, b, c, d=d: (a, (b + 2 * d) % Y, c)))  7.64 us
    pallas_call x1, Pallas kernels, gather(): pl.pallas_call(gather_kernel, out_shape=jax.ShapeDtypeStruct((OWNERS, S,...  3.88 us
  transfers between devices with their start and end apart: 11, of which 7 were waited for; matrix products, arithmetic and copies ran while one was open for 1% of the time, Pallas kernels for 4%

profile of v3, /device:TPU:1, one launch (start us, length us, event | category | flops | bytes accessed | tf_op | source)
XLA Modules:
  0.0 144.3 jit_solution(1807945999297228636)
XLA Ops:
  0.6 3.9 %gather.1 = bf16[16,8,6144]{2,1,0:T(8,128)(2,1)} custom-call(s32[256]{0:T(256)} %cols.3, s32[256]{0:T(256)} %rows.3, bf16[8,32768]{1,0:T(8,128)(2,1)} %x_ref.1, bf16[8,32768]{1,0:T(8,128)(2,1)} %g_ref.1), custom_call_target="tpu_custom_call" | custom-call | tf_op jit(solution)/shard_map/gather/pallas_call | solution.py:66
  4.5 20.5 %all-to-all-start = ((bf16[16,8,6144]{2,1,0:T(8,128)(2,1)}), bf16[16,8,6144]{2,1,0:T(8,128)(2,1)S(1)}, u32[]{:S(2)}, u32[]{:S(2)}) async-start(bf16[16,8,6144]{2,1,0:T(8,128)(2,1)} %gather.1), calls=%async_computation | async-start | bytes 3145728 | tf_op jit(solution)/shard_map/all_to_all | solution.py:308
  25.1 40.2 %all-to-all-done = bf16[16,8,6144]{2,1,0:T(8,128)(2,1)S(1)} async-done(((bf16[16,8,6144]{2,1,0:T(8,128)(2,1)}), bf16[16,8,6144]{2,1,0:T(8,128)(2,1)S(1)}, u32[]{:S(2)}, u32[]{:S(2)}) %all-to-all-start) | async-done | bytes 1572896 | tf_op jit(solution)/shard_map/all_to_all | solution.py:308
  65.3 3.7 %collective-permute-start = (bf16[128,3072]{1,0:T(8,128)(2,1)S(1)}, bf16[128,3072]{1,0:T(8,128)(2,1)S(1)}, u32[]{:S(2)}, u32[]{:S(2)}) collective-permute-start(bf16[128,3072]{1,0:T(8,128)(2,1)S(1)} %constant_dynamic-slice_fusion), channel_id=1, source_target_pairs={{0,16},{1,17},{2,18},{3,19},{4,20},{5,21},{6,22},{7,23},{8,24},{9,... | collective-permute-start | bytes 2359304 | tf_op jit(solution)/shard_map/ppermute | solution.py:310
  69.1 1.8 %collective-permute-done.other_ref = bf16[128,3072]{1,0:T(8,128)(2,1)S(1)} collective-permute-done((bf16[128,3072]{1,0:T(8,128)(2,1)S(1)}, bf16[128,3072]{1,0:T(8,128)(2,1)S(1)}, u32[]{:S(2)}, u32[]{:S(2)}) %collective-permute-start) | collective-permute-done | bytes 786464 | tf_op jit(solution)/shard_map/ppermute | solution.py:310
  70.8 2.9 %grad.1 = (s16[128,2176]{1,0:T(8,128)(2,1)}, f32[128,2048]{1,0:T(8,128)S(1)}) custom-call(s32[3]{0:T(128)S(1)} %pad_add_fusion.ids, bf16[128,6144]{1,0:T(8,128)(2,1)S(1)} %bitcast.6, bf16[128,3072]{1,0:T(8,128)(2,1)S(1)} %collective-permute-done.other_ref), custom_call_target="tpu_custom_call" | custom-call | tf_op jit(solution)/shard_map/grad/pallas_call | solution.py:159
  73.8 3.3 %collective-permute-start.1 = (s16[128,2176]{1,0:T(8,128)(2,1)}, s16[128,2176]{1,0:T(8,128)(2,1)S(1)}, u32[]{:S(2)}, u32[]{:S(2)}) collective-permute-start(s16[128,2176]{1,0:T(8,128)(2,1)} %get-tuple-element.20), channel_id=1, source_target_pairs={{0,32},{1,33},{2,34},{3,35},{4,36},{5,37},{6,38},{7,39},{8,40},{9,... | collective-permute-start | bytes 1671176 | tf_op jit(solution)/shard_map/ppermute | solution.py:313
  77.1 2.5 %apply.1 = s16[128,6272]{1,0:T(8,128)(2,1)} custom-call(bf16[128,6144]{1,0:T(8,128)(2,1)S(1)} %bitcast.7, bf16[16,256,256]{2,1,0:T(8,128)(2,1)S(1)} %copy-done.2, f32[128,2048]{1,0:T(8,128)S(1)} %get-tuple-element.17.after_ref.keep_ref), custom_call_target="tpu_custom_call" | custom-call | flops 5000000000 | bytes 20000000 | tf_op jit(solution)/shard_map/apply/pallas_call | solution.py:171
  79.6 12.9 %all-to-all-start.1 = ((s16[16,8,6272]{2,1,0:T(8,128)(2,1)}), s16[16,8,6272]{2,1,0:T(8,128)(2,1)S(1)}, u32[]{:S(2)}, u32[]{:S(2)}) async-start(s16[16,8,6272]{2,1,0:T(8,128)(2,1)} %bitcast.4), calls=%async_computation.1 | async-start | bytes 3211264 | tf_op jit(solution)/shard_map/all_to_all | solution.py:314
  92.5 1.5 %pairs.1 = (s16[32,2176]{1,0:T(8,128)(2,1)S(1)}, s16[32,2176]{1,0:T(8,128)(2,1)S(1)}, s16[32,2176]{1,0:T(8,128)(2,1)S(1)}, f32[32,2048]{1,0:T(8,128)S(1)}) custom-call(s32[3]{0:T(128)S(1)} %pad_add_fusion.ids, f32[128,2048]{1,0:T(8,128)S(1)} %get-tuple-element.17.after_ref.keep_ref, s16[128,2176]{1,0:T(8,128)(2,1)S(1)} %collective-permute-done.1.got_ref), custom_call_target="tpu_custom_call" | custom-call | flops 80000000000 | bytes 1000000 | tf_op jit(solution)/shard_map/pairs/pallas_call | solution.py:199
  94.0 4.4 %collective-permute-start.2 = (s16[32,2176]{1,0:T(8,128)(2,1)S(1)}, s16[32,2176]{1,0:T(8,128)(2,1)S(1)}, u32[]{:S(2)}, u32[]{:S(2)}) collective-permute-start(s16[32,2176]{1,0:T(8,128)(2,1)S(1)} %get-tuple-element.22), channel_id=1, source_target_pairs={{0,64},{1,65},{2,66},{3,67},{4,68},{5,69},{6,70},{7,71},{8,72},{9,... | collective-permute-start | bytes 417800 | tf_op jit(solution)/shard_map/ppermute | solution.py:317
  98.4 3.1 %collective-permute-start.3 = (s16[32,2176]{1,0:T(8,128)(2,1)S(1)}, s16[32,2176]{1,0:T(8,128)(2,1)S(1)}, u32[]{:S(2)}, u32[]{:S(2)}) collective-permute-start(s16[32,2176]{1,0:T(8,128)(2,1)S(1)} %get-tuple-element.23), channel_id=1, source_target_pairs={{0,192},{1,193},{2,194},{3,195},{4,196},{5,197},{6,198},{7,199},{8... | collective-permute-start | bytes 417800 | tf_op jit(solution)/shard_map/ppermute | solution.py:317
  101.6 6.8 %collective-permute-start.4 = (s16[32,2176]{1,0:T(8,128)(2,1)S(1)}, s16[32,2176]{1,0:T(8,128)(2,1)S(1)}, u32[]{:S(2)}, u32[]{:S(2)}) collective-permute-start(s16[32,2176]{1,0:T(8,128)(2,1)S(1)} %get-tuple-element.24), channel_id=1, source_target_pairs={{0,128},{1,129},{2,130},{3,131},{4,132},{5,133},{6,134},{7,135},{8... | collective-permute-start | bytes 417800 | tf_op jit(solution)/shard_map/ppermute | solution.py:317
  108.4 1.2 collective-permute-done.3.b_ref
  109.6 6.5 %collective-permute-done.4.c_ref = s16[32,2176]{1,0:T(8,128)(2,1)S(1)} collective-permute-done((s16[32,2176]{1,0:T(8,128)(2,1)S(1)}, s16[32,2176]{1,0:T(8,128)(2,1)S(1)}, u32[]{:S(2)}, u32[]{:S(2)}) %collective-permute-start.4) | collective-permute-done | bytes 139296 | tf_op jit(solution)/shard_map/ppermute | solution.py:317
  116.1 1.2 cut.1
  117.2 1.9 %collective-permute-start.5 = (s16[8,2176]{1,0:T(8,128)(2,1)S(1)}, s16[8,2176]{1,0:T(8,128)(2,1)S(1)}, u32[]{:S(2)}, u32[]{:S(2)}) collective-permute-start(s16[8,2176]{1,0:T(8,128)(2,1)S(1)} %get-tuple-element.26), channel_id=1, source_target_pairs={{0,256},{1,257},{2,258},{3,259},{4,260},{5,261},{6,262},{7,263},{8... | collective-permute-start | bytes 104456 | tf_op jit(solution)/shard_map/ppermute | solution.py:321
  119.2 1.9 %collective-permute-start.6 = (s16[8,2176]{1,0:T(8,128)(2,1)S(1)}, s16[8,2176]{1,0:T(8,128)(2,1)S(1)}, u32[]{:S(2)}, u32[]{:S(2)}) collective-permute-start(s16[8,2176]{1,0:T(8,128)(2,1)S(1)} %get-tuple-element.27), channel_id=1, source_target_pairs={{0,512},{1,513},{2,514},{3,515},{4,516},{5,517},{6,518},{7,519},{8... | collective-permute-start | bytes 104456 | tf_op jit(solution)/shard_map/ppermute | solution.py:321
  121.1 5.4 %collective-permute-start.7 = (s16[8,2176]{1,0:T(8,128)(2,1)S(1)}, s16[8,2176]{1,0:T(8,128)(2,1)S(1)}, u32[]{:S(2)}, u32[]{:S(2)}) collective-permute-start(s16[8,2176]{1,0:T(8,128)(2,1)S(1)} %get-tuple-element.28), channel_id=1, source_target_pairs={{0,768},{1,769},{2,770},{3,771},{4,772},{5,773},{6,774},{7,775},{8... | collective-permute-start | bytes 104456 | tf_op jit(solution)/shard_map/ppermute | solution.py:321
  126.6 0.7 collective-permute-done.6.b_ref
  127.3 1.4 collective-permute-done.7.c_ref
  129.3 9.8 %collective-permute-start.8 = (f32[8,4,256]{2,1,0:T(4,128)S(1)}, f32[8,4,256]{2,1,0:T(4,128)S(1)}, u32[]{:S(2)}, u32[]{:S(2)}) collective-permute-start(f32[8,4,256]{2,1,0:T(4,128)S(1)} %get-tuple-element.30), channel_id=1, source_target_pairs={{0,16},{1,17},{2,18},{3,19},{4,20},{5,21},{6,22},{7,23},{8,24},{9,... | collective-permute-start | bytes 98312 | tf_op jit(solution)/shard_map/ppermute | solution.py:324
  139.2 0.8 collective-permute-done.8
  140.7 3.6 %place.1 = (bf16[8,32768]{1,0:T(8,128)(2,1)}, bf16[8,32768]{1,0:T(8,128)(2,1)}) custom-call(s32[256]{0:T(256)S(1)} %copy-done, s32[256]{0:T(256)S(1)} %copy-done.1, s16[16,8,6272]{2,1,0:T(8,128)(2,1)S(1)} %all-to-all-done.1.in_ref), custom_call_target="tpu_custom_call" | custom-call | tf_op jit(solution)/shard_map/place/pallas_call | solution.py:289
  (14 shorter events, 1.5 us)
Async XLA Ops:
  4.5 60.7 %all-to-all-start = ((bf16[16,8,6144]{2,1,0:T(8,128)(2,1)}), bf16[16,8,6144]{2,1,0:T(8,128)(2,1)S(1)}, u32[]{:S(2)}, u32[]{:S(2)}) async-start(bf16[16,8,6144]{2,1,0:T(8,128)(2,1)} %gather.1), calls=%async_computation | async-start | bytes 3145728 | tf_op jit(solution)/shard_map/all_to_all | solution.py:308
  65.3 5.6 %collective-permute-start = (bf16[128,3072]{1,0:T(8,128)(2,1)S(1)}, bf16[128,3072]{1,0:T(8,128)(2,1)S(1)}, u32[]{:S(2)}, u32[]{:S(2)}) collective-permute-start(bf16[128,3072]{1,0:T(8,128)(2,1)S(1)} %constant_dynamic-slice_fusion), channel_id=1, source_target_pairs={{0,16},{1,17},{2,18},{3,19},{4,20},{5,21},{6,22},{7,23},{8,24},{9,... | collective-permute-start | bytes 2359304 | tf_op jit(solution)/shard_map/ppermute | solution.py:310
  69.0 8.1 %copy-start.2 = (bf16[16,256,256]{2,1,0:T(8,128)(2,1)S(1)}, bf16[16,256,256]{2,1,0:T(8,128)(2,1)}, u32[]{:S(2)}) copy-start(bf16[16,256,256]{2,1,0:T(8,128)(2,1)} %w_ref.1) | copy-start | bytes 6291460
  73.8 18.7 %collective-permute-start.1 = (s16[128,2176]{1,0:T(8,128)(2,1)}, s16[128,2176]{1,0:T(8,128)(2,1)S(1)}, u32[]{:S(2)}, u32[]{:S(2)}) collective-permute-start(s16[128,2176]{1,0:T(8,128)(2,1)} %get-tuple-element.20), channel_id=1, source_target_pairs={{0,32},{1,33},{2,34},{3,35},{4,36},{5,37},{6,38},{7,39},{8,40},{9,... | collective-permute-start | bytes 1671176 | tf_op jit(solution)/shard_map/ppermute | solution.py:313
  79.6 61.1 %all-to-all-start.1 = ((s16[16,8,6272]{2,1,0:T(8,128)(2,1)}), s16[16,8,6272]{2,1,0:T(8,128)(2,1)S(1)}, u32[]{:S(2)}, u32[]{:S(2)}) async-start(s16[16,8,6272]{2,1,0:T(8,128)(2,1)} %bitcast.4), calls=%async_computation.1 | async-start | bytes 3211264 | tf_op jit(solution)/shard_map/all_to_all | solution.py:314
  92.4 48.2 %copy-start = (s32[256]{0:T(256)S(1)}, s32[256]{0:T(256)}, u32[]{:S(2)}) copy-start(s32[256]{0:T(256)} %cols.3) | copy-start | bytes 3076
  92.4 48.2 %copy-start.1 = (s32[256]{0:T(256)S(1)}, s32[256]{0:T(256)}, u32[]{:S(2)}) copy-start(s32[256]{0:T(256)} %rows.3) | copy-start | bytes 3076
  94.0 14.4 %collective-permute-start.2 = (s16[32,2176]{1,0:T(8,128)(2,1)S(1)}, s16[32,2176]{1,0:T(8,128)(2,1)S(1)}, u32[]{:S(2)}, u32[]{:S(2)}) collective-permute-start(s16[32,2176]{1,0:T(8,128)(2,1)S(1)} %get-tuple-element.22), channel_id=1, source_target_pairs={{0,64},{1,65},{2,66},{3,67},{4,68},{5,69},{6,70},{7,71},{8,72},{9,... | collective-permute-start | bytes 417800 | tf_op jit(solution)/shard_map/ppermute | solution.py:317
  98.4 11.1 %collective-permute-start.3 = (s16[32,2176]{1,0:T(8,128)(2,1)S(1)}, s16[32,2176]{1,0:T(8,128)(2,1)S(1)}, u32[]{:S(2)}, u32[]{:S(2)}) collective-permute-start(s16[32,2176]{1,0:T(8,128)(2,1)S(1)} %get-tuple-element.23), channel_id=1, source_target_pairs={{0,192},{1,193},{2,194},{3,195},{4,196},{5,197},{6,198},{7,199},{8... | collective-permute-start | bytes 417800 | tf_op jit(solution)/shard_map/ppermute | solution.py:317
  101.6 14.5 %collective-permute-start.4 = (s16[32,2176]{1,0:T(8,128)(2,1)S(1)}, s16[32,2176]{1,0:T(8,128)(2,1)S(1)}, u32[]{:S(2)}, u32[]{:S(2)}) collective-permute-start(s16[32,2176]{1,0:T(8,128)(2,1)S(1)} %get-tuple-element.24), channel_id=1, source_target_pairs={{0,128},{1,129},{2,130},{3,131},{4,132},{5,133},{6,134},{7,135},{8... | collective-permute-start | bytes 417800 | tf_op jit(solution)/shard_map/ppermute | solution.py:317
  117.2 9.3 %collective-permute-start.5 = (s16[8,2176]{1,0:T(8,128)(2,1)S(1)}, s16[8,2176]{1,0:T(8,128)(2,1)S(1)}, u32[]{:S(2)}, u32[]{:S(2)}) collective-permute-start(s16[8,2176]{1,0:T(8,128)(2,1)S(1)} %get-tuple-element.26), channel_id=1, source_target_pairs={{0,256},{1,257},{2,258},{3,259},{4,260},{5,261},{6,262},{7,263},{8... | collective-permute-start | bytes 104456 | tf_op jit(solution)/shard_map/ppermute | solution.py:321
  119.2 8.1 %collective-permute-start.6 = (s16[8,2176]{1,0:T(8,128)(2,1)S(1)}, s16[8,2176]{1,0:T(8,128)(2,1)S(1)}, u32[]{:S(2)}, u32[]{:S(2)}) collective-permute-start(s16[8,2176]{1,0:T(8,128)(2,1)S(1)} %get-tuple-element.27), channel_id=1, source_target_pairs={{0,512},{1,513},{2,514},{3,515},{4,516},{5,517},{6,518},{7,519},{8... | collective-permute-start | bytes 104456 | tf_op jit(solution)/shard_map/ppermute | solution.py:321
  121.1 7.5 %collective-permute-start.7 = (s16[8,2176]{1,0:T(8,128)(2,1)S(1)}, s16[8,2176]{1,0:T(8,128)(2,1)S(1)}, u32[]{:S(2)}, u32[]{:S(2)}) collective-permute-start(s16[8,2176]{1,0:T(8,128)(2,1)S(1)} %get-tuple-element.28), channel_id=1, source_target_pairs={{0,768},{1,769},{2,770},{3,771},{4,772},{5,773},{6,774},{7,775},{8... | collective-permute-start | bytes 104456 | tf_op jit(solution)/shard_map/ppermute | solution.py:321
  129.3 10.7 %collective-permute-start.8 = (f32[8,4,256]{2,1,0:T(4,128)S(1)}, f32[8,4,256]{2,1,0:T(4,128)S(1)}, u32[]{:S(2)}, u32[]{:S(2)}) collective-permute-start(f32[8,4,256]{2,1,0:T(4,128)S(1)} %get-tuple-element.30), channel_id=1, source_target_pairs={{0,16},{1,17},{2,18},{3,19},{4,20},{5,21},{6,22},{7,23},{8,24},{9,... | collective-permute-start | bytes 98312 | tf_op jit(solution)/shard_map/ppermute | solution.py:324

commit v4 on v3

--- a/solution.py
+++ b/solution.py
@@ -17,11 +17,18 @@
 SCALES = 128
 STEPS = 16.0
 PAIR_STEPS = (1, 3, 2)
+SMEM = pl.BlockSpec(memory_space=pltpu.SMEM)
+ANY = pl.BlockSpec(memory_space=pl.ANY)
 ROOM = pltpu.CompilerParams(vmem_limit_bytes=24 * 2**20)
 
 
 def device(xl, y, core, xh, z):
     return (((xl * Y + y) * CORES + core) * XH + xh) * Z + z
+
+
+def position():
+    dp = lax.axis_index("dp")
+    return lax.rem(dp, CORES), lax.rem(lax.div(dp, CORES), Y), lax.div(dp, CORES * Y)
 
 
 def groups():
@@ -47,34 +54,46 @@
 LONG = pl.CostEstimate(flops=80_000_000_000, bytes_accessed=1_000_000, transcendentals=0)
 
 
-def gather_kernel(cols, rows, x_ref, g_ref, out_ref):
-    base = pl.program_id(0) * 4
-    for p in range(4):
-        for half in range(2):
-            first = (base + p) * 16 + half * 8
-            for j in range(8):
-                col = pl.multiple_of(cols[first + j] * B, B)
-                at = half * HALF + j * B
-                out_ref[p, :, at : at + B] = x_ref[:, pl.ds(col, B)]
-            for j in range(4):
-                row = pl.multiple_of(rows[first + 2 * j] * B, B)
-                at = half * HALF + (8 + j) * B
-                out_ref[p, :, at : at + B] = g_ref[:, pl.ds(row, B)]
+def gather_kernel(cols, rows, x_hbm, g_hbm, out_hbm, x_ref, g_ref, out_ref, in_sems, out_sems):
+    loads = [
+        pltpu.make_async_copy(x_hbm, x_ref, in_sems.at[0]),
+        pltpu.make_async_copy(g_hbm, g_ref, in_sems.at[1]),
+    ]
+    for load in loads:
+        load.start()
+    for load in loads:
+        load.wait()
+    stores = []
+    for chunk in range(4):
+        owners = slice(chunk * 4, chunk * 4 + 4)
+        for p in range(owners.start, owners.stop):
+            for half in range(2):
+                first = p * 16 + half * 8
+                for j in range(8):
+                    col = pl.multiple_of(cols[first + j] * B, B)
+                    out_ref[p, :, at(half * 12 + j)] = x_ref[:, pl.ds(col, B)]
+                for j in range(4):
+                    row = pl.multiple_of(rows[first + 2 * j] * B, B)
+                    out_ref[p, :, at(half * 12 + 8 + j)] = g_ref[:, pl.ds(row, B)]
+        stores.append(pltpu.make_async_copy(out_ref.at[owners], out_hbm.at[owners], out_sems.at[chunk]))
+        stores[-1].start()
+    for store in stores:
+        store.wait()
 
 
 def gather(block_cols, block_rows, shots_in, cotangent):
+    message = (OWNERS, S, MESSAGE)
     return pl.pallas_call(
         gather_kernel,
-        out_shape=jax.ShapeDtypeStruct((OWNERS, S, MESSAGE), jnp.bfloat16),
-        grid_spec=pltpu.PrefetchScalarGridSpec(
-            num_scalar_prefetch=2,
-            grid=(4,),
-            in_specs=[
-                pl.BlockSpec((S, 128 * B), lambda i, c, r: (0, 0)),
-                pl.BlockSpec((S, 128 * B), lambda i, c, r: (0, 0)),
-            ],
-            out_specs=pl.BlockSpec((4, S, MESSAGE), lambda i, c, r: (i, 0, 0)),
-        ),
+        out_shape=jax.ShapeDtypeStruct(message, jnp.bfloat16),
+        in_specs=[SMEM, SMEM, ANY, ANY],
+        out_specs=ANY,
+        scratch_shapes=[pltpu.VMEM((S, 128 * B), jnp.bfloat16)] * 2
+        + [
+            pltpu.VMEM(message, jnp.bfloat16),
+            pltpu.SemaphoreType.DMA((2,)),
+            pltpu.SemaphoreType.DMA((4,)),
+        ],
         name="gather",
     )(block_cols, block_rows, shots_in, cotangent)
 
@@ -109,8 +128,9 @@
     ref[:, ref.shape[1] - SCALES :] = out.astype(jnp.int32).astype(jnp.int16)
 
 
-def grad_kernel(ids, in_ref, other_ref, send_ref, keep_ref, wg_ref):
-    core, parity = ids[0], lax.rem(ids[1], 2)
+def grad_kernel(in_ref, other_ref, after_ref, send_ref, keep_ref, wg_ref):
+    core, y, _ = position()
+    parity = y % 2
     scales = []
     for j in range(8):
         own = lambda slot: in_ref[:, pl.ds(pl.multiple_of(core * HALF + slot * B, B), B)]
@@ -125,9 +145,15 @@
     put_scales(send_ref, scales)
 
 
-def apply_kernel(in_ref, w_ref, after_ref, out_ref):
+def apply_kernel(in_ref, w_hbm, out_ref, w_ref, sems):
+    loads = [
+        pltpu.make_async_copy(w_hbm.at[2 * s : 2 * s + 2], w_ref.at[2 * s : 2 * s + 2], sems.at[s]) for s in range(8)
+    ]
+    for load in loads:
+        load.start()
     scales = []
     for s in range(8):
+        loads[s].wait()
         first = s // 4 * 12 + s % 4 * 2
         x0, x1, g = in_ref[:, at(first)], in_ref[:, at(first + 1)], in_ref[:, at(s // 4 * 12 + 8 + s % 4)]
         w0, w1 = w_ref[2 * s], w_ref[2 * s + 1]
@@ -151,36 +177,36 @@
     return [pl.BlockSpec(memory_space=pltpu.VMEM)] * n
 
 
-SMEM = pl.BlockSpec(memory_space=pltpu.SMEM)
 PART = 8 * B + SCALES
 
 
-def grad(ids, received, other):
+def grad(received, other, after):
     return pl.pallas_call(
         grad_kernel,
         out_shape=[pltpu.VMEM((128, PART), jnp.int16), pltpu.VMEM((128, 8 * B), jnp.float32)],
-        in_specs=[SMEM] + vmem(2),
+        in_specs=vmem(2) + [ANY],
         out_specs=vmem(2),
         scratch_shapes=[pltpu.VMEM((16, 2, S, B), jnp.float32)],
         compiler_params=ROOM,
         name="grad",
-    )(ids, *here(received, other))
-
-
-def apply(received, blocks, after):
+    )(*here(received, other), after)
+
+
+def apply(received, blocks):
     return pl.pallas_call(
         apply_kernel,
         out_shape=jax.ShapeDtypeStruct((OWNERS * S, MESSAGE + SCALES), jnp.int16),
-        in_specs=vmem(3),
+        in_specs=vmem(1) + [ANY],
+        scratch_shapes=[pltpu.VMEM((16, B, B), jnp.bfloat16), pltpu.SemaphoreType.DMA((8,))],
         compiler_params=ROOM,
         cost_estimate=pl.CostEstimate(flops=5_000_000_000, bytes_accessed=20_000_000, transcendentals=0),
         name="apply",
-    )(*here(received, blocks, after))
-
-
-def pairs_kernel(ids, keep_ref, got_ref, *refs):
+    )(*here(received), pltpu.with_memory_space_constraint(blocks, pltpu.HBM))
+
+
+def pairs_kernel(keep_ref, got_ref, *refs):
     outs, own_ref, total_ref = refs[:3], refs[3], refs[4]
-    pair = ids[1] // 2
+    pair = position()[1] // 2
     scale = decoded(got_ref[:, 8 * B :])
     scales = [[] for _ in range(3)]
     for j in range(8):
@@ -195,23 +221,23 @@
         put_scales(outs[d], scales[d])
 
 
-def pairs(ids, keep, got):
+def pairs(keep, got):
     return pl.pallas_call(
         pairs_kernel,
         out_shape=[pltpu.VMEM((32, PART), jnp.int16)] * 3
         + [pltpu.VMEM((32, 8 * B), jnp.float32)],
-        in_specs=[SMEM] + vmem(2),
+        in_specs=vmem(2),
         out_specs=vmem(4),
         scratch_shapes=[pltpu.VMEM((XL, 4, S, B), jnp.float32)],
         compiler_params=ROOM,
         cost_estimate=LONG,
         name="pairs",
-    )(ids, *here(keep, got))
-
-
-def cut_kernel(ids, own_ref, a_ref, b_ref, c_ref, *refs):
+    )(*here(keep, got))
+
+
+def cut_kernel(own_ref, a_ref, b_ref, c_ref, *refs):
     outs, keep_ref, total_ref = refs[:3], refs[3], refs[4]
-    xl = ids[2]
+    xl = position()[2]
     ins = (a_ref, b_ref, c_ref)
     before = [decoded(ref[:, 8 * B :]) for ref in ins]
     scales = [[] for _ in range(3)]
@@ -229,22 +255,22 @@
         put_scales(outs[d], scales[d])
 
 
-def cut(ids, own, parts):
+def cut(own, parts):
     return pl.pallas_call(
         cut_kernel,
         out_shape=[pltpu.VMEM((S, PART), jnp.int16)] * 3 + [pltpu.VMEM((S, 8 * B), jnp.float32)],
-        in_specs=[SMEM] + vmem(4),
+        in_specs=vmem(4),
         out_specs=vmem(4),
         scratch_shapes=[pltpu.VMEM((XL, S, B), jnp.float32)],
         compiler_params=ROOM,
         name="cut",
-    )(ids, *here(own, *parts))
-
-
-def last_kernel(ids, own_ref, a_ref, b_ref, c_ref, mine_ref, send_ref):
+    )(*here(own, *parts))
+
+
+def last_kernel(own_ref, a_ref, b_ref, c_ref, after_ref, mine_ref, send_ref):
     ins = (a_ref, b_ref, c_ref)
     scales = [decoded(ref[:, 8 * B :]) for ref in ins]
-    first = ids[0] == 0
+    first = position()[0] == 0
     for j in range(8):
         total = own_ref[:, at(j)]
         for ref, scale in zip(ins, scales):
@@ -255,18 +281,19 @@
         send_ref[j] = jnp.where(first, bottom, top)
 
 
-def last(ids, own, parts):
+def last(own, parts, after):
     return pl.pallas_call(
         last_kernel,
         out_shape=[pltpu.VMEM((8, 4, B), jnp.float32)] * 2,
-        in_specs=[SMEM] + vmem(4),
+        in_specs=vmem(5),
         out_specs=vmem(2),
         compiler_params=ROOM,
         name="last",
-    )(ids, *here(own, *parts))
-
-
-def place_kernel(cols, rows, in_ref, out_ref, grad_ref, first_ref, second_ref):
+    )(*here(own, *parts, after))
+
+
+def place_kernel(cols, rows, in_ref, out_ref, grad_ref, mark_ref, first_ref, second_ref):
+    mark_ref[...] = jnp.zeros_like(mark_ref)
     totals = (first_ref, second_ref)
     for ref in totals:
         ref[...] = jnp.zeros_like(ref)
@@ -288,7 +315,7 @@
 def place(block_cols, block_rows, back):
     return pl.pallas_call(
         place_kernel,
-        out_shape=[jax.ShapeDtypeStruct((S, 128 * B), jnp.bfloat16)] * 2,
+        out_shape=[jax.ShapeDtypeStruct((S, 128 * B), jnp.bfloat16)] * 2 + [pltpu.VMEM((S, 128), jnp.float32)],
         in_specs=[SMEM, SMEM] + vmem(1),
         scratch_shapes=[pltpu.VMEM((S, 128 * B), jnp.float32)] * 2,
         compiler_params=ROOM,
@@ -297,9 +324,7 @@
 
 
 def shards(shots_in, cotangent, blocks, block_rows, block_cols):
-    dp = lax.axis_index("dp")
-    core, y, xl = dp % CORES, dp // CORES % Y, dp // (CORES * Y)
-    ids = jnp.stack([core, y, xl]).astype(jnp.int32)
+    core = position()[0]
     permute = functools.partial(lax.ppermute, axis_name=AXES)
     exchange = functools.partial(
         lax.all_to_all, axis_name=AXES, split_axis=0, concat_axis=0, axis_index_groups=groups(), tiled=True
@@ -308,22 +333,22 @@
     received = exchange(gather(block_cols, block_rows, shots_in, cotangent)).reshape(OWNERS * S, MESSAGE)
     theirs = lax.dynamic_slice_in_dim(received, (1 - core) * HALF, HALF, axis=1)
     other = permute(theirs, perm=moves(lambda a, b, c: (a, b, 1 - c)))
-    send, keep = grad(ids, received, other)
-    result = apply(received, blocks, keep)
+    result = apply(received, blocks)
+    send, keep = grad(received, other, result)
     got = permute(send, perm=moves(lambda a, b, c: (a, b ^ 1, c)))
     back = exchange(result.reshape(OWNERS, S, MESSAGE + SCALES))
-    *parts, own = pairs(ids, keep, got)
+    *parts, own = pairs(keep, got)
     parts = [
         permute(part, perm=moves(lambda a, b, c, d=d: (a, (b + 2 * d) % Y, c))) for d, part in zip(PAIR_STEPS, parts)
     ]
-    *parts, own = cut(ids, own, parts)
+    *parts, own = cut(own, parts)
     parts = [
         permute(part, perm=moves(lambda a, b, c, d=d: (a ^ (d + 1), b, c))) for d, part in enumerate(parts)
     ]
-    mine, send = last(ids, own, parts)
+    shots_out, input_grad, placed = place(block_cols, block_rows, back)
+    mine, send = last(own, parts, placed)
     swapped = permute(send, perm=moves(lambda a, b, c: (a, b, 1 - c)))
     weight_grad = jnp.where(core == 0, jnp.concatenate([mine, swapped]), jnp.concatenate([swapped, mine]))
-    shots_out, input_grad = place(block_cols, block_rows, back)
     return shots_out, input_grad, weight_grad
 
 

time: 145 us -> 145 us (level)
  starting transfers between devices: 73.8 us -> 71.2 us
  waiting for transfers between devices: 52.5 us -> 54.2 us
    all_to_all x1, waiting for transfers between devices: 0.01 us -> 9.9 us  [shards(): back = exchange(result.reshape(OWNERS, S, MESSAGE + SCALES))]
    ppermute x1, starting transfers between devices: 9.85 us -> 3.29 us  [shards(): swapped = permute(send, perm=moves(lambda a, b, c: (a, b, 1 - c)))]
    ppermute x3, waiting for transfers between devices: 7.64 us -> 3.17 us  [shards(): permute(part, perm=moves(lambda a, b, c, d=d: (a, (b + 2 * d) % Y, c)))]
    ppermute x3, starting transfers between devices: 9.27 us -> 12.3 us  [shards(): permute(part, perm=moves(lambda a, b, c, d=d: (a ^ d + 1, b, c)))]
    pallas_call x1, Pallas kernels: 2.46 us -> 5.41 us  [apply(): pl.pallas_call(apply_kernel, out_shape=jax.ShapeDtypeStruct((OWNERS * S,...]
    ppermute x3, waiting for transfers between devices: 2.1 us -> 0.01 us  [shards(): permute(part, perm=moves(lambda a, b, c, d=d: (a ^ d + 1, b, c)))]
    ppermute x1, waiting for transfers between devices: 1.76 us -> 0.01 us  [shards(): other = permute(theirs, perm=moves(lambda a, b, c: (a, b, 1 - c)))]
  transfers between devices with their start and end apart: 11 -> 11, of which waited for: 7 -> 6; matrix products, arithmetic and copies ran while one was open for 1% -> 0% of each run, Pallas kernels for 4% -> 7%
where the time goes in v4:
time: 145 us; the launch traced here: 143 us
  starting transfers between devices  71.2 us (49%)
  waiting for transfers between devices  54.2 us (37%)
  Pallas kernels  16.4 us (11%)
    all_to_all x1, waiting for transfers between devices, shards(): exchange(gather(block_cols, block_rows, shots_in, cotangent))  40.2 us
    all_to_all x1, starting transfers between devices, shards(): exchange(gather(block_cols, block_rows, shots_in, cotangent))  20.5 us
    ppermute x3, starting transfers between devices, shards(): permute(part, perm=moves(lambda a, b, c, d=d: (a, (b + 2 * d) % Y, c)))  15.3 us
    all_to_all x1, starting transfers between devices, shards(): back = exchange(result.reshape(OWNERS, S, MESSAGE + SCALES))  12.9 us
    ppermute x3, starting transfers between devices, shards(): permute(part, perm=moves(lambda a, b, c, d=d: (a ^ d + 1, b, c)))  12.3 us
    all_to_all x1, waiting for transfers between devices, shards(): back = exchange(result.reshape(OWNERS, S, MESSAGE + SCALES))  9.9 us
    pallas_call x1, Pallas kernels, apply(): pl.pallas_call(apply_kernel, out_shape=jax.ShapeDtypeStruct((OWNERS * S,...  5.41 us
    ppermute x1, starting transfers between devices, shards(): other = permute(theirs, perm=moves(lambda a, b, c: (a, b, 1 - c)))  3.66 us
  transfers between devices with their start and end apart: 11, of which 6 were waited for; matrix products, arithmetic and copies ran while one was open for 0% of the time, Pallas kernels for 7%

profile of v4, /device:TPU:1, one launch (start us, length us, event | category | flops | bytes accessed | tf_op | source)
XLA Modules:
  0.0 143.3 jit_solution(17460040495093223779)
XLA Ops:
  0.6 3.3 %gather.1 = bf16[16,8,6144]{2,1,0:T(8,128)(2,1)} custom-call(s32[256]{0:T(256)} %cols.3, s32[256]{0:T(256)} %rows.3, bf16[8,32768]{1,0:T(8,128)(2,1)} %x_hbm.1, bf16[8,32768]{1,0:T(8,128)(2,1)} %g_hbm.1), custom_call_target="tpu_custom_call" | custom-call | tf_op jit(solution)/shard_map/gather/pallas_call | solution.py:86
  3.9 20.5 %all-to-all-start = ((bf16[16,8,6144]{2,1,0:T(8,128)(2,1)}), bf16[16,8,6144]{2,1,0:T(8,128)(2,1)S(1)}, u32[]{:S(2)}, u32[]{:S(2)}) async-start(bf16[16,8,6144]{2,1,0:T(8,128)(2,1)} %gather.1), calls=%async_computation | async-start | bytes 3145728 | tf_op jit(solution)/shard_map/all_to_all | solution.py:333
  24.4 40.2 %all-to-all-done = bf16[16,8,6144]{2,1,0:T(8,128)(2,1)S(1)} async-done(((bf16[16,8,6144]{2,1,0:T(8,128)(2,1)}), bf16[16,8,6144]{2,1,0:T(8,128)(2,1)S(1)}, u32[]{:S(2)}, u32[]{:S(2)}) %all-to-all-start) | async-done | bytes 1572896 | tf_op jit(solution)/shard_map/all_to_all | solution.py:333
  64.7 3.7 %collective-permute-start = (bf16[128,3072]{1,0:T(8,128)(2,1)S(1)}, bf16[128,3072]{1,0:T(8,128)(2,1)S(1)}, u32[]{:S(2)}, u32[]{:S(2)}) collective-permute-start(bf16[128,3072]{1,0:T(8,128)(2,1)S(1)} %constant_dynamic-slice_fusion), channel_id=1, source_target_pairs={{0,16},{1,17},{2,18},{3,19},{4,20},{5,21},{6,22},{7,23},{8,24},{9,... | collective-permute-start | bytes 2359304 | tf_op jit(solution)/shard_map/ppermute | solution.py:335
  68.3 5.4 %apply.1.after_ref = s16[128,6272]{1,0:T(8,128)(2,1)} custom-call(bf16[128,6144]{1,0:T(8,128)(2,1)S(1)} %bitcast.3, bf16[16,256,256]{2,1,0:T(8,128)(2,1)} %w_hbm.1), custom_call_target="tpu_custom_call" | custom-call | flops 5000000000 | bytes 20000000 | tf_op jit(solution)/shard_map/apply/pallas_call | solution.py:196
  73.8 2.3 %grad.1 = (s16[128,2176]{1,0:T(8,128)(2,1)}, f32[128,2048]{1,0:T(8,128)S(1)}) custom-call(bf16[128,6144]{1,0:T(8,128)(2,1)S(1)} %bitcast.4, bf16[128,3072]{1,0:T(8,128)(2,1)S(1)} %collective-permute-done.other_ref, s16[128,6272]{1,0:T(8,128)(2,1)} %apply.1.after_ref), custom_call_target="tpu_custom_call" | custom-call | tf_op jit(solution)/shard_map/grad/pallas_call | solution.py:184
  76.1 3.3 %collective-permute-start.1 = (s16[128,2176]{1,0:T(8,128)(2,1)}, s16[128,2176]{1,0:T(8,128)(2,1)S(1)}, u32[]{:S(2)}, u32[]{:S(2)}) collective-permute-start(s16[128,2176]{1,0:T(8,128)(2,1)} %get-tuple-element.21), channel_id=1, source_target_pairs={{0,32},{1,33},{2,34},{3,35},{4,36},{5,37},{6,38},{7,39},{8,40},{9,... | collective-permute-start | bytes 1671176 | tf_op jit(solution)/shard_map/ppermute | solution.py:338
  79.4 12.9 %all-to-all-start.1 = ((s16[16,8,6272]{2,1,0:T(8,128)(2,1)}), s16[16,8,6272]{2,1,0:T(8,128)(2,1)S(1)}, u32[]{:S(2)}, u32[]{:S(2)}) async-start(s16[16,8,6272]{2,1,0:T(8,128)(2,1)} %bitcast.1), calls=%async_computation.1 | async-start | bytes 3211264 | tf_op jit(solution)/shard_map/all_to_all | solution.py:339
  92.3 0.1 collective-permute-done.1.got_ref
  92.4 1.0 pairs.1
  93.4 4.4 %collective-permute-start.2 = (s16[32,2176]{1,0:T(8,128)(2,1)S(1)}, s16[32,2176]{1,0:T(8,128)(2,1)S(1)}, u32[]{:S(2)}, u32[]{:S(2)}) collective-permute-start(s16[32,2176]{1,0:T(8,128)(2,1)S(1)} %get-tuple-element.23), channel_id=1, source_target_pairs={{0,64},{1,65},{2,66},{3,67},{4,68},{5,69},{6,70},{7,71},{8,72},{9,... | collective-permute-start | bytes 417800 | tf_op jit(solution)/shard_map/ppermute | solution.py:342
  97.9 4.0 %collective-permute-start.3 = (s16[32,2176]{1,0:T(8,128)(2,1)S(1)}, s16[32,2176]{1,0:T(8,128)(2,1)S(1)}, u32[]{:S(2)}, u32[]{:S(2)}) collective-permute-start(s16[32,2176]{1,0:T(8,128)(2,1)S(1)} %get-tuple-element.24), channel_id=1, source_target_pairs={{0,192},{1,193},{2,194},{3,195},{4,196},{5,197},{6,198},{7,199},{8... | collective-permute-start | bytes 417800 | tf_op jit(solution)/shard_map/ppermute | solution.py:342
  101.9 6.8 %collective-permute-start.4 = (s16[32,2176]{1,0:T(8,128)(2,1)S(1)}, s16[32,2176]{1,0:T(8,128)(2,1)S(1)}, u32[]{:S(2)}, u32[]{:S(2)}) collective-permute-start(s16[32,2176]{1,0:T(8,128)(2,1)S(1)} %get-tuple-element.25), channel_id=1, source_target_pairs={{0,128},{1,129},{2,130},{3,131},{4,132},{5,133},{6,134},{7,135},{8... | collective-permute-start | bytes 417800 | tf_op jit(solution)/shard_map/ppermute | solution.py:342
  108.8 2.9 %collective-permute-done.3.b_ref = s16[32,2176]{1,0:T(8,128)(2,1)S(1)} collective-permute-done((s16[32,2176]{1,0:T(8,128)(2,1)S(1)}, s16[32,2176]{1,0:T(8,128)(2,1)S(1)}, u32[]{:S(2)}, u32[]{:S(2)}) %collective-permute-start.3) | collective-permute-done | bytes 139296 | tf_op jit(solution)/shard_map/ppermute | solution.py:342
  111.7 0.3 collective-permute-done.4.c_ref
  111.9 0.7 cut.1
  112.6 4.4 %collective-permute-start.5 = (s16[8,2176]{1,0:T(8,128)(2,1)S(1)}, s16[8,2176]{1,0:T(8,128)(2,1)S(1)}, u32[]{:S(2)}, u32[]{:S(2)}) collective-permute-start(s16[8,2176]{1,0:T(8,128)(2,1)S(1)} %get-tuple-element.27), channel_id=1, source_target_pairs={{0,256},{1,257},{2,258},{3,259},{4,260},{5,261},{6,262},{7,263},{8... | collective-permute-start | bytes 104456 | tf_op jit(solution)/shard_map/ppermute | solution.py:346
  117.0 4.8 %collective-permute-start.6 = (s16[8,2176]{1,0:T(8,128)(2,1)S(1)}, s16[8,2176]{1,0:T(8,128)(2,1)S(1)}, u32[]{:S(2)}, u32[]{:S(2)}) collective-permute-start(s16[8,2176]{1,0:T(8,128)(2,1)S(1)} %get-tuple-element.28), channel_id=1, source_target_pairs={{0,512},{1,513},{2,514},{3,515},{4,516},{5,517},{6,518},{7,519},{8... | collective-permute-start | bytes 104456 | tf_op jit(solution)/shard_map/ppermute | solution.py:346
  121.8 3.1 %collective-permute-start.7 = (s16[8,2176]{1,0:T(8,128)(2,1)S(1)}, s16[8,2176]{1,0:T(8,128)(2,1)S(1)}, u32[]{:S(2)}, u32[]{:S(2)}) collective-permute-start(s16[8,2176]{1,0:T(8,128)(2,1)S(1)} %get-tuple-element.29), channel_id=1, source_target_pairs={{0,768},{1,769},{2,770},{3,771},{4,772},{5,773},{6,774},{7,775},{8... | collective-permute-start | bytes 104456 | tf_op jit(solution)/shard_map/ppermute | solution.py:346
  124.9 9.9 %all-to-all-done.1.in_ref = s16[16,8,6272]{2,1,0:T(8,128)(2,1)S(1)} async-done(((s16[16,8,6272]{2,1,0:T(8,128)(2,1)}), s16[16,8,6272]{2,1,0:T(8,128)(2,1)S(1)}, u32[]{:S(2)}, u32[]{:S(2)}) %all-to-all-start.1) | async-done | bytes 1605664 | tf_op jit(solution)/shard_map/all_to_all | solution.py:339
  134.8 3.6 %place.1 = (bf16[8,32768]{1,0:T(8,128)(2,1)}, bf16[8,32768]{1,0:T(8,128)(2,1)}, f32[8,128]{1,0:T(8,128)S(1)}) custom-call(s32[256]{0:T(256)S(1)} %copy-done, s32[256]{0:T(256)S(1)} %copy-done.1, s16[16,8,6272]{2,1,0:T(8,128)(2,1)S(1)} %all-to-all-done.1.in_ref), custom_call_target="tpu_custom_call" | custom-call | tf_op jit(solution)/shard_map/place/pallas_call | solution.py:316
  138.6 3.3 %collective-permute-start.8 = (f32[8,4,256]{2,1,0:T(4,128)S(1)}, f32[8,4,256]{2,1,0:T(4,128)S(1)}, u32[]{:S(2)}, u32[]{:S(2)}) collective-permute-start(f32[8,4,256]{2,1,0:T(4,128)S(1)} %get-tuple-element.32), channel_id=1, source_target_pairs={{0,16},{1,17},{2,18},{3,19},{4,20},{5,21},{6,22},{7,23},{8,24},{9,... | collective-permute-start | bytes 98312 | tf_op jit(solution)/shard_map/ppermute | solution.py:350
  141.9 0.8 collective-permute-done.8
  142.7 0.6 maximum_select_fusion
  (11 shorter events, 0.2 us)
Async XLA Ops:
  3.9 60.7 %all-to-all-start = ((bf16[16,8,6144]{2,1,0:T(8,128)(2,1)}), bf16[16,8,6144]{2,1,0:T(8,128)(2,1)S(1)}, u32[]{:S(2)}, u32[]{:S(2)}) async-start(bf16[16,8,6144]{2,1,0:T(8,128)(2,1)} %gather.1), calls=%async_computation | async-start | bytes 3145728 | tf_op jit(solution)/shard_map/all_to_all | solution.py:333
  64.7 9.1 %collective-permute-start = (bf16[128,3072]{1,0:T(8,128)(2,1)S(1)}, bf16[128,3072]{1,0:T(8,128)(2,1)S(1)}, u32[]{:S(2)}, u32[]{:S(2)}) collective-permute-start(bf16[128,3072]{1,0:T(8,128)(2,1)S(1)} %constant_dynamic-slice_fusion), channel_id=1, source_target_pairs={{0,16},{1,17},{2,18},{3,19},{4,20},{5,21},{6,22},{7,23},{8,24},{9,... | collective-permute-start | bytes 2359304 | tf_op jit(solution)/shard_map/ppermute | solution.py:335
  76.1 16.3 %collective-permute-start.1 = (s16[128,2176]{1,0:T(8,128)(2,1)}, s16[128,2176]{1,0:T(8,128)(2,1)S(1)}, u32[]{:S(2)}, u32[]{:S(2)}) collective-permute-start(s16[128,2176]{1,0:T(8,128)(2,1)} %get-tuple-element.21), channel_id=1, source_target_pairs={{0,32},{1,33},{2,34},{3,35},{4,36},{5,37},{6,38},{7,39},{8,40},{9,... | collective-permute-start | bytes 1671176 | tf_op jit(solution)/shard_map/ppermute | solution.py:338
  79.4 55.4 %all-to-all-start.1 = ((s16[16,8,6272]{2,1,0:T(8,128)(2,1)}), s16[16,8,6272]{2,1,0:T(8,128)(2,1)S(1)}, u32[]{:S(2)}, u32[]{:S(2)}) async-start(s16[16,8,6272]{2,1,0:T(8,128)(2,1)} %bitcast.1), calls=%async_computation.1 | async-start | bytes 3211264 | tf_op jit(solution)/shard_map/all_to_all | solution.py:339
  92.4 42.4 %copy-start = (s32[256]{0:T(256)S(1)}, s32[256]{0:T(256)}, u32[]{:S(2)}) copy-start(s32[256]{0:T(256)} %cols.3) | copy-start | bytes 3076
  92.4 42.4 %copy-start.1 = (s32[256]{0:T(256)S(1)}, s32[256]{0:T(256)}, u32[]{:S(2)}) copy-start(s32[256]{0:T(256)} %rows.3) | copy-start | bytes 3076
  93.4 15.3 %collective-permute-start.2 = (s16[32,2176]{1,0:T(8,128)(2,1)S(1)}, s16[32,2176]{1,0:T(8,128)(2,1)S(1)}, u32[]{:S(2)}, u32[]{:S(2)}) collective-permute-start(s16[32,2176]{1,0:T(8,128)(2,1)S(1)} %get-tuple-element.23), channel_id=1, source_target_pairs={{0,64},{1,65},{2,66},{3,67},{4,68},{5,69},{6,70},{7,71},{8,72},{9,... | collective-permute-start | bytes 417800 | tf_op jit(solution)/shard_map/ppermute | solution.py:342
  97.9 13.8 %collective-permute-start.3 = (s16[32,2176]{1,0:T(8,128)(2,1)S(1)}, s16[32,2176]{1,0:T(8,128)(2,1)S(1)}, u32[]{:S(2)}, u32[]{:S(2)}) collective-permute-start(s16[32,2176]{1,0:T(8,128)(2,1)S(1)} %get-tuple-element.24), channel_id=1, source_target_pairs={{0,192},{1,193},{2,194},{3,195},{4,196},{5,197},{6,198},{7,199},{8... | collective-permute-start | bytes 417800 | tf_op jit(solution)/shard_map/ppermute | solution.py:342
  101.9 10.0 %collective-permute-start.4 = (s16[32,2176]{1,0:T(8,128)(2,1)S(1)}, s16[32,2176]{1,0:T(8,128)(2,1)S(1)}, u32[]{:S(2)}, u32[]{:S(2)}) collective-permute-start(s16[32,2176]{1,0:T(8,128)(2,1)S(1)} %get-tuple-element.25), channel_id=1, source_target_pairs={{0,128},{1,129},{2,130},{3,131},{4,132},{5,133},{6,134},{7,135},{8... | collective-permute-start | bytes 417800 | tf_op jit(solution)/shard_map/ppermute | solution.py:342
  112.6 25.8 %collective-permute-start.5 = (s16[8,2176]{1,0:T(8,128)(2,1)S(1)}, s16[8,2176]{1,0:T(8,128)(2,1)S(1)}, u32[]{:S(2)}, u32[]{:S(2)}) collective-permute-start(s16[8,2176]{1,0:T(8,128)(2,1)S(1)} %get-tuple-element.27), channel_id=1, source_target_pairs={{0,256},{1,257},{2,258},{3,259},{4,260},{5,261},{6,262},{7,263},{8... | collective-permute-start | bytes 104456 | tf_op jit(solution)/shard_map/ppermute | solution.py:346
  117.0 21.4 %collective-permute-start.6 = (s16[8,2176]{1,0:T(8,128)(2,1)S(1)}, s16[8,2176]{1,0:T(8,128)(2,1)S(1)}, u32[]{:S(2)}, u32[]{:S(2)}) collective-permute-start(s16[8,2176]{1,0:T(8,128)(2,1)S(1)} %get-tuple-element.28), channel_id=1, source_target_pairs={{0,512},{1,513},{2,514},{3,515},{4,516},{5,517},{6,518},{7,519},{8... | collective-permute-start | bytes 104456 | tf_op jit(solution)/shard_map/ppermute | solution.py:346
  121.8 16.6 %collective-permute-start.7 = (s16[8,2176]{1,0:T(8,128)(2,1)S(1)}, s16[8,2176]{1,0:T(8,128)(2,1)S(1)}, u32[]{:S(2)}, u32[]{:S(2)}) collective-permute-start(s16[8,2176]{1,0:T(8,128)(2,1)S(1)} %get-tuple-element.29), channel_id=1, source_target_pairs={{0,768},{1,769},{2,770},{3,771},{4,772},{5,773},{6,774},{7,775},{8... | collective-permute-start | bytes 104456 | tf_op jit(solution)/shard_map/ppermute | solution.py:346
  138.6 4.1 %collective-permute-start.8 = (f32[8,4,256]{2,1,0:T(4,128)S(1)}, f32[8,4,256]{2,1,0:T(4,128)S(1)}, u32[]{:S(2)}, u32[]{:S(2)}) collective-permute-start(f32[8,4,256]{2,1,0:T(4,128)S(1)} %get-tuple-element.32), channel_id=1, source_target_pairs={{0,16},{1,17},{2,18},{3,19},{4,20},{5,21},{6,22},{7,23},{8,24},{9,... | collective-permute-start | bytes 98312 | tf_op jit(solution)/shard_map/ppermute | solution.py:350

commit v5 on v4

--- a/solution.py
+++ b/solution.py
@@ -128,7 +128,7 @@
     ref[:, ref.shape[1] - SCALES :] = out.astype(jnp.int32).astype(jnp.int16)
 
 
-def grad_kernel(in_ref, other_ref, after_ref, send_ref, keep_ref, wg_ref):
+def grad_kernel(in_ref, other_ref, after_ref, first_ref, second_ref, keep_ref, wg_ref):
     core, y, _ = position()
     parity = y % 2
     scales = []
@@ -140,20 +140,15 @@
         wg_ref[...] = wg.reshape(16, 2, S, B)
         keep_ref[:, at(j)] = wg_ref[:, pl.ds(parity, 1)].reshape(128, B)
         q, e = fixed(wg_ref[:, pl.ds(1 - parity, 1)].reshape(128, B))
-        send_ref[:, at(j)] = q
+        (first_ref, second_ref)[j // 4][:, at(j % 4)] = q
         scales.append(e)
-    put_scales(send_ref, scales)
-
-
-def apply_kernel(in_ref, w_hbm, out_ref, w_ref, sems):
-    loads = [
-        pltpu.make_async_copy(w_hbm.at[2 * s : 2 * s + 2], w_ref.at[2 * s : 2 * s + 2], sems.at[s]) for s in range(8)
-    ]
-    for load in loads:
-        load.start()
+    put_scales(first_ref, scales[:4])
+    put_scales(second_ref, scales[4:])
+
+
+def apply_kernel(in_ref, w_ref, out_ref):
     scales = []
     for s in range(8):
-        loads[s].wait()
         first = s // 4 * 12 + s % 4 * 2
         x0, x1, g = in_ref[:, at(first)], in_ref[:, at(first + 1)], in_ref[:, at(s // 4 * 12 + 8 + s % 4)]
         w0, w1 = w_ref[2 * s], w_ref[2 * s + 1]
@@ -183,34 +178,52 @@
 def grad(received, other, after):
     return pl.pallas_call(
         grad_kernel,
-        out_shape=[pltpu.VMEM((128, PART), jnp.int16), pltpu.VMEM((128, 8 * B), jnp.float32)],
+        out_shape=[pltpu.VMEM((128, 4 * B + SCALES), jnp.int16)] * 2 + [pltpu.VMEM((128, 8 * B), jnp.float32)],
         in_specs=vmem(2) + [ANY],
-        out_specs=vmem(2),
+        out_specs=vmem(3),
         scratch_shapes=[pltpu.VMEM((16, 2, S, B), jnp.float32)],
         compiler_params=ROOM,
         name="grad",
     )(*here(received, other), after)
 
 
+def half_kernel(in_ref, out_ref):
+    theirs = 1 - position()[0]
+    for j in range(12):
+        out_ref[:, at(j)] = in_ref[:, pl.ds(pl.multiple_of(theirs * HALF + j * B, B), B)]
+
+
+def half(received):
+    return pl.pallas_call(
+        half_kernel,
+        out_shape=pltpu.VMEM((OWNERS * S, HALF), jnp.bfloat16),
+        in_specs=vmem(1),
+        out_specs=vmem(1)[0],
+        compiler_params=ROOM,
+        name="half",
+    )(*here(received))
+
+
 def apply(received, blocks):
     return pl.pallas_call(
         apply_kernel,
         out_shape=jax.ShapeDtypeStruct((OWNERS * S, MESSAGE + SCALES), jnp.int16),
-        in_specs=vmem(1) + [ANY],
-        scratch_shapes=[pltpu.VMEM((16, B, B), jnp.bfloat16), pltpu.SemaphoreType.DMA((8,))],
+        in_specs=vmem(2),
         compiler_params=ROOM,
         cost_estimate=pl.CostEstimate(flops=5_000_000_000, bytes_accessed=20_000_000, transcendentals=0),
         name="apply",
-    )(*here(received), pltpu.with_memory_space_constraint(blocks, pltpu.HBM))
-
-
-def pairs_kernel(keep_ref, got_ref, *refs):
+    )(*here(received, blocks))
+
+
+def pairs_kernel(keep_ref, first_ref, second_ref, *refs):
     outs, own_ref, total_ref = refs[:3], refs[3], refs[4]
     pair = position()[1] // 2
-    scale = decoded(got_ref[:, 8 * B :])
+    got = (first_ref, second_ref)
+    before = [decoded(ref[:, 4 * B :]) for ref in got]
     scales = [[] for _ in range(3)]
     for j in range(8):
-        total = keep_ref[:, at(j)] + widened(got_ref[:, at(j)]) * scale[:, j : j + 1]
+        i = j % 4
+        total = keep_ref[:, at(j)] + widened(got[j // 4][:, at(i)]) * before[j // 4][:, i : i + 1]
         total_ref[...] = total.reshape(XL, 4, S, B)
         own_ref[:, at(j)] = total_ref[:, pl.ds(pair, 1)].reshape(32, B)
         for d in range(3):
@@ -221,18 +234,18 @@
         put_scales(outs[d], scales[d])
 
 
-def pairs(keep, got):
+def pairs(keep, first, second):
     return pl.pallas_call(
         pairs_kernel,
         out_shape=[pltpu.VMEM((32, PART), jnp.int16)] * 3
         + [pltpu.VMEM((32, 8 * B), jnp.float32)],
-        in_specs=vmem(2),
+        in_specs=vmem(3),
         out_specs=vmem(4),
         scratch_shapes=[pltpu.VMEM((XL, 4, S, B), jnp.float32)],
         compiler_params=ROOM,
         cost_estimate=LONG,
         name="pairs",
-    )(*here(keep, got))
+    )(*here(keep, first, second))
 
 
 def cut_kernel(own_ref, a_ref, b_ref, c_ref, *refs):
@@ -267,7 +280,7 @@
     )(*here(own, *parts))
 
 
-def last_kernel(own_ref, a_ref, b_ref, c_ref, after_ref, mine_ref, send_ref):
+def last_kernel(own_ref, a_ref, b_ref, c_ref, mine_ref, send_ref):
     ins = (a_ref, b_ref, c_ref)
     scales = [decoded(ref[:, 8 * B :]) for ref in ins]
     first = position()[0] == 0
@@ -281,19 +294,18 @@
         send_ref[j] = jnp.where(first, bottom, top)
 
 
-def last(own, parts, after):
+def last(own, parts):
     return pl.pallas_call(
         last_kernel,
         out_shape=[pltpu.VMEM((8, 4, B), jnp.float32)] * 2,
-        in_specs=vmem(5),
+        in_specs=vmem(4),
         out_specs=vmem(2),
         compiler_params=ROOM,
         name="last",
-    )(*here(own, *parts, after))
-
-
-def place_kernel(cols, rows, in_ref, out_ref, grad_ref, mark_ref, first_ref, second_ref):
-    mark_ref[...] = jnp.zeros_like(mark_ref)
+    )(*here(own, *parts))
+
+
+def place_kernel(cols, rows, in_ref, out_ref, grad_ref, first_ref, second_ref):
     totals = (first_ref, second_ref)
     for ref in totals:
         ref[...] = jnp.zeros_like(ref)
@@ -315,7 +327,7 @@
 def place(block_cols, block_rows, back):
     return pl.pallas_call(
         place_kernel,
-        out_shape=[jax.ShapeDtypeStruct((S, 128 * B), jnp.bfloat16)] * 2 + [pltpu.VMEM((S, 128), jnp.float32)],
+        out_shape=[jax.ShapeDtypeStruct((S, 128 * B), jnp.bfloat16)] * 2,
         in_specs=[SMEM, SMEM] + vmem(1),
         scratch_shapes=[pltpu.VMEM((S, 128 * B), jnp.float32)] * 2,
         compiler_params=ROOM,
@@ -331,13 +343,13 @@
     )
 
     received = exchange(gather(block_cols, block_rows, shots_in, cotangent)).reshape(OWNERS * S, MESSAGE)
-    theirs = lax.dynamic_slice_in_dim(received, (1 - core) * HALF, HALF, axis=1)
-    other = permute(theirs, perm=moves(lambda a, b, c: (a, b, 1 - c)))
+    other = permute(half(received), perm=moves(lambda a, b, c: (a, b, 1 - c)))
     result = apply(received, blocks)
-    send, keep = grad(received, other, result)
-    got = permute(send, perm=moves(lambda a, b, c: (a, b ^ 1, c)))
+    first, second, keep = grad(received, other, result)
+    first = permute(first, perm=moves(lambda a, b, c: (a, b ^ 1, c)))
+    second = permute(second, perm=moves(lambda a, b, c: (a, ((b + 1) ^ 1) - 1 & 7, c)))
     back = exchange(result.reshape(OWNERS, S, MESSAGE + SCALES))
-    *parts, own = pairs(keep, got)
+    *parts, own = pairs(keep, first, second)
     parts = [
         permute(part, perm=moves(lambda a, b, c, d=d: (a, (b + 2 * d) % Y, c))) for d, part in zip(PAIR_STEPS, parts)
     ]
@@ -345,10 +357,10 @@
     parts = [
         permute(part, perm=moves(lambda a, b, c, d=d: (a ^ (d + 1), b, c))) for d, part in enumerate(parts)
     ]
-    shots_out, input_grad, placed = place(block_cols, block_rows, back)
-    mine, send = last(own, parts, placed)
+    mine, send = last(own, parts)
     swapped = permute(send, perm=moves(lambda a, b, c: (a, b, 1 - c)))
     weight_grad = jnp.where(core == 0, jnp.concatenate([mine, swapped]), jnp.concatenate([swapped, mine]))
+    shots_out, input_grad = place(block_cols, block_rows, back)
     return shots_out, input_grad, weight_grad
 
 

time: 145 us -> 142 us (0.979)
  blocking collectives: 0 us -> 56 us
  waiting for transfers between devices: 54.2 us -> 15.1 us
  starting transfers between devices: 71.2 us -> 54.8 us
  Pallas kernels: 16.4 us -> 14 us
    all_to_all x0 -> x1, blocking collectives: none -> 56 us  [shards(): exchange(gather(block_cols, block_rows, shots_in, cotangent))]
    all_to_all x1 -> x0, waiting for transfers between devices: 40.2 us -> none  [shards(): exchange(gather(block_cols, block_rows, shots_in, cotangent))]
    all_to_all x1 -> x0, starting transfers between devices: 20.5 us -> none  [shards(): exchange(gather(block_cols, block_rows, shots_in, cotangent))]
    all_to_all x1, waiting for transfers between devices: 9.9 us -> 0.01 us  [shards(): back = exchange(result.reshape(OWNERS, S, MESSAGE + SCALES))]
    ppermute x3, waiting for transfers between devices: 3.17 us -> 10.4 us  [shards(): permute(part, perm=moves(lambda a, b, c, d=d: (a, (b + 2 * d) % Y, c)))]
    ppermute x2 -> x3, starting transfers between devices: 6.97 us -> 13.6 us  [the longest x1 5.44 us: shards(): permute(second, perm=moves(lambda a, b, c: (a, (b + 1 ^ 1) - 1 & 7, c)))]
    ppermute x1, starting transfers between devices: 3.29 us -> 8.27 us  [shards(): swapped = permute(send, perm=moves(lambda a, b, c: (a, b, 1 - c)))]
    ppermute x3, starting transfers between devices: 15.3 us -> 10.9 us  [shards(): permute(part, perm=moves(lambda a, b, c, d=d: (a, (b + 2 * d) % Y, c)))]
  transfers between devices with their start and end apart: 11 -> 11, of which waited for: 6 -> 5; matrix products, arithmetic and copies ran while one was open for 0% -> 0% of each run, Pallas kernels for 7% -> 4%
where the time goes in v5:
time: 142 us; the launch traced here: 141 us
  blocking collectives  56 us (39%)
  starting transfers between devices  54.8 us (39%)
  waiting for transfers between devices  15.1 us (11%)
  Pallas kernels  14 us (10%)
    all_to_all x1, blocking collectives, shards(): exchange(gather(block_cols, block_rows, shots_in, cotangent))  56 us
    all_to_all x1, starting transfers between devices, shards(): back = exchange(result.reshape(OWNERS, S, MESSAGE + SCALES))  11.2 us
    ppermute x3, starting transfers between devices, shards(): permute(part, perm=moves(lambda a, b, c, d=d: (a, (b + 2 * d) % Y, c)))  10.9 us
    ppermute x3, starting transfers between devices, shards(): permute(part, perm=moves(lambda a, b, c, d=d: (a ^ d + 1, b, c)))  10.8 us
    ppermute x3, waiting for transfers between devices, shards(): permute(part, perm=moves(lambda a, b, c, d=d: (a, (b + 2 * d) % Y, c)))  10.4 us
    ppermute x1, starting transfers between devices, shards(): swapped = permute(send, perm=moves(lambda a, b, c: (a, b, 1 - c)))  8.27 us
    ppermute x1, starting transfers between devices, shards(): permute(second, perm=moves(lambda a, b, c: (a, (b + 1 ^ 1) - 1 & 7, c)))  5.44 us
    ppermute x1, starting transfers between devices, shards(): other = permute(half(received), perm=moves(lambda a, b, c: (a, b, 1 - c)))  4.87 us
  transfers between devices with their start and end apart: 11, of which 5 were waited for; matrix products, arithmetic and copies ran while one was open for 0% of the time, Pallas kernels for 4%

profile of v5, /device:TPU:1, one launch (start us, length us, event | category | flops | bytes accessed | tf_op | source)
XLA Modules:
  0.0 141.3 jit_solution(8942154794273118953)
XLA Ops:
  0.6 3.3 %gather.1 = bf16[16,8,6144]{2,1,0:T(8,128)(2,1)} custom-call(s32[256]{0:T(256)} %cols.3, s32[256]{0:T(256)} %rows.3, bf16[8,32768]{1,0:T(8,128)(2,1)} %x_hbm.1, bf16[8,32768]{1,0:T(8,128)(2,1)} %g_hbm.1), custom_call_target="tpu_custom_call" | custom-call | tf_op jit(solution)/shard_map/gather/pallas_call | solution.py:86
  3.9 56.0 %all_to_all.10 = bf16[16,8,6144]{2,1,0:T(8,128)(2,1)S(1)} all-to-all(bf16[16,8,6144]{2,1,0:T(8,128)(2,1)} %gather.1), channel_id=1, replica_groups={{0,1,2,3,4,5,6,7,520,521,522,523,524,525,526,527},{16,17,18,19,20,21,22..., dimensions={0} | all-to-all | bytes 3145728 | tf_op jit(solution)/shard_map/all_to_all | solution.py:345
  60.0 4.9 %collective-permute-start = (bf16[128,3072]{1,0:T(8,128)(2,1)S(1)}, bf16[128,3072]{1,0:T(8,128)(2,1)S(1)}, u32[]{:S(2)}, u32[]{:S(2)}) collective-permute-start(bf16[128,3072]{1,0:T(8,128)(2,1)S(1)} %half.1), channel_id=1, source_target_pairs={{0,16},{1,17},{2,18},{3,19},{4,20},{5,21},{6,22},{7,23},{8,24},{9,... | collective-permute-start | bytes 2359304 | tf_op jit(solution)/shard_map/ppermute | solution.py:346
  64.9 2.6 %apply.1.after_ref = s16[128,6272]{1,0:T(8,128)(2,1)} custom-call(bf16[128,6144]{1,0:T(8,128)(2,1)S(1)} %bitcast.3, bf16[16,256,256]{2,1,0:T(8,128)(2,1)S(1)} %copy-done.2), custom_call_target="tpu_custom_call" | custom-call | flops 5000000000 | bytes 20000000 | tf_op jit(solution)/shard_map/apply/pallas_call | solution.py:208
  67.4 1.8 %grad.1 = (s16[128,1152]{1,0:T(8,128)(2,1)}, s16[128,1152]{1,0:T(8,128)(2,1)S(1)}, f32[128,2048]{1,0:T(8,128)S(1)}) custom-call(bf16[128,6144]{1,0:T(8,128)(2,1)S(1)} %bitcast.4, bf16[128,3072]{1,0:T(8,128)(2,1)S(1)} %collective-permute-done.other_ref, s16[128,6272]{1,0:T(8,128)(2,1)} %apply.1.after_ref), custom_call_target="tpu_custom_call" | custom-call | tf_op jit(solution)/shard_map/grad/pallas_call | solution.py:179
  69.2 3.3 %collective-permute-start.1 = (s16[128,1152]{1,0:T(8,128)(2,1)}, s16[128,1152]{1,0:T(8,128)(2,1)S(1)}, u32[]{:S(2)}, u32[]{:S(2)}) collective-permute-start(s16[128,1152]{1,0:T(8,128)(2,1)} %get-tuple-element.21), channel_id=1, source_target_pairs={{0,32},{1,33},{2,34},{3,35},{4,36},{5,37},{6,38},{7,39},{8,40},{9,... | collective-permute-start | bytes 884744 | tf_op jit(solution)/shard_map/ppermute | solution.py:349
  72.5 5.4 %collective-permute-start.2 = (s16[128,1152]{1,0:T(8,128)(2,1)S(1)}, s16[128,1152]{1,0:T(8,128)(2,1)}, u32[]{:S(2)}, u32[]{:S(2)}) collective-permute-start(s16[128,1152]{1,0:T(8,128)(2,1)S(1)} %get-tuple-element.22), channel_id=1, source_target_pairs={{0,224},{1,225},{2,226},{3,227},{4,228},{5,229},{6,230},{7,231},{8... | collective-permute-start | bytes 884744 | tf_op jit(solution)/shard_map/ppermute | solution.py:350
  78.0 11.2 %all-to-all-start.1 = ((s16[16,8,6272]{2,1,0:T(8,128)(2,1)}), s16[16,8,6272]{2,1,0:T(8,128)(2,1)S(1)}, u32[]{:S(2)}, u32[]{:S(2)}) async-start(s16[16,8,6272]{2,1,0:T(8,128)(2,1)} %bitcast.1), calls=%async_computation.1 | async-start | bytes 3211264 | tf_op jit(solution)/shard_map/all_to_all | solution.py:351
  89.2 1.9 %pairs.1 = (s16[32,2176]{1,0:T(8,128)(2,1)S(1)}, s16[32,2176]{1,0:T(8,128)(2,1)S(1)}, s16[32,2176]{1,0:T(8,128)(2,1)S(1)}, f32[32,2048]{1,0:T(8,128)S(1)}) custom-call(f32[128,2048]{1,0:T(8,128)S(1)} %get-tuple-element.20.keep_ref, s16[128,1152]{1,0:T(8,128)(2,1)S(1)} %collective-permute-done.1.first_ref, s16[128,1152]{1,0:T(8,128)(2,1)} %collective-permute-done.2.second_ref), custom_call_target="tpu_custom_call" | custom-call | flops 80000000000 | bytes 1000000 | tf_op jit(solution)/shard_map/pairs/pallas_call | solution.py:238
  91.1 1.9 %collective-permute-start.3 = (s16[32,2176]{1,0:T(8,128)(2,1)S(1)}, s16[32,2176]{1,0:T(8,128)(2,1)S(1)}, u32[]{:S(2)}, u32[]{:S(2)}) collective-permute-start(s16[32,2176]{1,0:T(8,128)(2,1)S(1)} %get-tuple-element.24), channel_id=1, source_target_pairs={{0,64},{1,65},{2,66},{3,67},{4,68},{5,69},{6,70},{7,71},{8,72},{9,... | collective-permute-start | bytes 417800 | tf_op jit(solution)/shard_map/ppermute | solution.py:354
  93.1 5.5 %collective-permute-start.4 = (s16[32,2176]{1,0:T(8,128)(2,1)S(1)}, s16[32,2176]{1,0:T(8,128)(2,1)S(1)}, u32[]{:S(2)}, u32[]{:S(2)}) collective-permute-start(s16[32,2176]{1,0:T(8,128)(2,1)S(1)} %get-tuple-element.25), channel_id=1, source_target_pairs={{0,192},{1,193},{2,194},{3,195},{4,196},{5,197},{6,198},{7,199},{8... | collective-permute-start | bytes 417800 | tf_op jit(solution)/shard_map/ppermute | solution.py:354
  98.5 3.5 %collective-permute-start.5 = (s16[32,2176]{1,0:T(8,128)(2,1)S(1)}, s16[32,2176]{1,0:T(8,128)(2,1)S(1)}, u32[]{:S(2)}, u32[]{:S(2)}) collective-permute-start(s16[32,2176]{1,0:T(8,128)(2,1)S(1)} %get-tuple-element.26), channel_id=1, source_target_pairs={{0,128},{1,129},{2,130},{3,131},{4,132},{5,133},{6,134},{7,135},{8... | collective-permute-start | bytes 417800 | tf_op jit(solution)/shard_map/ppermute | solution.py:354
  102.1 7.9 %collective-permute-done.4.b_ref = s16[32,2176]{1,0:T(8,128)(2,1)S(1)} collective-permute-done((s16[32,2176]{1,0:T(8,128)(2,1)S(1)}, s16[32,2176]{1,0:T(8,128)(2,1)S(1)}, u32[]{:S(2)}, u32[]{:S(2)}) %collective-permute-start.4) | collective-permute-done | bytes 139296 | tf_op jit(solution)/shard_map/ppermute | solution.py:354
  110.0 2.5 %collective-permute-done.5.c_ref = s16[32,2176]{1,0:T(8,128)(2,1)S(1)} collective-permute-done((s16[32,2176]{1,0:T(8,128)(2,1)S(1)}, s16[32,2176]{1,0:T(8,128)(2,1)S(1)}, u32[]{:S(2)}, u32[]{:S(2)}) %collective-permute-start.5) | collective-permute-done | bytes 139296 | tf_op jit(solution)/shard_map/ppermute | solution.py:354
  112.5 0.7 cut.1
  113.2 3.0 %collective-permute-start.6 = (s16[8,2176]{1,0:T(8,128)(2,1)S(1)}, s16[8,2176]{1,0:T(8,128)(2,1)S(1)}, u32[]{:S(2)}, u32[]{:S(2)}) collective-permute-start(s16[8,2176]{1,0:T(8,128)(2,1)S(1)} %get-tuple-element.28), channel_id=1, source_target_pairs={{0,256},{1,257},{2,258},{3,259},{4,260},{5,261},{6,262},{7,263},{8... | collective-permute-start | bytes 104456 | tf_op jit(solution)/shard_map/ppermute | solution.py:358
  116.2 4.7 %collective-permute-start.7 = (s16[8,2176]{1,0:T(8,128)(2,1)S(1)}, s16[8,2176]{1,0:T(8,128)(2,1)S(1)}, u32[]{:S(2)}, u32[]{:S(2)}) collective-permute-start(s16[8,2176]{1,0:T(8,128)(2,1)S(1)} %get-tuple-element.29), channel_id=1, source_target_pairs={{0,512},{1,513},{2,514},{3,515},{4,516},{5,517},{6,518},{7,519},{8... | collective-permute-start | bytes 104456 | tf_op jit(solution)/shard_map/ppermute | solution.py:358
  120.9 3.1 %collective-permute-start.8 = (s16[8,2176]{1,0:T(8,128)(2,1)S(1)}, s16[8,2176]{1,0:T(8,128)(2,1)S(1)}, u32[]{:S(2)}, u32[]{:S(2)}) collective-permute-start(s16[8,2176]{1,0:T(8,128)(2,1)S(1)} %get-tuple-element.30), channel_id=1, source_target_pairs={{0,768},{1,769},{2,770},{3,771},{4,772},{5,773},{6,774},{7,775},{8... | collective-permute-start | bytes 104456 | tf_op jit(solution)/shard_map/ppermute | solution.py:358
  124.0 0.2 collective-permute-done.7.b_ref
  124.2 3.6 %collective-permute-done.8.c_ref = s16[8,2176]{1,0:T(8,128)(2,1)S(1)} collective-permute-done((s16[8,2176]{1,0:T(8,128)(2,1)S(1)}, s16[8,2176]{1,0:T(8,128)(2,1)S(1)}, u32[]{:S(2)}, u32[]{:S(2)}) %collective-permute-start.8) | collective-permute-done | bytes 34848 | tf_op jit(solution)/shard_map/ppermute | solution.py:358
  128.0 8.3 %collective-permute-start.9 = (f32[8,4,256]{2,1,0:T(4,128)S(1)}, f32[8,4,256]{2,1,0:T(4,128)S(1)}, u32[]{:S(2)}, u32[]{:S(2)}) collective-permute-start(f32[8,4,256]{2,1,0:T(4,128)S(1)} %get-tuple-element.32), channel_id=1, source_target_pairs={{0,16},{1,17},{2,18},{3,19},{4,20},{5,21},{6,22},{7,23},{8,24},{9,... | collective-permute-start | bytes 98312 | tf_op jit(solution)/shard_map/ppermute | solution.py:361
  136.3 0.8 collective-permute-done.9
  137.1 0.6 maximum_select_fusion
  137.7 3.6 %place.1 = (bf16[8,32768]{1,0:T(8,128)(2,1)}, bf16[8,32768]{1,0:T(8,128)(2,1)}) custom-call(s32[256]{0:T(256)S(1)} %copy-done, s32[256]{0:T(256)S(1)} %copy-done.1, s16[16,8,6272]{2,1,0:T(8,128)(2,1)S(1)} %all-to-all-done.1.in_ref), custom_call_target="tpu_custom_call" | custom-call | tf_op jit(solution)/shard_map/place/pallas_call | solution.py:328
  (14 shorter events, 0.3 us)
Async XLA Ops:
  59.9 5.0 %copy-start.2 = (bf16[16,256,256]{2,1,0:T(8,128)(2,1)S(1)}, bf16[16,256,256]{2,1,0:T(8,128)(2,1)}, u32[]{:S(2)}) copy-start(bf16[16,256,256]{2,1,0:T(8,128)(2,1)} %w_ref.1) | copy-start | bytes 6291460
  60.0 7.5 %collective-permute-start = (bf16[128,3072]{1,0:T(8,128)(2,1)S(1)}, bf16[128,3072]{1,0:T(8,128)(2,1)S(1)}, u32[]{:S(2)}, u32[]{:S(2)}) collective-permute-start(bf16[128,3072]{1,0:T(8,128)(2,1)S(1)} %half.1), channel_id=1, source_target_pairs={{0,16},{1,17},{2,18},{3,19},{4,20},{5,21},{6,22},{7,23},{8,24},{9,... | collective-permute-start | bytes 2359304 | tf_op jit(solution)/shard_map/ppermute | solution.py:346
  69.2 19.9 %collective-permute-start.1 = (s16[128,1152]{1,0:T(8,128)(2,1)}, s16[128,1152]{1,0:T(8,128)(2,1)S(1)}, u32[]{:S(2)}, u32[]{:S(2)}) collective-permute-start(s16[128,1152]{1,0:T(8,128)(2,1)} %get-tuple-element.21), channel_id=1, source_target_pairs={{0,32},{1,33},{2,34},{3,35},{4,36},{5,37},{6,38},{7,39},{8,40},{9,... | collective-permute-start | bytes 884744 | tf_op jit(solution)/shard_map/ppermute | solution.py:349
  72.5 16.6 %collective-permute-start.2 = (s16[128,1152]{1,0:T(8,128)(2,1)S(1)}, s16[128,1152]{1,0:T(8,128)(2,1)}, u32[]{:S(2)}, u32[]{:S(2)}) collective-permute-start(s16[128,1152]{1,0:T(8,128)(2,1)S(1)} %get-tuple-element.22), channel_id=1, source_target_pairs={{0,224},{1,225},{2,226},{3,227},{4,228},{5,229},{6,230},{7,231},{8... | collective-permute-start | bytes 884744 | tf_op jit(solution)/shard_map/ppermute | solution.py:350
  78.0 59.8 %all-to-all-start.1 = ((s16[16,8,6272]{2,1,0:T(8,128)(2,1)}), s16[16,8,6272]{2,1,0:T(8,128)(2,1)S(1)}, u32[]{:S(2)}, u32[]{:S(2)}) async-start(s16[16,8,6272]{2,1,0:T(8,128)(2,1)} %bitcast.1), calls=%async_computation.1 | async-start | bytes 3211264 | tf_op jit(solution)/shard_map/all_to_all | solution.py:351
  89.2 48.6 %copy-start = (s32[256]{0:T(256)S(1)}, s32[256]{0:T(256)}, u32[]{:S(2)}) copy-start(s32[256]{0:T(256)} %cols.3) | copy-start | bytes 3076
  89.2 48.6 %copy-start.1 = (s32[256]{0:T(256)S(1)}, s32[256]{0:T(256)}, u32[]{:S(2)}) copy-start(s32[256]{0:T(256)} %rows.3) | copy-start | bytes 3076
  91.1 10.9 %collective-permute-start.3 = (s16[32,2176]{1,0:T(8,128)(2,1)S(1)}, s16[32,2176]{1,0:T(8,128)(2,1)S(1)}, u32[]{:S(2)}, u32[]{:S(2)}) collective-permute-start(s16[32,2176]{1,0:T(8,128)(2,1)S(1)} %get-tuple-element.24), channel_id=1, source_target_pairs={{0,64},{1,65},{2,66},{3,67},{4,68},{5,69},{6,70},{7,71},{8,72},{9,... | collective-permute-start | bytes 417800 | tf_op jit(solution)/shard_map/ppermute | solution.py:354
  93.1 16.9 %collective-permute-start.4 = (s16[32,2176]{1,0:T(8,128)(2,1)S(1)}, s16[32,2176]{1,0:T(8,128)(2,1)S(1)}, u32[]{:S(2)}, u32[]{:S(2)}) collective-permute-start(s16[32,2176]{1,0:T(8,128)(2,1)S(1)} %get-tuple-element.25), channel_id=1, source_target_pairs={{0,192},{1,193},{2,194},{3,195},{4,196},{5,197},{6,198},{7,199},{8... | collective-permute-start | bytes 417800 | tf_op jit(solution)/shard_map/ppermute | solution.py:354
  98.5 14.0 %collective-permute-start.5 = (s16[32,2176]{1,0:T(8,128)(2,1)S(1)}, s16[32,2176]{1,0:T(8,128)(2,1)S(1)}, u32[]{:S(2)}, u32[]{:S(2)}) collective-permute-start(s16[32,2176]{1,0:T(8,128)(2,1)S(1)} %get-tuple-element.26), channel_id=1, source_target_pairs={{0,128},{1,129},{2,130},{3,131},{4,132},{5,133},{6,134},{7,135},{8... | collective-permute-start | bytes 417800 | tf_op jit(solution)/shard_map/ppermute | solution.py:354
  113.2 10.9 %collective-permute-start.6 = (s16[8,2176]{1,0:T(8,128)(2,1)S(1)}, s16[8,2176]{1,0:T(8,128)(2,1)S(1)}, u32[]{:S(2)}, u32[]{:S(2)}) collective-permute-start(s16[8,2176]{1,0:T(8,128)(2,1)S(1)} %get-tuple-element.28), channel_id=1, source_target_pairs={{0,256},{1,257},{2,258},{3,259},{4,260},{5,261},{6,262},{7,263},{8... | collective-permute-start | bytes 104456 | tf_op jit(solution)/shard_map/ppermute | solution.py:358
  116.2 8.0 %collective-permute-start.7 = (s16[8,2176]{1,0:T(8,128)(2,1)S(1)}, s16[8,2176]{1,0:T(8,128)(2,1)S(1)}, u32[]{:S(2)}, u32[]{:S(2)}) collective-permute-start(s16[8,2176]{1,0:T(8,128)(2,1)S(1)} %get-tuple-element.29), channel_id=1, source_target_pairs={{0,512},{1,513},{2,514},{3,515},{4,516},{5,517},{6,518},{7,519},{8... | collective-permute-start | bytes 104456 | tf_op jit(solution)/shard_map/ppermute | solution.py:358
  120.9 6.9 %collective-permute-start.8 = (s16[8,2176]{1,0:T(8,128)(2,1)S(1)}, s16[8,2176]{1,0:T(8,128)(2,1)S(1)}, u32[]{:S(2)}, u32[]{:S(2)}) collective-permute-start(s16[8,2176]{1,0:T(8,128)(2,1)S(1)} %get-tuple-element.30), channel_id=1, source_target_pairs={{0,768},{1,769},{2,770},{3,771},{4,772},{5,773},{6,774},{7,775},{8... | collective-permute-start | bytes 104456 | tf_op jit(solution)/shard_map/ppermute | solution.py:358
  128.0 9.1 %collective-permute-start.9 = (f32[8,4,256]{2,1,0:T(4,128)S(1)}, f32[8,4,256]{2,1,0:T(4,128)S(1)}, u32[]{:S(2)}, u32[]{:S(2)}) collective-permute-start(f32[8,4,256]{2,1,0:T(4,128)S(1)} %get-tuple-element.32), channel_id=1, source_target_pairs={{0,16},{1,17},{2,18},{3,19},{4,20},{5,21},{6,22},{7,23},{8,24},{9,... | collective-permute-start | bytes 98312 | tf_op jit(solution)/shard_map/ppermute | solution.py:361

commit v6 on v5

--- a/solution.py
+++ b/solution.py
@@ -305,12 +305,13 @@
     )(*here(own, *parts))
 
 
-def place_kernel(cols, rows, in_ref, out_ref, grad_ref, first_ref, second_ref):
+def place_kernel(cols, rows, in_ref, out_ref, grad_ref, mark_ref, first_ref, second_ref):
+    mark_ref[...] = jnp.zeros_like(mark_ref)
     totals = (first_ref, second_ref)
     for ref in totals:
         ref[...] = jnp.zeros_like(ref)
 
-    @pl.loop(0, OWNERS)
+    @pl.loop(0, OWNERS, unroll=8)
     def _(p):
         scale = decoded(in_ref[p, :, MESSAGE:])
         values = [widened(in_ref[p, :, at(j)]) * scale[:, j : j + 1] for j in range(24)]
@@ -327,7 +328,7 @@
 def place(block_cols, block_rows, back):
     return pl.pallas_call(
         place_kernel,
-        out_shape=[jax.ShapeDtypeStruct((S, 128 * B), jnp.bfloat16)] * 2,
+        out_shape=[jax.ShapeDtypeStruct((S, 128 * B), jnp.bfloat16)] * 2 + [pltpu.VMEM((S, 128), jnp.float32)],
         in_specs=[SMEM, SMEM] + vmem(1),
         scratch_shapes=[pltpu.VMEM((S, 128 * B), jnp.float32)] * 2,
         compiler_params=ROOM,
@@ -335,8 +336,24 @@
     )(block_cols, block_rows, *here(back))
 
 
+def join_kernel(mine_ref, swapped_ref, after_ref, out_ref):
+    first = position()[0] == 0
+    mine, swapped = mine_ref[...], swapped_ref[...]
+    out_ref[:8] = jnp.where(first, mine, swapped)
+    out_ref[8:] = jnp.where(first, swapped, mine)
+
+
+def join(mine, swapped, after):
+    return pl.pallas_call(
+        join_kernel,
+        out_shape=jax.ShapeDtypeStruct((16, 4, B), jnp.float32),
+        in_specs=vmem(3),
+        compiler_params=ROOM,
+        name="join",
+    )(*here(mine, swapped, after))
+
+
 def shards(shots_in, cotangent, blocks, block_rows, block_cols):
-    core = position()[0]
     permute = functools.partial(lax.ppermute, axis_name=AXES)
     exchange = functools.partial(
         lax.all_to_all, axis_name=AXES, split_axis=0, concat_axis=0, axis_index_groups=groups(), tiled=True
@@ -359,8 +376,8 @@
     ]
     mine, send = last(own, parts)
     swapped = permute(send, perm=moves(lambda a, b, c: (a, b, 1 - c)))
-    weight_grad = jnp.where(core == 0, jnp.concatenate([mine, swapped]), jnp.concatenate([swapped, mine]))
-    shots_out, input_grad = place(block_cols, block_rows, back)
+    shots_out, input_grad, placed = place(block_cols, block_rows, back)
+    weight_grad = join(mine, swapped, placed)
     return shots_out, input_grad, weight_grad
 
 

time: 142 us -> 140 us (0.986)
  transfers between devices with their start and end apart: 11 -> 11, of which waited for: 5 -> 4; matrix products, arithmetic and copies ran while one was open for 0% -> 0% of each run, Pallas kernels for 4% -> 6%
where the time goes in v6:
time: 140 us; the launch traced here: 139 us
  blocking collectives  56 us (40%)
  starting transfers between devices  54.8 us (39%)
  waiting for transfers between devices  14.3 us (10%)
  Pallas kernels  13.5 us (10%)
    all_to_all x1, blocking collectives, shards(): exchange(gather(block_cols, block_rows, shots_in, cotangent))  56 us
    all_to_all x1, starting transfers between devices, shards(): back = exchange(result.reshape(OWNERS, S, MESSAGE + SCALES))  11.2 us
    ppermute x3, starting transfers between devices, shards(): permute(part, perm=moves(lambda a, b, c, d=d: (a, (b + 2 * d) % Y, c)))  10.9 us
    ppermute x3, starting transfers between devices, shards(): permute(part, perm=moves(lambda a, b, c, d=d: (a ^ d + 1, b, c)))  10.8 us
    ppermute x3, waiting for transfers between devices, shards(): permute(part, perm=moves(lambda a, b, c, d=d: (a, (b + 2 * d) % Y, c)))  10.5 us
    ppermute x1, starting transfers between devices, shards(): swapped = permute(send, perm=moves(lambda a, b, c: (a, b, 1 - c)))  8.29 us
    ppermute x1, starting transfers between devices, shards(): permute(second, perm=moves(lambda a, b, c: (a, (b + 1 ^ 1) - 1 & 7, c)))  5.45 us
    ppermute x1, starting transfers between devices, shards(): other = permute(half(received), perm=moves(lambda a, b, c: (a, b, 1 - c)))  4.87 us
  transfers between devices with their start and end apart: 11, of which 4 were waited for; matrix products, arithmetic and copies ran while one was open for 0% of the time, Pallas kernels for 6%

profile of v6, /device:TPU:1, one launch (start us, length us, event | category | flops | bytes accessed | tf_op | source)
XLA Modules:
  0.0 139.3 jit_solution(3340002303658794145)
XLA Ops:
  0.6 3.3 %gather.1 = bf16[16,8,6144]{2,1,0:T(8,128)(2,1)} custom-call(s32[256]{0:T(256)} %cols.3, s32[256]{0:T(256)} %rows.3, bf16[8,32768]{1,0:T(8,128)(2,1)} %x_hbm.1, bf16[8,32768]{1,0:T(8,128)(2,1)} %g_hbm.1), custom_call_target="tpu_custom_call" | custom-call | tf_op jit(solution)/shard_map/gather/pallas_call | solution.py:86
  3.9 56.0 %all_to_all.10 = bf16[16,8,6144]{2,1,0:T(8,128)(2,1)S(1)} all-to-all(bf16[16,8,6144]{2,1,0:T(8,128)(2,1)} %gather.1), channel_id=1, replica_groups={{0,1,2,3,4,5,6,7,520,521,522,523,524,525,526,527},{16,17,18,19,20,21,22..., dimensions={0} | all-to-all | bytes 3145728 | tf_op jit(solution)/shard_map/all_to_all | solution.py:362
  59.9 0.1 half.1
  60.0 4.9 %collective-permute-start = (bf16[128,3072]{1,0:T(8,128)(2,1)S(1)}, bf16[128,3072]{1,0:T(8,128)(2,1)S(1)}, u32[]{:S(2)}, u32[]{:S(2)}) collective-permute-start(bf16[128,3072]{1,0:T(8,128)(2,1)S(1)} %half.1), channel_id=1, source_target_pairs={{0,16},{1,17},{2,18},{3,19},{4,20},{5,21},{6,22},{7,23},{8,24},{9,... | collective-permute-start | bytes 2359304 | tf_op jit(solution)/shard_map/ppermute | solution.py:363
  64.9 2.5 %apply.1.after_ref = s16[128,6272]{1,0:T(8,128)(2,1)} custom-call(bf16[128,6144]{1,0:T(8,128)(2,1)S(1)} %bitcast.3, bf16[16,256,256]{2,1,0:T(8,128)(2,1)S(1)} %copy-done.2), custom_call_target="tpu_custom_call" | custom-call | flops 5000000000 | bytes 20000000 | tf_op jit(solution)/shard_map/apply/pallas_call | solution.py:208
  67.3 1.8 %grad.1 = (s16[128,1152]{1,0:T(8,128)(2,1)}, s16[128,1152]{1,0:T(8,128)(2,1)S(1)}, f32[128,2048]{1,0:T(8,128)S(1)}) custom-call(bf16[128,6144]{1,0:T(8,128)(2,1)S(1)} %bitcast.4, bf16[128,3072]{1,0:T(8,128)(2,1)S(1)} %collective-permute-done.other_ref, s16[128,6272]{1,0:T(8,128)(2,1)} %apply.1.after_ref), custom_call_target="tpu_custom_call" | custom-call | tf_op jit(solution)/shard_map/grad/pallas_call | solution.py:179
  69.1 3.3 %collective-permute-start.1 = (s16[128,1152]{1,0:T(8,128)(2,1)}, s16[128,1152]{1,0:T(8,128)(2,1)S(1)}, u32[]{:S(2)}, u32[]{:S(2)}) collective-permute-start(s16[128,1152]{1,0:T(8,128)(2,1)} %get-tuple-element.22), channel_id=1, source_target_pairs={{0,32},{1,33},{2,34},{3,35},{4,36},{5,37},{6,38},{7,39},{8,40},{9,... | collective-permute-start | bytes 884744 | tf_op jit(solution)/shard_map/ppermute | solution.py:366
  72.4 5.4 %collective-permute-start.2 = (s16[128,1152]{1,0:T(8,128)(2,1)S(1)}, s16[128,1152]{1,0:T(8,128)(2,1)}, u32[]{:S(2)}, u32[]{:S(2)}) collective-permute-start(s16[128,1152]{1,0:T(8,128)(2,1)S(1)} %get-tuple-element.23), channel_id=1, source_target_pairs={{0,224},{1,225},{2,226},{3,227},{4,228},{5,229},{6,230},{7,231},{8... | collective-permute-start | bytes 884744 | tf_op jit(solution)/shard_map/ppermute | solution.py:367
  77.9 11.2 %all-to-all-start.1 = ((s16[16,8,6272]{2,1,0:T(8,128)(2,1)}), s16[16,8,6272]{2,1,0:T(8,128)(2,1)S(1)}, u32[]{:S(2)}, u32[]{:S(2)}) async-start(s16[16,8,6272]{2,1,0:T(8,128)(2,1)} %bitcast.1), calls=%async_computation.1 | async-start | bytes 3211264 | tf_op jit(solution)/shard_map/all_to_all | solution.py:368
  89.1 1.9 %pairs.1 = (s16[32,2176]{1,0:T(8,128)(2,1)S(1)}, s16[32,2176]{1,0:T(8,128)(2,1)S(1)}, s16[32,2176]{1,0:T(8,128)(2,1)S(1)}, f32[32,2048]{1,0:T(8,128)S(1)}) custom-call(f32[128,2048]{1,0:T(8,128)S(1)} %get-tuple-element.21.keep_ref, s16[128,1152]{1,0:T(8,128)(2,1)S(1)} %collective-permute-done.1.first_ref, s16[128,1152]{1,0:T(8,128)(2,1)} %collective-permute-done.2.second_ref), custom_call_target="tpu_custom_call" | custom-call | flops 80000000000 | bytes 1000000 | tf_op jit(solution)/shard_map/pairs/pallas_call | solution.py:238
  91.1 1.9 %collective-permute-start.3 = (s16[32,2176]{1,0:T(8,128)(2,1)S(1)}, s16[32,2176]{1,0:T(8,128)(2,1)S(1)}, u32[]{:S(2)}, u32[]{:S(2)}) collective-permute-start(s16[32,2176]{1,0:T(8,128)(2,1)S(1)} %get-tuple-element.25), channel_id=1, source_target_pairs={{0,64},{1,65},{2,66},{3,67},{4,68},{5,69},{6,70},{7,71},{8,72},{9,... | collective-permute-start | bytes 417800 | tf_op jit(solution)/shard_map/ppermute | solution.py:371
  93.0 5.5 %collective-permute-start.4 = (s16[32,2176]{1,0:T(8,128)(2,1)S(1)}, s16[32,2176]{1,0:T(8,128)(2,1)S(1)}, u32[]{:S(2)}, u32[]{:S(2)}) collective-permute-start(s16[32,2176]{1,0:T(8,128)(2,1)S(1)} %get-tuple-element.26), channel_id=1, source_target_pairs={{0,192},{1,193},{2,194},{3,195},{4,196},{5,197},{6,198},{7,199},{8... | collective-permute-start | bytes 417800 | tf_op jit(solution)/shard_map/ppermute | solution.py:371
  98.5 3.5 %collective-permute-start.5 = (s16[32,2176]{1,0:T(8,128)(2,1)S(1)}, s16[32,2176]{1,0:T(8,128)(2,1)S(1)}, u32[]{:S(2)}, u32[]{:S(2)}) collective-permute-start(s16[32,2176]{1,0:T(8,128)(2,1)S(1)} %get-tuple-element.27), channel_id=1, source_target_pairs={{0,128},{1,129},{2,130},{3,131},{4,132},{5,133},{6,134},{7,135},{8... | collective-permute-start | bytes 417800 | tf_op jit(solution)/shard_map/ppermute | solution.py:371
  102.0 8.0 %collective-permute-done.4.b_ref = s16[32,2176]{1,0:T(8,128)(2,1)S(1)} collective-permute-done((s16[32,2176]{1,0:T(8,128)(2,1)S(1)}, s16[32,2176]{1,0:T(8,128)(2,1)S(1)}, u32[]{:S(2)}, u32[]{:S(2)}) %collective-permute-start.4) | collective-permute-done | bytes 139296 | tf_op jit(solution)/shard_map/ppermute | solution.py:371
  109.9 2.5 %collective-permute-done.5.c_ref = s16[32,2176]{1,0:T(8,128)(2,1)S(1)} collective-permute-done((s16[32,2176]{1,0:T(8,128)(2,1)S(1)}, s16[32,2176]{1,0:T(8,128)(2,1)S(1)}, u32[]{:S(2)}, u32[]{:S(2)}) %collective-permute-start.5) | collective-permute-done | bytes 139296 | tf_op jit(solution)/shard_map/ppermute | solution.py:371
  112.4 0.7 cut.1
  113.1 3.0 %collective-permute-start.6 = (s16[8,2176]{1,0:T(8,128)(2,1)S(1)}, s16[8,2176]{1,0:T(8,128)(2,1)S(1)}, u32[]{:S(2)}, u32[]{:S(2)}) collective-permute-start(s16[8,2176]{1,0:T(8,128)(2,1)S(1)} %get-tuple-element.29), channel_id=1, source_target_pairs={{0,256},{1,257},{2,258},{3,259},{4,260},{5,261},{6,262},{7,263},{8... | collective-permute-start | bytes 104456 | tf_op jit(solution)/shard_map/ppermute | solution.py:375
  116.1 4.7 %collective-permute-start.7 = (s16[8,2176]{1,0:T(8,128)(2,1)S(1)}, s16[8,2176]{1,0:T(8,128)(2,1)S(1)}, u32[]{:S(2)}, u32[]{:S(2)}) collective-permute-start(s16[8,2176]{1,0:T(8,128)(2,1)S(1)} %get-tuple-element.30), channel_id=1, source_target_pairs={{0,512},{1,513},{2,514},{3,515},{4,516},{5,517},{6,518},{7,519},{8... | collective-permute-start | bytes 104456 | tf_op jit(solution)/shard_map/ppermute | solution.py:375
  120.8 3.1 %collective-permute-start.8 = (s16[8,2176]{1,0:T(8,128)(2,1)S(1)}, s16[8,2176]{1,0:T(8,128)(2,1)S(1)}, u32[]{:S(2)}, u32[]{:S(2)}) collective-permute-start(s16[8,2176]{1,0:T(8,128)(2,1)S(1)} %get-tuple-element.31), channel_id=1, source_target_pairs={{0,768},{1,769},{2,770},{3,771},{4,772},{5,773},{6,774},{7,775},{8... | collective-permute-start | bytes 104456 | tf_op jit(solution)/shard_map/ppermute | solution.py:375
  123.9 0.2 collective-permute-done.7.b_ref
  124.1 3.6 %collective-permute-done.8.c_ref = s16[8,2176]{1,0:T(8,128)(2,1)S(1)} collective-permute-done((s16[8,2176]{1,0:T(8,128)(2,1)S(1)}, s16[8,2176]{1,0:T(8,128)(2,1)S(1)}, u32[]{:S(2)}, u32[]{:S(2)}) %collective-permute-start.8) | collective-permute-done | bytes 34848 | tf_op jit(solution)/shard_map/ppermute | solution.py:375
  127.9 8.3 %collective-permute-start.9 = (f32[8,4,256]{2,1,0:T(4,128)S(1)}, f32[8,4,256]{2,1,0:T(4,128)S(1)}, u32[]{:S(2)}, u32[]{:S(2)}) collective-permute-start(f32[8,4,256]{2,1,0:T(4,128)S(1)} %get-tuple-element.33), channel_id=1, source_target_pairs={{0,16},{1,17},{2,18},{3,19},{4,20},{5,21},{6,22},{7,23},{8,24},{9,... | collective-permute-start | bytes 98312 | tf_op jit(solution)/shard_map/ppermute | solution.py:378
  136.2 2.5 %place.1 = (bf16[8,32768]{1,0:T(8,128)(2,1)}, bf16[8,32768]{1,0:T(8,128)(2,1)}, f32[8,128]{1,0:T(8,128)S(1)}) custom-call(s32[256]{0:T(256)S(1)} %copy-done, s32[256]{0:T(256)S(1)} %copy-done.1, s16[16,8,6272]{2,1,0:T(8,128)(2,1)S(1)} %all-to-all-done.1.in_ref), custom_call_target="tpu_custom_call" | custom-call | tf_op jit(solution)/shard_map/place/pallas_call | solution.py:329
  138.7 0.6 join.1
  (14 shorter events, 0.2 us)
Async XLA Ops:
  59.9 5.0 %copy-start.2 = (bf16[16,256,256]{2,1,0:T(8,128)(2,1)S(1)}, bf16[16,256,256]{2,1,0:T(8,128)(2,1)}, u32[]{:S(2)}) copy-start(bf16[16,256,256]{2,1,0:T(8,128)(2,1)} %w_ref.1) | copy-start | bytes 6291460
  60.0 7.3 %collective-permute-start = (bf16[128,3072]{1,0:T(8,128)(2,1)S(1)}, bf16[128,3072]{1,0:T(8,128)(2,1)S(1)}, u32[]{:S(2)}, u32[]{:S(2)}) collective-permute-start(bf16[128,3072]{1,0:T(8,128)(2,1)S(1)} %half.1), channel_id=1, source_target_pairs={{0,16},{1,17},{2,18},{3,19},{4,20},{5,21},{6,22},{7,23},{8,24},{9,... | collective-permute-start | bytes 2359304 | tf_op jit(solution)/shard_map/ppermute | solution.py:363
  69.1 19.9 %collective-permute-start.1 = (s16[128,1152]{1,0:T(8,128)(2,1)}, s16[128,1152]{1,0:T(8,128)(2,1)S(1)}, u32[]{:S(2)}, u32[]{:S(2)}) collective-permute-start(s16[128,1152]{1,0:T(8,128)(2,1)} %get-tuple-element.22), channel_id=1, source_target_pairs={{0,32},{1,33},{2,34},{3,35},{4,36},{5,37},{6,38},{7,39},{8,40},{9,... | collective-permute-start | bytes 884744 | tf_op jit(solution)/shard_map/ppermute | solution.py:366
  72.4 16.6 %collective-permute-start.2 = (s16[128,1152]{1,0:T(8,128)(2,1)S(1)}, s16[128,1152]{1,0:T(8,128)(2,1)}, u32[]{:S(2)}, u32[]{:S(2)}) collective-permute-start(s16[128,1152]{1,0:T(8,128)(2,1)S(1)} %get-tuple-element.23), channel_id=1, source_target_pairs={{0,224},{1,225},{2,226},{3,227},{4,228},{5,229},{6,230},{7,231},{8... | collective-permute-start | bytes 884744 | tf_op jit(solution)/shard_map/ppermute | solution.py:367
  77.9 58.3 %all-to-all-start.1 = ((s16[16,8,6272]{2,1,0:T(8,128)(2,1)}), s16[16,8,6272]{2,1,0:T(8,128)(2,1)S(1)}, u32[]{:S(2)}, u32[]{:S(2)}) async-start(s16[16,8,6272]{2,1,0:T(8,128)(2,1)} %bitcast.1), calls=%async_computation.1 | async-start | bytes 3211264 | tf_op jit(solution)/shard_map/all_to_all | solution.py:368
  89.1 47.1 %copy-start = (s32[256]{0:T(256)S(1)}, s32[256]{0:T(256)}, u32[]{:S(2)}) copy-start(s32[256]{0:T(256)} %cols.3) | copy-start | bytes 3076
  89.1 47.1 %copy-start.1 = (s32[256]{0:T(256)S(1)}, s32[256]{0:T(256)}, u32[]{:S(2)}) copy-start(s32[256]{0:T(256)} %rows.3) | copy-start | bytes 3076
  91.1 10.9 %collective-permute-start.3 = (s16[32,2176]{1,0:T(8,128)(2,1)S(1)}, s16[32,2176]{1,0:T(8,128)(2,1)S(1)}, u32[]{:S(2)}, u32[]{:S(2)}) collective-permute-start(s16[32,2176]{1,0:T(8,128)(2,1)S(1)} %get-tuple-element.25), channel_id=1, source_target_pairs={{0,64},{1,65},{2,66},{3,67},{4,68},{5,69},{6,70},{7,71},{8,72},{9,... | collective-permute-start | bytes 417800 | tf_op jit(solution)/shard_map/ppermute | solution.py:371
  93.0 16.9 %collective-permute-start.4 = (s16[32,2176]{1,0:T(8,128)(2,1)S(1)}, s16[32,2176]{1,0:T(8,128)(2,1)S(1)}, u32[]{:S(2)}, u32[]{:S(2)}) collective-permute-start(s16[32,2176]{1,0:T(8,128)(2,1)S(1)} %get-tuple-element.26), channel_id=1, source_target_pairs={{0,192},{1,193},{2,194},{3,195},{4,196},{5,197},{6,198},{7,199},{8... | collective-permute-start | bytes 417800 | tf_op jit(solution)/shard_map/ppermute | solution.py:371
  98.5 14.0 %collective-permute-start.5 = (s16[32,2176]{1,0:T(8,128)(2,1)S(1)}, s16[32,2176]{1,0:T(8,128)(2,1)S(1)}, u32[]{:S(2)}, u32[]{:S(2)}) collective-permute-start(s16[32,2176]{1,0:T(8,128)(2,1)S(1)} %get-tuple-element.27), channel_id=1, source_target_pairs={{0,128},{1,129},{2,130},{3,131},{4,132},{5,133},{6,134},{7,135},{8... | collective-permute-start | bytes 417800 | tf_op jit(solution)/shard_map/ppermute | solution.py:371
  113.1 10.8 %collective-permute-start.6 = (s16[8,2176]{1,0:T(8,128)(2,1)S(1)}, s16[8,2176]{1,0:T(8,128)(2,1)S(1)}, u32[]{:S(2)}, u32[]{:S(2)}) collective-permute-start(s16[8,2176]{1,0:T(8,128)(2,1)S(1)} %get-tuple-element.29), channel_id=1, source_target_pairs={{0,256},{1,257},{2,258},{3,259},{4,260},{5,261},{6,262},{7,263},{8... | collective-permute-start | bytes 104456 | tf_op jit(solution)/shard_map/ppermute | solution.py:375
  116.1 8.0 %collective-permute-start.7 = (s16[8,2176]{1,0:T(8,128)(2,1)S(1)}, s16[8,2176]{1,0:T(8,128)(2,1)S(1)}, u32[]{:S(2)}, u32[]{:S(2)}) collective-permute-start(s16[8,2176]{1,0:T(8,128)(2,1)S(1)} %get-tuple-element.30), channel_id=1, source_target_pairs={{0,512},{1,513},{2,514},{3,515},{4,516},{5,517},{6,518},{7,519},{8... | collective-permute-start | bytes 104456 | tf_op jit(solution)/shard_map/ppermute | solution.py:375
  120.8 6.9 %collective-permute-start.8 = (s16[8,2176]{1,0:T(8,128)(2,1)S(1)}, s16[8,2176]{1,0:T(8,128)(2,1)S(1)}, u32[]{:S(2)}, u32[]{:S(2)}) collective-permute-start(s16[8,2176]{1,0:T(8,128)(2,1)S(1)} %get-tuple-element.31), channel_id=1, source_target_pairs={{0,768},{1,769},{2,770},{3,771},{4,772},{5,773},{6,774},{7,775},{8... | collective-permute-start | bytes 104456 | tf_op jit(solution)/shard_map/ppermute | solution.py:375
  127.9 10.8 %collective-permute-start.9 = (f32[8,4,256]{2,1,0:T(4,128)S(1)}, f32[8,4,256]{2,1,0:T(4,128)S(1)}, u32[]{:S(2)}, u32[]{:S(2)}) collective-permute-start(f32[8,4,256]{2,1,0:T(4,128)S(1)} %get-tuple-element.33), channel_id=1, source_target_pairs={{0,16},{1,17},{2,18},{3,19},{4,20},{5,21},{6,22},{7,23},{8,24},{9,... | collective-permute-start | bytes 98312 | tf_op jit(solution)/shard_map/ppermute | solution.py:378

commit v7 on v6

--- a/solution.py
+++ b/solution.py
@@ -16,7 +16,7 @@
 MESSAGE = 2 * HALF
 SCALES = 128
 STEPS = 16.0
-PAIR_STEPS = (1, 3, 2)
+PAIR_STEPS = (2, 1, 3)
 SMEM = pl.BlockSpec(memory_space=pltpu.SMEM)
 ANY = pl.BlockSpec(memory_space=pl.ANY)
 ROOM = pltpu.CompilerParams(vmem_limit_bytes=24 * 2**20)

time: 140 us -> 136 us (0.971)
  starting transfers between devices: 54.8 us -> 51.2 us
  waiting for transfers between devices: 14.3 us -> 12.5 us
    ppermute x1, starting transfers between devices: 8.29 us -> 3.75 us  [shards(): swapped = permute(send, perm=moves(lambda a, b, c: (a, b, 1 - c)))]
    ppermute x3, waiting for transfers between devices: 10.5 us -> 7.32 us  [shards(): permute(part, perm=moves(lambda a, b, c, d=d: (a, (b + 2 * d) % Y, c)))]
  transfers between devices with their start and end apart: 11 -> 11, of which waited for: 4 -> 5; matrix products, arithmetic and copies ran while one was open for 0% -> 0% of each run, Pallas kernels for 6% -> 6%
where the time goes in v7:
time: 136 us; the launch traced here: 134 us
  blocking collectives  56 us (41%)
  starting transfers between devices  51.2 us (38%)
  Pallas kernels  13.5 us (10%)
  waiting for transfers between devices  12.5 us (9%)
    all_to_all x1, blocking collectives, shards(): exchange(gather(block_cols, block_rows, shots_in, cotangent))  56 us
    ppermute x3, starting transfers between devices, shards(): permute(part, perm=moves(lambda a, b, c, d=d: (a ^ d + 1, b, c)))  11.8 us
    all_to_all x1, starting transfers between devices, shards(): back = exchange(result.reshape(OWNERS, S, MESSAGE + SCALES))  11.2 us
    ppermute x3, starting transfers between devices, shards(): permute(part, perm=moves(lambda a, b, c, d=d: (a, (b + 2 * d) % Y, c)))  10.9 us
    ppermute x3, waiting for transfers between devices, shards(): permute(part, perm=moves(lambda a, b, c, d=d: (a, (b + 2 * d) % Y, c)))  7.32 us
    ppermute x1, starting transfers between devices, shards(): permute(second, perm=moves(lambda a, b, c: (a, (b + 1 ^ 1) - 1 & 7, c)))  5.45 us
    ppermute x1, starting transfers between devices, shards(): other = permute(half(received), perm=moves(lambda a, b, c: (a, b, 1 - c)))  4.87 us
    ppermute x3, waiting for transfers between devices, shards(): permute(part, perm=moves(lambda a, b, c, d=d: (a ^ d + 1, b, c)))  4.12 us
  transfers between devices with their start and end apart: 11, of which 5 were waited for; matrix products, arithmetic and copies ran while one was open for 0% of the time, Pallas kernels for 6%

profile of v7, /device:TPU:1, one launch (start us, length us, event | category | flops | bytes accessed | tf_op | source)
XLA Modules:
  0.0 134.0 jit_solution(3341493014545621910)
XLA Ops:
  0.6 3.3 %gather.1 = bf16[16,8,6144]{2,1,0:T(8,128)(2,1)} custom-call(s32[256]{0:T(256)} %cols.3, s32[256]{0:T(256)} %rows.3, bf16[8,32768]{1,0:T(8,128)(2,1)} %x_hbm.1, bf16[8,32768]{1,0:T(8,128)(2,1)} %g_hbm.1), custom_call_target="tpu_custom_call" | custom-call | tf_op jit(solution)/shard_map/gather/pallas_call | solution.py:86
  3.9 56.0 %all_to_all.10 = bf16[16,8,6144]{2,1,0:T(8,128)(2,1)S(1)} all-to-all(bf16[16,8,6144]{2,1,0:T(8,128)(2,1)} %gather.1), channel_id=1, replica_groups={{0,1,2,3,4,5,6,7,520,521,522,523,524,525,526,527},{16,17,18,19,20,21,22..., dimensions={0} | all-to-all | bytes 3145728 | tf_op jit(solution)/shard_map/all_to_all | solution.py:362
  60.0 4.9 %collective-permute-start = (bf16[128,3072]{1,0:T(8,128)(2,1)S(1)}, bf16[128,3072]{1,0:T(8,128)(2,1)S(1)}, u32[]{:S(2)}, u32[]{:S(2)}) collective-permute-start(bf16[128,3072]{1,0:T(8,128)(2,1)S(1)} %half.1), channel_id=1, source_target_pairs={{0,16},{1,17},{2,18},{3,19},{4,20},{5,21},{6,22},{7,23},{8,24},{9,... | collective-permute-start | bytes 2359304 | tf_op jit(solution)/shard_map/ppermute | solution.py:363
  64.9 2.5 %apply.1.after_ref = s16[128,6272]{1,0:T(8,128)(2,1)} custom-call(bf16[128,6144]{1,0:T(8,128)(2,1)S(1)} %bitcast.3, bf16[16,256,256]{2,1,0:T(8,128)(2,1)S(1)} %copy-done.2), custom_call_target="tpu_custom_call" | custom-call | flops 5000000000 | bytes 20000000 | tf_op jit(solution)/shard_map/apply/pallas_call | solution.py:208
  67.3 1.8 %grad.1 = (s16[128,1152]{1,0:T(8,128)(2,1)}, s16[128,1152]{1,0:T(8,128)(2,1)S(1)}, f32[128,2048]{1,0:T(8,128)S(1)}) custom-call(bf16[128,6144]{1,0:T(8,128)(2,1)S(1)} %bitcast.4, bf16[128,3072]{1,0:T(8,128)(2,1)S(1)} %collective-permute-done.other_ref, s16[128,6272]{1,0:T(8,128)(2,1)} %apply.1.after_ref), custom_call_target="tpu_custom_call" | custom-call | tf_op jit(solution)/shard_map/grad/pallas_call | solution.py:179
  69.1 3.3 %collective-permute-start.1 = (s16[128,1152]{1,0:T(8,128)(2,1)}, s16[128,1152]{1,0:T(8,128)(2,1)S(1)}, u32[]{:S(2)}, u32[]{:S(2)}) collective-permute-start(s16[128,1152]{1,0:T(8,128)(2,1)} %get-tuple-element.22), channel_id=1, source_target_pairs={{0,32},{1,33},{2,34},{3,35},{4,36},{5,37},{6,38},{7,39},{8,40},{9,... | collective-permute-start | bytes 884744 | tf_op jit(solution)/shard_map/ppermute | solution.py:366
  72.4 5.4 %collective-permute-start.2 = (s16[128,1152]{1,0:T(8,128)(2,1)S(1)}, s16[128,1152]{1,0:T(8,128)(2,1)}, u32[]{:S(2)}, u32[]{:S(2)}) collective-permute-start(s16[128,1152]{1,0:T(8,128)(2,1)S(1)} %get-tuple-element.23), channel_id=1, source_target_pairs={{0,224},{1,225},{2,226},{3,227},{4,228},{5,229},{6,230},{7,231},{8... | collective-permute-start | bytes 884744 | tf_op jit(solution)/shard_map/ppermute | solution.py:367
  77.9 11.2 %all-to-all-start.1 = ((s16[16,8,6272]{2,1,0:T(8,128)(2,1)}), s16[16,8,6272]{2,1,0:T(8,128)(2,1)S(1)}, u32[]{:S(2)}, u32[]{:S(2)}) async-start(s16[16,8,6272]{2,1,0:T(8,128)(2,1)} %bitcast.1), calls=%async_computation.1 | async-start | bytes 3211264 | tf_op jit(solution)/shard_map/all_to_all | solution.py:368
  89.1 1.9 %pairs.1 = (s16[32,2176]{1,0:T(8,128)(2,1)S(1)}, s16[32,2176]{1,0:T(8,128)(2,1)S(1)}, s16[32,2176]{1,0:T(8,128)(2,1)S(1)}, f32[32,2048]{1,0:T(8,128)S(1)}) custom-call(f32[128,2048]{1,0:T(8,128)S(1)} %get-tuple-element.21.keep_ref, s16[128,1152]{1,0:T(8,128)(2,1)S(1)} %collective-permute-done.1.first_ref, s16[128,1152]{1,0:T(8,128)(2,1)} %collective-permute-done.2.second_ref), custom_call_target="tpu_custom_call" | custom-call | flops 80000000000 | bytes 1000000 | tf_op jit(solution)/shard_map/pairs/pallas_call | solution.py:238
  91.1 3.5 %collective-permute-start.3 = (s16[32,2176]{1,0:T(8,128)(2,1)S(1)}, s16[32,2176]{1,0:T(8,128)(2,1)S(1)}, u32[]{:S(2)}, u32[]{:S(2)}) collective-permute-start(s16[32,2176]{1,0:T(8,128)(2,1)S(1)} %get-tuple-element.25), channel_id=1, source_target_pairs={{0,128},{1,129},{2,130},{3,131},{4,132},{5,133},{6,134},{7,135},{8... | collective-permute-start | bytes 417800 | tf_op jit(solution)/shard_map/ppermute | solution.py:371
  94.5 4.0 %collective-permute-start.4 = (s16[32,2176]{1,0:T(8,128)(2,1)S(1)}, s16[32,2176]{1,0:T(8,128)(2,1)S(1)}, u32[]{:S(2)}, u32[]{:S(2)}) collective-permute-start(s16[32,2176]{1,0:T(8,128)(2,1)S(1)} %get-tuple-element.26), channel_id=1, source_target_pairs={{0,64},{1,65},{2,66},{3,67},{4,68},{5,69},{6,70},{7,71},{8,72},{9,... | collective-permute-start | bytes 417800 | tf_op jit(solution)/shard_map/ppermute | solution.py:371
  98.6 3.4 %collective-permute-start.5 = (s16[32,2176]{1,0:T(8,128)(2,1)S(1)}, s16[32,2176]{1,0:T(8,128)(2,1)S(1)}, u32[]{:S(2)}, u32[]{:S(2)}) collective-permute-start(s16[32,2176]{1,0:T(8,128)(2,1)S(1)} %get-tuple-element.27), channel_id=1, source_target_pairs={{0,192},{1,193},{2,194},{3,195},{4,196},{5,197},{6,198},{7,199},{8... | collective-permute-start | bytes 417800 | tf_op jit(solution)/shard_map/ppermute | solution.py:371
  102.0 1.6 %collective-permute-done.4.b_ref = s16[32,2176]{1,0:T(8,128)(2,1)S(1)} collective-permute-done((s16[32,2176]{1,0:T(8,128)(2,1)S(1)}, s16[32,2176]{1,0:T(8,128)(2,1)S(1)}, u32[]{:S(2)}, u32[]{:S(2)}) %collective-permute-start.4) | collective-permute-done | bytes 139296 | tf_op jit(solution)/shard_map/ppermute | solution.py:371
  103.6 5.7 %collective-permute-done.5.c_ref = s16[32,2176]{1,0:T(8,128)(2,1)S(1)} collective-permute-done((s16[32,2176]{1,0:T(8,128)(2,1)S(1)}, s16[32,2176]{1,0:T(8,128)(2,1)S(1)}, u32[]{:S(2)}, u32[]{:S(2)}) %collective-permute-start.5) | collective-permute-done | bytes 139296 | tf_op jit(solution)/shard_map/ppermute | solution.py:371
  109.3 0.7 cut.1
  110.0 4.1 %collective-permute-start.6 = (s16[8,2176]{1,0:T(8,128)(2,1)S(1)}, s16[8,2176]{1,0:T(8,128)(2,1)S(1)}, u32[]{:S(2)}, u32[]{:S(2)}) collective-permute-start(s16[8,2176]{1,0:T(8,128)(2,1)S(1)} %get-tuple-element.29), channel_id=1, source_target_pairs={{0,256},{1,257},{2,258},{3,259},{4,260},{5,261},{6,262},{7,263},{8... | collective-permute-start | bytes 104456 | tf_op jit(solution)/shard_map/ppermute | solution.py:375
  114.1 4.6 %collective-permute-start.7 = (s16[8,2176]{1,0:T(8,128)(2,1)S(1)}, s16[8,2176]{1,0:T(8,128)(2,1)S(1)}, u32[]{:S(2)}, u32[]{:S(2)}) collective-permute-start(s16[8,2176]{1,0:T(8,128)(2,1)S(1)} %get-tuple-element.30), channel_id=1, source_target_pairs={{0,512},{1,513},{2,514},{3,515},{4,516},{5,517},{6,518},{7,519},{8... | collective-permute-start | bytes 104456 | tf_op jit(solution)/shard_map/ppermute | solution.py:375
  118.7 3.1 %collective-permute-start.8 = (s16[8,2176]{1,0:T(8,128)(2,1)S(1)}, s16[8,2176]{1,0:T(8,128)(2,1)S(1)}, u32[]{:S(2)}, u32[]{:S(2)}) collective-permute-start(s16[8,2176]{1,0:T(8,128)(2,1)S(1)} %get-tuple-element.31), channel_id=1, source_target_pairs={{0,768},{1,769},{2,770},{3,771},{4,772},{5,773},{6,774},{7,775},{8... | collective-permute-start | bytes 104456 | tf_op jit(solution)/shard_map/ppermute | solution.py:375
  121.8 2.6 %collective-permute-done.7.b_ref = s16[8,2176]{1,0:T(8,128)(2,1)S(1)} collective-permute-done((s16[8,2176]{1,0:T(8,128)(2,1)S(1)}, s16[8,2176]{1,0:T(8,128)(2,1)S(1)}, u32[]{:S(2)}, u32[]{:S(2)}) %collective-permute-start.7) | collective-permute-done | bytes 34848 | tf_op jit(solution)/shard_map/ppermute | solution.py:375
  124.4 1.5 %collective-permute-done.8.c_ref = s16[8,2176]{1,0:T(8,128)(2,1)S(1)} collective-permute-done((s16[8,2176]{1,0:T(8,128)(2,1)S(1)}, s16[8,2176]{1,0:T(8,128)(2,1)S(1)}, u32[]{:S(2)}, u32[]{:S(2)}) %collective-permute-start.8) | collective-permute-done | bytes 34848 | tf_op jit(solution)/shard_map/ppermute | solution.py:375
  126.0 3.8 %collective-permute-start.9 = (f32[8,4,256]{2,1,0:T(4,128)S(1)}, f32[8,4,256]{2,1,0:T(4,128)S(1)}, u32[]{:S(2)}, u32[]{:S(2)}) collective-permute-start(f32[8,4,256]{2,1,0:T(4,128)S(1)} %get-tuple-element.33), channel_id=1, source_target_pairs={{0,16},{1,17},{2,18},{3,19},{4,20},{5,21},{6,22},{7,23},{8,24},{9,... | collective-permute-start | bytes 98312 | tf_op jit(solution)/shard_map/ppermute | solution.py:378
  129.8 1.0 all-to-all-done.1.in_ref
  130.8 2.5 %place.1 = (bf16[8,32768]{1,0:T(8,128)(2,1)}, bf16[8,32768]{1,0:T(8,128)(2,1)}, f32[8,128]{1,0:T(8,128)S(1)}) custom-call(s32[256]{0:T(256)S(1)} %copy-done, s32[256]{0:T(256)S(1)} %copy-done.1, s16[16,8,6272]{2,1,0:T(8,128)(2,1)S(1)} %all-to-all-done.1.in_ref), custom_call_target="tpu_custom_call" | custom-call | tf_op jit(solution)/shard_map/place/pallas_call | solution.py:329
  133.3 0.6 join.1
  (14 shorter events, 0.3 us)
Async XLA Ops:
  59.9 5.0 %copy-start.2 = (bf16[16,256,256]{2,1,0:T(8,128)(2,1)S(1)}, bf16[16,256,256]{2,1,0:T(8,128)(2,1)}, u32[]{:S(2)}) copy-start(bf16[16,256,256]{2,1,0:T(8,128)(2,1)} %w_ref.1) | copy-start | bytes 6291460
  60.0 7.3 %collective-permute-start = (bf16[128,3072]{1,0:T(8,128)(2,1)S(1)}, bf16[128,3072]{1,0:T(8,128)(2,1)S(1)}, u32[]{:S(2)}, u32[]{:S(2)}) collective-permute-start(bf16[128,3072]{1,0:T(8,128)(2,1)S(1)} %half.1), channel_id=1, source_target_pairs={{0,16},{1,17},{2,18},{3,19},{4,20},{5,21},{6,22},{7,23},{8,24},{9,... | collective-permute-start | bytes 2359304 | tf_op jit(solution)/shard_map/ppermute | solution.py:363
  69.1 19.9 %collective-permute-start.1 = (s16[128,1152]{1,0:T(8,128)(2,1)}, s16[128,1152]{1,0:T(8,128)(2,1)S(1)}, u32[]{:S(2)}, u32[]{:S(2)}) collective-permute-start(s16[128,1152]{1,0:T(8,128)(2,1)} %get-tuple-element.22), channel_id=1, source_target_pairs={{0,32},{1,33},{2,34},{3,35},{4,36},{5,37},{6,38},{7,39},{8,40},{9,... | collective-permute-start | bytes 884744 | tf_op jit(solution)/shard_map/ppermute | solution.py:366
  72.4 16.6 %collective-permute-start.2 = (s16[128,1152]{1,0:T(8,128)(2,1)S(1)}, s16[128,1152]{1,0:T(8,128)(2,1)}, u32[]{:S(2)}, u32[]{:S(2)}) collective-permute-start(s16[128,1152]{1,0:T(8,128)(2,1)S(1)} %get-tuple-element.23), channel_id=1, source_target_pairs={{0,224},{1,225},{2,226},{3,227},{4,228},{5,229},{6,230},{7,231},{8... | collective-permute-start | bytes 884744 | tf_op jit(solution)/shard_map/ppermute | solution.py:367
  77.9 52.9 %all-to-all-start.1 = ((s16[16,8,6272]{2,1,0:T(8,128)(2,1)}), s16[16,8,6272]{2,1,0:T(8,128)(2,1)S(1)}, u32[]{:S(2)}, u32[]{:S(2)}) async-start(s16[16,8,6272]{2,1,0:T(8,128)(2,1)} %bitcast.1), calls=%async_computation.1 | async-start | bytes 3211264 | tf_op jit(solution)/shard_map/all_to_all | solution.py:368
  89.1 41.7 %copy-start = (s32[256]{0:T(256)S(1)}, s32[256]{0:T(256)}, u32[]{:S(2)}) copy-start(s32[256]{0:T(256)} %cols.3) | copy-start | bytes 3076
  89.1 41.7 %copy-start.1 = (s32[256]{0:T(256)S(1)}, s32[256]{0:T(256)}, u32[]{:S(2)}) copy-start(s32[256]{0:T(256)} %rows.3) | copy-start | bytes 3076
  91.1 10.9 %collective-permute-start.3 = (s16[32,2176]{1,0:T(8,128)(2,1)S(1)}, s16[32,2176]{1,0:T(8,128)(2,1)S(1)}, u32[]{:S(2)}, u32[]{:S(2)}) collective-permute-start(s16[32,2176]{1,0:T(8,128)(2,1)S(1)} %get-tuple-element.25), channel_id=1, source_target_pairs={{0,128},{1,129},{2,130},{3,131},{4,132},{5,133},{6,134},{7,135},{8... | collective-permute-start | bytes 417800 | tf_op jit(solution)/shard_map/ppermute | solution.py:371
  94.5 9.1 %collective-permute-start.4 = (s16[32,2176]{1,0:T(8,128)(2,1)S(1)}, s16[32,2176]{1,0:T(8,128)(2,1)S(1)}, u32[]{:S(2)}, u32[]{:S(2)}) collective-permute-start(s16[32,2176]{1,0:T(8,128)(2,1)S(1)} %get-tuple-element.26), channel_id=1, source_target_pairs={{0,64},{1,65},{2,66},{3,67},{4,68},{5,69},{6,70},{7,71},{8,72},{9,... | collective-permute-start | bytes 417800 | tf_op jit(solution)/shard_map/ppermute | solution.py:371
  98.6 10.7 %collective-permute-start.5 = (s16[32,2176]{1,0:T(8,128)(2,1)S(1)}, s16[32,2176]{1,0:T(8,128)(2,1)S(1)}, u32[]{:S(2)}, u32[]{:S(2)}) collective-permute-start(s16[32,2176]{1,0:T(8,128)(2,1)S(1)} %get-tuple-element.27), channel_id=1, source_target_pairs={{0,192},{1,193},{2,194},{3,195},{4,196},{5,197},{6,198},{7,199},{8... | collective-permute-start | bytes 417800 | tf_op jit(solution)/shard_map/ppermute | solution.py:371
  110.0 11.8 %collective-permute-start.6 = (s16[8,2176]{1,0:T(8,128)(2,1)S(1)}, s16[8,2176]{1,0:T(8,128)(2,1)S(1)}, u32[]{:S(2)}, u32[]{:S(2)}) collective-permute-start(s16[8,2176]{1,0:T(8,128)(2,1)S(1)} %get-tuple-element.29), channel_id=1, source_target_pairs={{0,256},{1,257},{2,258},{3,259},{4,260},{5,261},{6,262},{7,263},{8... | collective-permute-start | bytes 104456 | tf_op jit(solution)/shard_map/ppermute | solution.py:375
  114.1 10.3 %collective-permute-start.7 = (s16[8,2176]{1,0:T(8,128)(2,1)S(1)}, s16[8,2176]{1,0:T(8,128)(2,1)S(1)}, u32[]{:S(2)}, u32[]{:S(2)}) collective-permute-start(s16[8,2176]{1,0:T(8,128)(2,1)S(1)} %get-tuple-element.30), channel_id=1, source_target_pairs={{0,512},{1,513},{2,514},{3,515},{4,516},{5,517},{6,518},{7,519},{8... | collective-permute-start | bytes 104456 | tf_op jit(solution)/shard_map/ppermute | solution.py:375
  118.7 7.2 %collective-permute-start.8 = (s16[8,2176]{1,0:T(8,128)(2,1)S(1)}, s16[8,2176]{1,0:T(8,128)(2,1)S(1)}, u32[]{:S(2)}, u32[]{:S(2)}) collective-permute-start(s16[8,2176]{1,0:T(8,128)(2,1)S(1)} %get-tuple-element.31), channel_id=1, source_target_pairs={{0,768},{1,769},{2,770},{3,771},{4,772},{5,773},{6,774},{7,775},{8... | collective-permute-start | bytes 104456 | tf_op jit(solution)/shard_map/ppermute | solution.py:375
  126.0 7.3 %collective-permute-start.9 = (f32[8,4,256]{2,1,0:T(4,128)S(1)}, f32[8,4,256]{2,1,0:T(4,128)S(1)}, u32[]{:S(2)}, u32[]{:S(2)}) collective-permute-start(f32[8,4,256]{2,1,0:T(4,128)S(1)} %get-tuple-element.33), channel_id=1, source_target_pairs={{0,16},{1,17},{2,18},{3,19},{4,20},{5,21},{6,22},{7,23},{8,24},{9,... | collective-permute-start | bytes 98312 | tf_op jit(solution)/shard_map/ppermute | solution.py:378

commit v8 on v7

--- a/solution.py
+++ b/solution.py
@@ -372,7 +372,7 @@
     ]
     *parts, own = cut(own, parts)
     parts = [
-        permute(part, perm=moves(lambda a, b, c, d=d: (a ^ (d + 1), b, c))) for d, part in enumerate(parts)
+        permute(part, perm=moves(lambda a, b, c, d=d: (a ^ (d + 1), b, c))) for d, part in reversed(list(enumerate(parts)))
     ]
     mine, send = last(own, parts)
     swapped = permute(send, perm=moves(lambda a, b, c: (a, b, 1 - c)))

time: 136 us -> 135 us (level)
  starting transfers between devices: 51.2 us -> 48.8 us
  waiting for transfers between devices: 12.5 us -> 14.8 us
    all_to_all x1, waiting for transfers between devices: 1.02 us -> 2.66 us  [shards(): back = exchange(result.reshape(OWNERS, S, MESSAGE + SCALES))]
    ppermute x1, starting transfers between devices: 3.75 us -> 2.29 us  [shards(): swapped = permute(send, perm=moves(lambda a, b, c: (a, b, 1 - c)))]
where the time goes in v8:
time: 135 us; the launch traced here: 134 us
  blocking collectives  56 us (41%)
  starting transfers between devices  48.8 us (36%)
  waiting for transfers between devices  14.8 us (11%)
  Pallas kernels  13.5 us (10%)
    all_to_all x1, blocking collectives, shards(): exchange(gather(block_cols, block_rows, shots_in, cotangent))  56 us
    all_to_all x1, starting transfers between devices, shards(): back = exchange(result.reshape(OWNERS, S, MESSAGE + SCALES))  11.2 us
    ppermute x3, starting transfers between devices, shards(): permute(part, perm=moves(lambda a, b, c, d=d: (a ^ d + 1, b, c)))  10.9 us
    ppermute x3, starting transfers between devices, shards(): permute(part, perm=moves(lambda a, b, c, d=d: (a, (b + 2 * d) % Y, c)))  10.9 us
    ppermute x3, waiting for transfers between devices, shards(): permute(part, perm=moves(lambda a, b, c, d=d: (a, (b + 2 * d) % Y, c)))  7.32 us
    ppermute x1, starting transfers between devices, shards(): permute(second, perm=moves(lambda a, b, c: (a, (b + 1 ^ 1) - 1 & 7, c)))  5.45 us
    ppermute x1, starting transfers between devices, shards(): other = permute(half(received), perm=moves(lambda a, b, c: (a, b, 1 - c)))  4.87 us
    ppermute x3, waiting for transfers between devices, shards(): permute(part, perm=moves(lambda a, b, c, d=d: (a ^ d + 1, b, c)))  4.84 us
  transfers between devices with their start and end apart: 11, of which 5 were waited for; matrix products, arithmetic and copies ran while one was open for 0% of the time, Pallas kernels for 6%

profile of v8, /device:TPU:1, one launch (start us, length us, event | category | flops | bytes accessed | tf_op | source)
XLA Modules:
  0.0 134.0 jit_solution(17791195925465093876)
XLA Ops:
  0.6 3.3 %gather.1 = bf16[16,8,6144]{2,1,0:T(8,128)(2,1)} custom-call(s32[256]{0:T(256)} %cols.3, s32[256]{0:T(256)} %rows.3, bf16[8,32768]{1,0:T(8,128)(2,1)} %x_hbm.1, bf16[8,32768]{1,0:T(8,128)(2,1)} %g_hbm.1), custom_call_target="tpu_custom_call" | custom-call | tf_op jit(solution)/shard_map/gather/pallas_call | solution.py:86
  3.9 56.0 %all_to_all.10 = bf16[16,8,6144]{2,1,0:T(8,128)(2,1)S(1)} all-to-all(bf16[16,8,6144]{2,1,0:T(8,128)(2,1)} %gather.1), channel_id=1, replica_groups={{0,1,2,3,4,5,6,7,520,521,522,523,524,525,526,527},{16,17,18,19,20,21,22..., dimensions={0} | all-to-all | bytes 3145728 | tf_op jit(solution)/shard_map/all_to_all | solution.py:362
  60.0 4.9 %collective-permute-start = (bf16[128,3072]{1,0:T(8,128)(2,1)S(1)}, bf16[128,3072]{1,0:T(8,128)(2,1)S(1)}, u32[]{:S(2)}, u32[]{:S(2)}) collective-permute-start(bf16[128,3072]{1,0:T(8,128)(2,1)S(1)} %half.1), channel_id=1, source_target_pairs={{0,16},{1,17},{2,18},{3,19},{4,20},{5,21},{6,22},{7,23},{8,24},{9,... | collective-permute-start | bytes 2359304 | tf_op jit(solution)/shard_map/ppermute | solution.py:363
  64.9 2.5 %apply.1.after_ref = s16[128,6272]{1,0:T(8,128)(2,1)} custom-call(bf16[128,6144]{1,0:T(8,128)(2,1)S(1)} %bitcast.3, bf16[16,256,256]{2,1,0:T(8,128)(2,1)S(1)} %copy-done.2), custom_call_target="tpu_custom_call" | custom-call | flops 5000000000 | bytes 20000000 | tf_op jit(solution)/shard_map/apply/pallas_call | solution.py:208
  67.3 1.8 %grad.1 = (s16[128,1152]{1,0:T(8,128)(2,1)}, s16[128,1152]{1,0:T(8,128)(2,1)S(1)}, f32[128,2048]{1,0:T(8,128)S(1)}) custom-call(bf16[128,6144]{1,0:T(8,128)(2,1)S(1)} %bitcast.4, bf16[128,3072]{1,0:T(8,128)(2,1)S(1)} %collective-permute-done.other_ref, s16[128,6272]{1,0:T(8,128)(2,1)} %apply.1.after_ref), custom_call_target="tpu_custom_call" | custom-call | tf_op jit(solution)/shard_map/grad/pallas_call | solution.py:179
  69.1 3.3 %collective-permute-start.1 = (s16[128,1152]{1,0:T(8,128)(2,1)}, s16[128,1152]{1,0:T(8,128)(2,1)S(1)}, u32[]{:S(2)}, u32[]{:S(2)}) collective-permute-start(s16[128,1152]{1,0:T(8,128)(2,1)} %get-tuple-element.22), channel_id=1, source_target_pairs={{0,32},{1,33},{2,34},{3,35},{4,36},{5,37},{6,38},{7,39},{8,40},{9,... | collective-permute-start | bytes 884744 | tf_op jit(solution)/shard_map/ppermute | solution.py:366
  72.4 5.4 %collective-permute-start.2 = (s16[128,1152]{1,0:T(8,128)(2,1)S(1)}, s16[128,1152]{1,0:T(8,128)(2,1)}, u32[]{:S(2)}, u32[]{:S(2)}) collective-permute-start(s16[128,1152]{1,0:T(8,128)(2,1)S(1)} %get-tuple-element.23), channel_id=1, source_target_pairs={{0,224},{1,225},{2,226},{3,227},{4,228},{5,229},{6,230},{7,231},{8... | collective-permute-start | bytes 884744 | tf_op jit(solution)/shard_map/ppermute | solution.py:367
  77.9 11.2 %all-to-all-start.1 = ((s16[16,8,6272]{2,1,0:T(8,128)(2,1)}), s16[16,8,6272]{2,1,0:T(8,128)(2,1)S(1)}, u32[]{:S(2)}, u32[]{:S(2)}) async-start(s16[16,8,6272]{2,1,0:T(8,128)(2,1)} %bitcast.1), calls=%async_computation.1 | async-start | bytes 3211264 | tf_op jit(solution)/shard_map/all_to_all | solution.py:368
  89.1 1.9 %pairs.1 = (s16[32,2176]{1,0:T(8,128)(2,1)S(1)}, s16[32,2176]{1,0:T(8,128)(2,1)S(1)}, s16[32,2176]{1,0:T(8,128)(2,1)S(1)}, f32[32,2048]{1,0:T(8,128)S(1)}) custom-call(f32[128,2048]{1,0:T(8,128)S(1)} %get-tuple-element.21.keep_ref, s16[128,1152]{1,0:T(8,128)(2,1)S(1)} %collective-permute-done.1.first_ref, s16[128,1152]{1,0:T(8,128)(2,1)} %collective-permute-done.2.second_ref), custom_call_target="tpu_custom_call" | custom-call | flops 80000000000 | bytes 1000000 | tf_op jit(solution)/shard_map/pairs/pallas_call | solution.py:238
  91.1 3.5 %collective-permute-start.3 = (s16[32,2176]{1,0:T(8,128)(2,1)S(1)}, s16[32,2176]{1,0:T(8,128)(2,1)S(1)}, u32[]{:S(2)}, u32[]{:S(2)}) collective-permute-start(s16[32,2176]{1,0:T(8,128)(2,1)S(1)} %get-tuple-element.25), channel_id=1, source_target_pairs={{0,128},{1,129},{2,130},{3,131},{4,132},{5,133},{6,134},{7,135},{8... | collective-permute-start | bytes 417800 | tf_op jit(solution)/shard_map/ppermute | solution.py:371
  94.5 4.0 %collective-permute-start.4 = (s16[32,2176]{1,0:T(8,128)(2,1)S(1)}, s16[32,2176]{1,0:T(8,128)(2,1)S(1)}, u32[]{:S(2)}, u32[]{:S(2)}) collective-permute-start(s16[32,2176]{1,0:T(8,128)(2,1)S(1)} %get-tuple-element.26), channel_id=1, source_target_pairs={{0,64},{1,65},{2,66},{3,67},{4,68},{5,69},{6,70},{7,71},{8,72},{9,... | collective-permute-start | bytes 417800 | tf_op jit(solution)/shard_map/ppermute | solution.py:371
  98.6 3.4 %collective-permute-start.5 = (s16[32,2176]{1,0:T(8,128)(2,1)S(1)}, s16[32,2176]{1,0:T(8,128)(2,1)S(1)}, u32[]{:S(2)}, u32[]{:S(2)}) collective-permute-start(s16[32,2176]{1,0:T(8,128)(2,1)S(1)} %get-tuple-element.27), channel_id=1, source_target_pairs={{0,192},{1,193},{2,194},{3,195},{4,196},{5,197},{6,198},{7,199},{8... | collective-permute-start | bytes 417800 | tf_op jit(solution)/shard_map/ppermute | solution.py:371
  102.0 1.6 %collective-permute-done.4.b_ref = s16[32,2176]{1,0:T(8,128)(2,1)S(1)} collective-permute-done((s16[32,2176]{1,0:T(8,128)(2,1)S(1)}, s16[32,2176]{1,0:T(8,128)(2,1)S(1)}, u32[]{:S(2)}, u32[]{:S(2)}) %collective-permute-start.4) | collective-permute-done | bytes 139296 | tf_op jit(solution)/shard_map/ppermute | solution.py:371
  103.6 5.7 %collective-permute-done.5.c_ref = s16[32,2176]{1,0:T(8,128)(2,1)S(1)} collective-permute-done((s16[32,2176]{1,0:T(8,128)(2,1)S(1)}, s16[32,2176]{1,0:T(8,128)(2,1)S(1)}, u32[]{:S(2)}, u32[]{:S(2)}) %collective-permute-start.5) | collective-permute-done | bytes 139296 | tf_op jit(solution)/shard_map/ppermute | solution.py:371
  109.3 0.7 cut.1
  110.0 1.9 %collective-permute-start.6 = (s16[8,2176]{1,0:T(8,128)(2,1)S(1)}, s16[8,2176]{1,0:T(8,128)(2,1)S(1)}, u32[]{:S(2)}, u32[]{:S(2)}) collective-permute-start(s16[8,2176]{1,0:T(8,128)(2,1)S(1)} %get-tuple-element.29), channel_id=1, source_target_pairs={{0,768},{1,769},{2,770},{3,771},{4,772},{5,773},{6,774},{7,775},{8... | collective-permute-start | bytes 104456 | tf_op jit(solution)/shard_map/ppermute | solution.py:375
  111.9 6.8 %collective-permute-start.7 = (s16[8,2176]{1,0:T(8,128)(2,1)S(1)}, s16[8,2176]{1,0:T(8,128)(2,1)S(1)}, u32[]{:S(2)}, u32[]{:S(2)}) collective-permute-start(s16[8,2176]{1,0:T(8,128)(2,1)S(1)} %get-tuple-element.30), channel_id=1, source_target_pairs={{0,512},{1,513},{2,514},{3,515},{4,516},{5,517},{6,518},{7,519},{8... | collective-permute-start | bytes 104456 | tf_op jit(solution)/shard_map/ppermute | solution.py:375
  118.7 2.2 %collective-permute-start.8 = (s16[8,2176]{1,0:T(8,128)(2,1)S(1)}, s16[8,2176]{1,0:T(8,128)(2,1)S(1)}, u32[]{:S(2)}, u32[]{:S(2)}) collective-permute-start(s16[8,2176]{1,0:T(8,128)(2,1)S(1)} %get-tuple-element.31), channel_id=1, source_target_pairs={{0,256},{1,257},{2,258},{3,259},{4,260},{5,261},{6,262},{7,263},{8... | collective-permute-start | bytes 104456 | tf_op jit(solution)/shard_map/ppermute | solution.py:375
  120.9 3.2 %collective-permute-done.7.b_ref = s16[8,2176]{1,0:T(8,128)(2,1)S(1)} collective-permute-done((s16[8,2176]{1,0:T(8,128)(2,1)S(1)}, s16[8,2176]{1,0:T(8,128)(2,1)S(1)}, u32[]{:S(2)}, u32[]{:S(2)}) %collective-permute-start.7) | collective-permute-done | bytes 34848 | tf_op jit(solution)/shard_map/ppermute | solution.py:375
  124.1 1.6 %collective-permute-done.8.c_ref = s16[8,2176]{1,0:T(8,128)(2,1)S(1)} collective-permute-done((s16[8,2176]{1,0:T(8,128)(2,1)S(1)}, s16[8,2176]{1,0:T(8,128)(2,1)S(1)}, u32[]{:S(2)}, u32[]{:S(2)}) %collective-permute-start.8) | collective-permute-done | bytes 34848 | tf_op jit(solution)/shard_map/ppermute | solution.py:375
  125.9 2.3 %collective-permute-start.9 = (f32[8,4,256]{2,1,0:T(4,128)S(1)}, f32[8,4,256]{2,1,0:T(4,128)S(1)}, u32[]{:S(2)}, u32[]{:S(2)}) collective-permute-start(f32[8,4,256]{2,1,0:T(4,128)S(1)} %get-tuple-element.33), channel_id=1, source_target_pairs={{0,16},{1,17},{2,18},{3,19},{4,20},{5,21},{6,22},{7,23},{8,24},{9,... | collective-permute-start | bytes 98312 | tf_op jit(solution)/shard_map/ppermute | solution.py:378
  128.2 2.7 %all-to-all-done.1.in_ref = s16[16,8,6272]{2,1,0:T(8,128)(2,1)S(1)} async-done(((s16[16,8,6272]{2,1,0:T(8,128)(2,1)}), s16[16,8,6272]{2,1,0:T(8,128)(2,1)S(1)}, u32[]{:S(2)}, u32[]{:S(2)}) %all-to-all-start.1) | async-done | bytes 1605664 | tf_op jit(solution)/shard_map/all_to_all | solution.py:368
  130.8 2.5 %place.1 = (bf16[8,32768]{1,0:T(8,128)(2,1)}, bf16[8,32768]{1,0:T(8,128)(2,1)}, f32[8,128]{1,0:T(8,128)S(1)}) custom-call(s32[256]{0:T(256)S(1)} %copy-done, s32[256]{0:T(256)S(1)} %copy-done.1, s16[16,8,6272]{2,1,0:T(8,128)(2,1)S(1)} %all-to-all-done.1.in_ref), custom_call_target="tpu_custom_call" | custom-call | tf_op jit(solution)/shard_map/place/pallas_call | solution.py:329
  133.3 0.6 join.1
  (14 shorter events, 0.3 us)
Async XLA Ops:
  59.9 5.0 %copy-start.2 = (bf16[16,256,256]{2,1,0:T(8,128)(2,1)S(1)}, bf16[16,256,256]{2,1,0:T(8,128)(2,1)}, u32[]{:S(2)}) copy-start(bf16[16,256,256]{2,1,0:T(8,128)(2,1)} %w_ref.1) | copy-start | bytes 6291460
  60.0 7.3 %collective-permute-start = (bf16[128,3072]{1,0:T(8,128)(2,1)S(1)}, bf16[128,3072]{1,0:T(8,128)(2,1)S(1)}, u32[]{:S(2)}, u32[]{:S(2)}) collective-permute-start(bf16[128,3072]{1,0:T(8,128)(2,1)S(1)} %half.1), channel_id=1, source_target_pairs={{0,16},{1,17},{2,18},{3,19},{4,20},{5,21},{6,22},{7,23},{8,24},{9,... | collective-permute-start | bytes 2359304 | tf_op jit(solution)/shard_map/ppermute | solution.py:363
  69.1 19.9 %collective-permute-start.1 = (s16[128,1152]{1,0:T(8,128)(2,1)}, s16[128,1152]{1,0:T(8,128)(2,1)S(1)}, u32[]{:S(2)}, u32[]{:S(2)}) collective-permute-start(s16[128,1152]{1,0:T(8,128)(2,1)} %get-tuple-element.22), channel_id=1, source_target_pairs={{0,32},{1,33},{2,34},{3,35},{4,36},{5,37},{6,38},{7,39},{8,40},{9,... | collective-permute-start | bytes 884744 | tf_op jit(solution)/shard_map/ppermute | solution.py:366
  72.4 16.6 %collective-permute-start.2 = (s16[128,1152]{1,0:T(8,128)(2,1)S(1)}, s16[128,1152]{1,0:T(8,128)(2,1)}, u32[]{:S(2)}, u32[]{:S(2)}) collective-permute-start(s16[128,1152]{1,0:T(8,128)(2,1)S(1)} %get-tuple-element.23), channel_id=1, source_target_pairs={{0,224},{1,225},{2,226},{3,227},{4,228},{5,229},{6,230},{7,231},{8... | collective-permute-start | bytes 884744 | tf_op jit(solution)/shard_map/ppermute | solution.py:367
  77.9 52.9 %all-to-all-start.1 = ((s16[16,8,6272]{2,1,0:T(8,128)(2,1)}), s16[16,8,6272]{2,1,0:T(8,128)(2,1)S(1)}, u32[]{:S(2)}, u32[]{:S(2)}) async-start(s16[16,8,6272]{2,1,0:T(8,128)(2,1)} %bitcast.1), calls=%async_computation.1 | async-start | bytes 3211264 | tf_op jit(solution)/shard_map/all_to_all | solution.py:368
  89.1 41.7 %copy-start = (s32[256]{0:T(256)S(1)}, s32[256]{0:T(256)}, u32[]{:S(2)}) copy-start(s32[256]{0:T(256)} %cols.3) | copy-start | bytes 3076
  89.1 41.7 %copy-start.1 = (s32[256]{0:T(256)S(1)}, s32[256]{0:T(256)}, u32[]{:S(2)}) copy-start(s32[256]{0:T(256)} %rows.3) | copy-start | bytes 3076
  91.1 10.9 %collective-permute-start.3 = (s16[32,2176]{1,0:T(8,128)(2,1)S(1)}, s16[32,2176]{1,0:T(8,128)(2,1)S(1)}, u32[]{:S(2)}, u32[]{:S(2)}) collective-permute-start(s16[32,2176]{1,0:T(8,128)(2,1)S(1)} %get-tuple-element.25), channel_id=1, source_target_pairs={{0,128},{1,129},{2,130},{3,131},{4,132},{5,133},{6,134},{7,135},{8... | collective-permute-start | bytes 417800 | tf_op jit(solution)/shard_map/ppermute | solution.py:371
  94.5 9.1 %collective-permute-start.4 = (s16[32,2176]{1,0:T(8,128)(2,1)S(1)}, s16[32,2176]{1,0:T(8,128)(2,1)S(1)}, u32[]{:S(2)}, u32[]{:S(2)}) collective-permute-start(s16[32,2176]{1,0:T(8,128)(2,1)S(1)} %get-tuple-element.26), channel_id=1, source_target_pairs={{0,64},{1,65},{2,66},{3,67},{4,68},{5,69},{6,70},{7,71},{8,72},{9,... | collective-permute-start | bytes 417800 | tf_op jit(solution)/shard_map/ppermute | solution.py:371
  98.6 10.7 %collective-permute-start.5 = (s16[32,2176]{1,0:T(8,128)(2,1)S(1)}, s16[32,2176]{1,0:T(8,128)(2,1)S(1)}, u32[]{:S(2)}, u32[]{:S(2)}) collective-permute-start(s16[32,2176]{1,0:T(8,128)(2,1)S(1)} %get-tuple-element.27), channel_id=1, source_target_pairs={{0,192},{1,193},{2,194},{3,195},{4,196},{5,197},{6,198},{7,199},{8... | collective-permute-start | bytes 417800 | tf_op jit(solution)/shard_map/ppermute | solution.py:371
  110.0 10.9 %collective-permute-start.6 = (s16[8,2176]{1,0:T(8,128)(2,1)S(1)}, s16[8,2176]{1,0:T(8,128)(2,1)S(1)}, u32[]{:S(2)}, u32[]{:S(2)}) collective-permute-start(s16[8,2176]{1,0:T(8,128)(2,1)S(1)} %get-tuple-element.29), channel_id=1, source_target_pairs={{0,768},{1,769},{2,770},{3,771},{4,772},{5,773},{6,774},{7,775},{8... | collective-permute-start | bytes 104456 | tf_op jit(solution)/shard_map/ppermute | solution.py:375
  111.9 12.3 %collective-permute-start.7 = (s16[8,2176]{1,0:T(8,128)(2,1)S(1)}, s16[8,2176]{1,0:T(8,128)(2,1)S(1)}, u32[]{:S(2)}, u32[]{:S(2)}) collective-permute-start(s16[8,2176]{1,0:T(8,128)(2,1)S(1)} %get-tuple-element.30), channel_id=1, source_target_pairs={{0,512},{1,513},{2,514},{3,515},{4,516},{5,517},{6,518},{7,519},{8... | collective-permute-start | bytes 104456 | tf_op jit(solution)/shard_map/ppermute | solution.py:375
  118.7 7.0 %collective-permute-start.8 = (s16[8,2176]{1,0:T(8,128)(2,1)S(1)}, s16[8,2176]{1,0:T(8,128)(2,1)S(1)}, u32[]{:S(2)}, u32[]{:S(2)}) collective-permute-start(s16[8,2176]{1,0:T(8,128)(2,1)S(1)} %get-tuple-element.31), channel_id=1, source_target_pairs={{0,256},{1,257},{2,258},{3,259},{4,260},{5,261},{6,262},{7,263},{8... | collective-permute-start | bytes 104456 | tf_op jit(solution)/shard_map/ppermute | solution.py:375
  125.9 7.5 %collective-permute-start.9 = (f32[8,4,256]{2,1,0:T(4,128)S(1)}, f32[8,4,256]{2,1,0:T(4,128)S(1)}, u32[]{:S(2)}, u32[]{:S(2)}) collective-permute-start(f32[8,4,256]{2,1,0:T(4,128)S(1)} %get-tuple-element.33), channel_id=1, source_target_pairs={{0,16},{1,17},{2,18},{3,19},{4,20},{5,21},{6,22},{7,23},{8,24},{9,... | collective-permute-start | bytes 98312 | tf_op jit(solution)/shard_map/ppermute | solution.py:378
